TPU v7x, 32 devices: a whole 2x2x4 slice. The times are simulated.
32 devices in a mesh: energy: 8 (over y, x, core), slab: 4 (over z).
Axes of the slice: x: 2, y: 2, z: 4, core: 2. Of those that a mesh axis runs over, the one named last changes fastest.
Arguments:
- left_green: bfloat16 [2, 8, 4, 512, 512], P(None, 'energy', 'slab'), may hold values from -0.1875 to 0.1875
- coupling: bfloat16 [4, 512, 512], P('slab'), may hold values from -0.1875 to 0.1875
- previous_lesser: bfloat16 [2, 8, 4, 512, 512], P(None, 'energy', 'slab'), may hold values from -3 to 3
- screened: bfloat16 [2, 4, 512, 512], P(None, 'slab'), may hold values from -6 to 6
- offsets: int32 [8, 2], P('energy'), may hold values from 1 to 3, as said below
- occupation: float32 [2], replicated, may hold values from 0.25 to 4
Outputs:
- lesser: bfloat16 [2, 8, 4, 512, 512], P(None, 'energy', 'slab')
Inputs may be any that keep to these rules, and one draw needn't show every extreme that they name: `offsets`: every entry is a whole number of energy points from 1 to 3; both ends occur in every draw.
All inputs are finite; a program needn't handle non-finite values.
Results may differ from a plain program's by a relative error of at most 0.0075.
Values may be sent and summed in bfloat16 or wider, within the bound.
No kernel may reach another device: no remote copies, remote signals or barrier semaphores. Data moves between devices by JAX's collectives and lax.ppermute only.
A program may use at most 64 MiB of HBM per device.

v0:
```python
import jax
import jax.numpy as jnp
from jax import lax
from jax.sharding import PartitionSpec as P

MODES = 2
REACH = 3


def from_behind(value, axis, steps):
    count = lax.axis_size(axis)
    pairs = [(source, (source + steps) % count) for source in range(count)]
    return lax.ppermute(value, axis, pairs)


def shortened(value):
    return jax.tree.map(lambda a: a.astype(jnp.bfloat16) if a.dtype == jnp.float32 else a, value)


def shifted(value, axis, by):
    devices = lax.axis_size(axis)
    pairs = [(i, i + by) for i in range(devices) if 0 <= i + by < devices]
    return lax.ppermute(value, axis, pairs)


def matmul_plain(left, right):
    return jnp.dot(left, right, preferred_element_type=jnp.float32)


def matmul_trans(left, right):
    return lax.dot_general(
        left, right, (((1,), (1,)), ((), ())), preferred_element_type=jnp.float32
    )


def complex_times(left, right):
    real_part = matmul_plain(left[0], right[0]) - matmul_plain(left[1], right[1])
    imag_part = matmul_plain(left[0], right[1]) + matmul_plain(left[1], right[0])
    return jnp.stack([real_part, imag_part])


def complex_adjoint(left, right):
    real_part = matmul_trans(left[0], right[0]) + matmul_trans(left[1], right[1])
    imag_part = matmul_trans(left[1], right[0]) - matmul_trans(left[0], right[1])
    return jnp.stack([real_part, imag_part])


def complex_real(left, right):
    return jnp.stack([matmul_plain(left[0], right), matmul_plain(left[1], right)])


def apply_map(transfer, source, state):
    carried = complex_times(transfer, state).astype(jnp.bfloat16)
    return (complex_adjoint(carried, transfer) + source.astype(jnp.float32)).astype(jnp.bfloat16)


def on_device(left_green, coupling, previous_lesser, screened, offsets, occupation):
    local_lesser = previous_lesser[:, 0]
    count = local_lesser.shape[1]
    width = local_lesser.shape[2]
    self_energy = jnp.zeros(local_lesser.shape, jnp.float32)
    above = local_lesser
    below = local_lesser
    for offset in range(1, REACH + 1):
        above = from_behind(above, "energy", -1)
        below = from_behind(below, "energy", 1)
        total = self_energy
        for mode in range(MODES):
            hit = (offsets[0, mode] == offset).astype(jnp.float32)
            weight = (screened[mode].astype(jnp.float32) * hit)[None]
            total = total + weight * (
                above.astype(jnp.float32) + occupation[mode] * below.astype(jnp.float32)
            )
        self_energy = total
    self_energy = self_energy.astype(jnp.bfloat16)
    transfers = []
    sources = []
    green_slab = left_green[:, 0, 0]
    transfers.append(complex_real(green_slab, coupling[0]).astype(jnp.bfloat16))
    half = complex_times(green_slab, self_energy[:, 0]).astype(jnp.bfloat16)
    sources.append(complex_adjoint(half, green_slab).astype(jnp.bfloat16))

    def sweep(state):
        state = apply_map(transfers[0], sources[0], state)
        results = [state]
        return jnp.stack(results, axis=1)

    def skipped(state):
        return jnp.zeros((2, count, width, width), jnp.bfloat16)

    start = jnp.zeros((2, width, width), jnp.bfloat16)
    position = lax.axis_index("slab")
    devices = lax.axis_size("slab")
    results = skipped(start)
    carry = start
    for step in range(devices):
        mine = position == step
        swept = lax.cond(mine, sweep, skipped, carry)
        results = jnp.where(mine, swept, results)
        if step + 1 < devices:
            carry = shifted(shortened(swept[:, count - 1]), "slab", 1)
    return results[:, None]


def solution(mesh):
    placed = (
        P(None, "energy", "slab", None, None),
        P("slab", None, None),
        P(None, "energy", "slab", None, None),
        P(None, "slab", None, None),
        P("energy", None),
        P(),
    )
    return jax.shard_map(
        on_device,
        mesh=mesh,
        in_specs=placed,
        out_specs=P(None, "energy", "slab", None, None),
        check_vma=False,
    )
```

profile of v0, /device:TPU:30, one launch (start us, length us, event | category | flops | bytes accessed | tf_op | source)
XLA Modules:
  0.0 192.1 jit_solution(13630212296849788220)
XLA Ops:
  0.5 21.5 %collective-permute-done = bf16[2,1,512,512]{3,2,0,1:T(8,128)(2,1)S(1)} collective-permute-done((bf16[2,1,512,512]{3,2,0,1:T(8,128)(2,1)}, bf16[2,1,512,512]{3,2,0,1:T(8,128)(2,1)S(1)}, u32[]{:S(2)}, u32[]{:S(2)}) %collective-permute-start) | collective-permute-done | bytes 1048608 | tf_op jit(solution)/shard_map/ppermute | solution.py:13
  22.0 2.1 %collective-permute-start.2 = (bf16[2,1,512,512]{3,2,0,1:T(8,128)(2,1)S(1)}, bf16[2,1,512,512]{3,2,0,1:T(8,128)(2,1)}, u32[]{:S(2)}, u32[]{:S(2)}) collective-permute-start(bf16[2,1,512,512]{3,2,0,1:T(8,128)(2,1)S(1)} %collective-permute-done), channel_id=1, source_target_pairs={{0,28},{4,0},{8,4},{12,8},{16,12},{20,16},{24,20},{28,24},{1,29},{... | collective-permute-start | bytes 3145736 | tf_op jit(solution)/shard_map/ppermute | solution.py:13
  24.1 1.5 collective-permute-done.1
  25.6 18.6 %collective-permute-done.2 = bf16[2,1,512,512]{3,2,0,1:T(8,128)(2,1)} collective-permute-done((bf16[2,1,512,512]{3,2,0,1:T(8,128)(2,1)S(1)}, bf16[2,1,512,512]{3,2,0,1:T(8,128)(2,1)}, u32[]{:S(2)}, u32[]{:S(2)}) %collective-permute-start.2) | collective-permute-done | bytes 1048608 | tf_op jit(solution)/shard_map/ppermute | solution.py:13
  44.3 2.3 %collective-permute-start.4 = (bf16[2,1,512,512]{3,2,0,1:T(8,128)(2,1)}, bf16[2,1,512,512]{3,2,0,1:T(8,128)(2,1)}, u32[]{:S(2)}, u32[]{:S(2)}) collective-permute-start(bf16[2,1,512,512]{3,2,0,1:T(8,128)(2,1)} %collective-permute-done.2), channel_id=1, source_target_pairs={{0,28},{4,0},{8,4},{12,8},{16,12},{20,16},{24,20},{28,24},{1,29},{... | collective-permute-start | bytes 3145736 | tf_op jit(solution)/shard_map/ppermute | solution.py:13
  46.6 3.9 %collective-permute-done.3 = bf16[2,1,512,512]{3,2,0,1:T(8,128)(2,1)} collective-permute-done((bf16[2,1,512,512]{3,2,0,1:T(8,128)(2,1)S(1)}, bf16[2,1,512,512]{3,2,0,1:T(8,128)(2,1)}, u32[]{:S(2)}, u32[]{:S(2)}) %collective-permute-start.3) | collective-permute-done | bytes 1048608 | tf_op jit(solution)/shard_map/ppermute | solution.py:13
  50.4 1.4 fusion.179
  55.7 1.3 fusion.178
  57.1 1.5 fusion.144
  59.8 0.8 fusion.146
  60.6 4.2 %collective-permute-done.4 = bf16[2,1,512,512]{3,2,0,1:T(8,128)(2,1)} collective-permute-done((bf16[2,1,512,512]{3,2,0,1:T(8,128)(2,1)}, bf16[2,1,512,512]{3,2,0,1:T(8,128)(2,1)}, u32[]{:S(2)}, u32[]{:S(2)}) %collective-permute-start.4) | collective-permute-done | bytes 1048608 | tf_op jit(solution)/shard_map/ppermute | solution.py:13
  64.8 9.7 %collective-permute-done.5 = bf16[2,1,512,512]{3,2,0,1:T(8,128)(2,1)} collective-permute-done((bf16[2,1,512,512]{3,2,0,1:T(8,128)(2,1)}, bf16[2,1,512,512]{3,2,0,1:T(8,128)(2,1)}, u32[]{:S(2)}, u32[]{:S(2)}) %collective-permute-start.5) | collective-permute-done | bytes 1048608 | tf_op jit(solution)/shard_map/ppermute | solution.py:13
  74.5 4.9 %fusion.132 = bf16[2,1,512,512]{3,2,0,1:T(8,128)(2,1)S(1)} fusion(bf16[2,1,512,512]{3,2,0,1:T(8,128)(2,1)S(1)} %copy-done.4, bf16[2,1,512,512]{3,2,0,1:T(8,128)(2,1)S(1)} %copy-done.6, bf16[2,1,512,512]{3,2,0,1:T(8,128)(2,1)} %collective-permute-done.2, bf16[2,1,512,512]{3,2,0,1:T(8,128)(2,1)} %collective-permute-done.3, ...), kind=kLoop, calls=%fused_computation.164 | loop fusion | flops 15728640 | bytes 13631496 | tf_op jit(solution)/shard_map/convert_element_type | solution.py:75
  83.5 1.1 conditional.4
  83.5 1.0 broadcast.36
  84.6 1.3 collective-permute-start.6
  85.9 25.6 %collective-permute-done.6 = bf16[2,512,512]{2,1,0:T(8,128)(2,1)} collective-permute-done((bf16[2,512,512]{2,1,0:T(8,128)(2,1)}, bf16[2,512,512]{2,1,0:T(8,128)(2,1)}, u32[]{:S(2)}, u32[]{:S(2)}) %collective-permute-start.6) | collective-permute-done | bytes 1048608 | tf_op jit(solution)/shard_map/ppermute | solution.py:23
  111.4 1.0 conditional.5
  111.4 1.0 broadcast.38
  112.5 1.5 collective-permute-start.7
  113.9 24.5 %collective-permute-done.7 = bf16[2,512,512]{2,1,0:T(8,128)(2,1)} collective-permute-done((bf16[2,512,512]{2,1,0:T(8,128)(2,1)}, bf16[2,512,512]{2,1,0:T(8,128)(2,1)}, u32[]{:S(2)}, u32[]{:S(2)}) %collective-permute-start.7) | collective-permute-done | bytes 1048608 | tf_op jit(solution)/shard_map/ppermute | solution.py:23
  138.4 1.1 conditional.6
  138.4 1.1 broadcast.39
  139.5 1.3 collective-permute-start.8
  140.8 39.8 %collective-permute-done.8 = bf16[2,512,512]{2,1,0:T(8,128)(2,1)} collective-permute-done((bf16[2,512,512]{2,1,0:T(8,128)(2,1)}, bf16[2,512,512]{2,1,0:T(8,128)(2,1)}, u32[]{:S(2)}, u32[]{:S(2)}) %collective-permute-start.8) | collective-permute-done | bytes 1048608 | tf_op jit(solution)/shard_map/ppermute | solution.py:23
  180.6 9.1 %conditional.7 = (bf16[2,1,512,512]{3,2,0,1:T(8,128)(2,1)}) conditional(s32[]{:T(128)} %convert_element_type.130, () %tuple.29, (bf16[2,512,512]{2,1,0:T(8,128)(2,1)S(1)}, bf16[2,512,512]{2,1,0:T(8,128)(2,1)}, bf16[2,512,512]{2,1,0:T(8,128)(2,1)S(1)}) %tuple.36), branch_computations={%region_6.7_spmd, %region_7.8_spmd} | conditional | flops 2151153664 | bytes 24117256 | solution.py:98
  180.6 1.5 fusion.98
  182.1 1.5 fusion.96
  184.0 1.5 fusion.106
  185.5 1.5 fusion.95
  188.4 1.3 fusion.97
  189.7 2.4 %select_bitcast_fusion = bf16[2,1,1,512,512]{4,3,2,1,0:T(8,128)(2,1)} fusion(bf16[2,1,512,512]{3,2,0,1:T(8,128)(2,1)} %get-tuple-element.67, bf16[2,1,512,512]{3,2,0,1:T(8,128)(2,1)} %get-tuple-element.66, bf16[2,1,512,512]{3,2,0,1:T(8,128)(2,1)} %get-tuple-element.65, bf16[2,1,512,512]{3,2,0,1:T(8,128)(2,1)} %get-tuple-element.64, pred[]{:T(512)S(6)} %eq.39, ...), kind=kLoop, calls=%fused_computation.198 | loop fusion | flops 2097152 | bytes 5242884 | tf_op jit(solution)/shard_map/broadcast_in_dim | solution.py:102
  (32 shorter events, 7.7 us)
Async XLA Ops:
  0.0 57.1 %copy-start = (bf16[1,512,512]{2,1,0:T(8,128)(2,1)S(1)}, bf16[1,512,512]{2,1,0:T(8,128)(2,1)}, u32[]{:S(2)}) copy-start(bf16[1,512,512]{2,1,0:T(8,128)(2,1)} %param.15) | copy-start | bytes 1572868
  0.0 58.5 %copy-start.1 = (bf16[2,1,1,512,512]{4,3,2,1,0:T(8,128)(2,1)S(1)}, bf16[2,1,1,512,512]{4,3,2,1,0:T(8,128)(2,1)}, u32[]{:S(2)}) copy-start(bf16[2,1,1,512,512]{4,3,2,1,0:T(8,128)(2,1)} %param.14) | copy-start | bytes 3145732
  0.0 22.0 %collective-permute-start = (bf16[2,1,512,512]{3,2,0,1:T(8,128)(2,1)}, bf16[2,1,512,512]{3,2,0,1:T(8,128)(2,1)S(1)}, u32[]{:S(2)}, u32[]{:S(2)}) collective-permute-start(bf16[2,1,512,512]{3,2,0,1:T(8,128)(2,1)} %bitcast.216), channel_id=1, source_target_pairs={{0,28},{4,0},{8,4},{12,8},{16,12},{20,16},{24,20},{28,24},{1,29},{... | collective-permute-start | bytes 3145736 | tf_op jit(solution)/shard_map/ppermute | solution.py:13
  0.0 25.6 %collective-permute-start.1 = (bf16[2,1,512,512]{3,2,0,1:T(8,128)(2,1)}, bf16[2,1,512,512]{3,2,0,1:T(8,128)(2,1)S(1)}, u32[]{:S(2)}, u32[]{:S(2)}) collective-permute-start(bf16[2,1,512,512]{3,2,0,1:T(8,128)(2,1)} %bitcast.217), channel_id=1, source_target_pairs={{0,4},{4,8},{8,12},{12,16},{16,20},{20,24},{24,28},{28,0},{1,5},{5... | collective-permute-start | bytes 3145736 | tf_op jit(solution)/shard_map/ppermute | solution.py:13
  22.0 35.0 %copy-start.3 = (bf16[2,1,512,512]{3,2,0,1:T(8,128)(2,1)}, bf16[2,1,512,512]{3,2,0,1:T(8,128)(2,1)S(1)}, u32[]{:S(2)}) copy-start(bf16[2,1,512,512]{3,2,0,1:T(8,128)(2,1)S(1)} %collective-permute-done) | copy-start | bytes 3145732
  22.0 22.2 %collective-permute-start.2 = (bf16[2,1,512,512]{3,2,0,1:T(8,128)(2,1)S(1)}, bf16[2,1,512,512]{3,2,0,1:T(8,128)(2,1)}, u32[]{:S(2)}, u32[]{:S(2)}) collective-permute-start(bf16[2,1,512,512]{3,2,0,1:T(8,128)(2,1)S(1)} %collective-permute-done), channel_id=1, source_target_pairs={{0,28},{4,0},{8,4},{12,8},{16,12},{20,16},{24,20},{28,24},{1,29},{... | collective-permute-start | bytes 3145736 | tf_op jit(solution)/shard_map/ppermute | solution.py:13
  25.6 18.6 %copy-start.5 = (bf16[2,1,512,512]{3,2,0,1:T(8,128)(2,1)}, bf16[2,1,512,512]{3,2,0,1:T(8,128)(2,1)S(1)}, u32[]{:S(2)}) copy-start(bf16[2,1,512,512]{3,2,0,1:T(8,128)(2,1)S(1)} %collective-permute-done.1) | copy-start | bytes 3145732
  25.6 24.8 %collective-permute-start.3 = (bf16[2,1,512,512]{3,2,0,1:T(8,128)(2,1)S(1)}, bf16[2,1,512,512]{3,2,0,1:T(8,128)(2,1)}, u32[]{:S(2)}, u32[]{:S(2)}) collective-permute-start(bf16[2,1,512,512]{3,2,0,1:T(8,128)(2,1)S(1)} %collective-permute-done.1), channel_id=1, source_target_pairs={{0,4},{4,8},{8,12},{12,16},{16,20},{20,24},{24,28},{28,0},{1,5},{5... | collective-permute-start | bytes 3145736 | tf_op jit(solution)/shard_map/ppermute | solution.py:13
  44.3 20.5 %collective-permute-start.4 = (bf16[2,1,512,512]{3,2,0,1:T(8,128)(2,1)}, bf16[2,1,512,512]{3,2,0,1:T(8,128)(2,1)}, u32[]{:S(2)}, u32[]{:S(2)}) collective-permute-start(bf16[2,1,512,512]{3,2,0,1:T(8,128)(2,1)} %collective-permute-done.2), channel_id=1, source_target_pairs={{0,28},{4,0},{8,4},{12,8},{16,12},{20,16},{24,20},{28,24},{1,29},{... | collective-permute-start | bytes 3145736 | tf_op jit(solution)/shard_map/ppermute | solution.py:13
  50.4 24.0 %collective-permute-start.5 = (bf16[2,1,512,512]{3,2,0,1:T(8,128)(2,1)}, bf16[2,1,512,512]{3,2,0,1:T(8,128)(2,1)}, u32[]{:S(2)}, u32[]{:S(2)}) collective-permute-start(bf16[2,1,512,512]{3,2,0,1:T(8,128)(2,1)} %collective-permute-done.3), channel_id=1, source_target_pairs={{0,4},{4,8},{8,12},{12,16},{16,20},{20,24},{24,28},{28,0},{1,5},{5... | collective-permute-start | bytes 3145736 | tf_op jit(solution)/shard_map/ppermute | solution.py:13
  58.6 1.2 copy-start.2
  59.8 14.7 %copy-start.4 = (bf16[2,1,512,512]{3,2,0,1:T(8,128)(2,1)S(1)}, bf16[2,1,512,512]{3,2,0,1:T(8,128)(2,1)}, u32[]{:S(2)}) copy-start(bf16[2,1,512,512]{3,2,0,1:T(8,128)(2,1)} %copy-done.3) | copy-start | bytes 3145732
  59.8 14.7 %copy-start.6 = (bf16[2,1,512,512]{3,2,0,1:T(8,128)(2,1)S(1)}, bf16[2,1,512,512]{3,2,0,1:T(8,128)(2,1)}, u32[]{:S(2)}) copy-start(bf16[2,1,512,512]{3,2,0,1:T(8,128)(2,1)} %copy-done.5) | copy-start | bytes 3145732
  84.6 26.9 %collective-permute-start.6 = (bf16[2,512,512]{2,1,0:T(8,128)(2,1)}, bf16[2,512,512]{2,1,0:T(8,128)(2,1)}, u32[]{:S(2)}, u32[]{:S(2)}) collective-permute-start(bf16[2,512,512]{2,1,0:T(8,128)(2,1)} %bitcast.213), channel_id=1, source_target_pairs={{0,1},{1,2},{2,3},{4,5},{5,6},{6,7},{8,9},{9,10},{10,11},{12,13},{... | collective-permute-start | bytes 3145736 | tf_op jit(solution)/shard_map/ppermute | solution.py:23
  112.5 26.0 %collective-permute-start.7 = (bf16[2,512,512]{2,1,0:T(8,128)(2,1)}, bf16[2,512,512]{2,1,0:T(8,128)(2,1)}, u32[]{:S(2)}, u32[]{:S(2)}) collective-permute-start(bf16[2,512,512]{2,1,0:T(8,128)(2,1)} %bitcast.214), channel_id=1, source_target_pairs={{0,1},{1,2},{2,3},{4,5},{5,6},{6,7},{8,9},{9,10},{10,11},{12,13},{... | collective-permute-start | bytes 3145736 | tf_op jit(solution)/shard_map/ppermute | solution.py:23
  139.5 41.1 %collective-permute-start.8 = (bf16[2,512,512]{2,1,0:T(8,128)(2,1)}, bf16[2,512,512]{2,1,0:T(8,128)(2,1)}, u32[]{:S(2)}, u32[]{:S(2)}) collective-permute-start(bf16[2,512,512]{2,1,0:T(8,128)(2,1)} %bitcast.215), channel_id=1, source_target_pairs={{0,1},{1,2},{2,3},{4,5},{5,6},{6,7},{8,9},{9,10},{10,11},{12,13},{... | collective-permute-start | bytes 3145736 | tf_op jit(solution)/shard_map/ppermute | solution.py:23
where the time goes:
time: 193 us; the launch traced here: 192 us
  waiting for transfers between devices  149 us (77%)
  matrix products  13.6 us (7%)
  other arithmetic  9.56 us (5%)
  starting transfers between devices  8.93 us (5%)
  local copies, waits for them, and re-layouts  6.63 us (3%)
  between operations  4.09 us (2%)
    ppermute x3, waiting for transfers between devices, shifted(): return lax.ppermute(value, axis, pairs)  89.9 us
    ppermute x6, waiting for transfers between devices, from_behind(): return lax.ppermute(value, axis, pairs)  59.4 us
    dot_general x10, matrix products, matmul_plain(): return jnp.dot(left, right, preferred_element_type=jnp.float32)  9.75 us
    ppermute x6, starting transfers between devices, from_behind(): return lax.ppermute(value, axis, pairs)  4.91 us
    convert_element_type x1, other arithmetic, on_device(): self_energy = self_energy.astype(jnp.bfloat16)  4.88 us
    ppermute x3, starting transfers between devices, shifted(): return lax.ppermute(value, axis, pairs)  4.02 us
  transfers between devices with their start and end apart: 9, of which 9 were waited for; matrix products, arithmetic and copies ran while one was open for 3% of the time, Pallas kernels for 0%

commit v1 on v0

v1 whole, which is shorter than its diff:
```python
import functools

import jax
import jax.numpy as jnp
from jax import lax
from jax.experimental import pallas as pl
from jax.experimental.pallas import tpu as pltpu
from jax.sharding import PartitionSpec as P

MODES = 2
REACH = 3
BF = jnp.bfloat16
F32 = jnp.float32
CUTS = 2

VMEM = pl.BlockSpec(memory_space=pltpu.VMEM)
SMEM = pl.BlockSpec(memory_space=pltpu.SMEM)
ANY = pl.BlockSpec(memory_space=pl.ANY)


def dot(left, right):
    return jnp.dot(left, right, preferred_element_type=F32)


def dot_t(left, right):
    return lax.dot_general(left, right, (((1,), (1,)), ((), ())), preferred_element_type=F32)


def call(kernel, outs, scalars, arrays, flops, scratch=(), after=(), tied=()):
    moved = sum(a.size * a.dtype.itemsize for a in [*arrays, *outs])
    inputs, extra = len(scalars) + len(arrays), len(after) + len(tied)

    def body(*refs):
        rest = refs[inputs + extra :]
        kernel(*refs[:inputs], *rest[: len(outs)], *rest[len(outs) + len(tied) :])

    found = pl.pallas_call(
        body,
        out_shape=[*outs, *(jax.ShapeDtypeStruct(t.shape, t.dtype) for t in tied)],
        in_specs=[SMEM] * len(scalars) + [VMEM] * len(arrays) + [ANY] * extra,
        out_specs=[VMEM] * len(outs) + [ANY] * len(tied),
        scratch_shapes=list(scratch),
        input_output_aliases={
            inputs + len(after) + n: len(outs) + n for n in range(len(tied))
        },
        compiler_params=pltpu.CompilerParams(vmem_limit_bytes=24 * 2**20),
        cost_estimate=pl.CostEstimate(flops=flops, bytes_accessed=moved, transcendentals=0),
    )(*scalars, *arrays, *after, *tied)
    return found[0] if len(found) == 1 else found


def block(*shape):
    return jax.ShapeDtypeStruct(shape, BF)


def either(core_ref, number, work):
    for n in range(2):
        pl.when(core_ref[0] == (number ^ n))(functools.partial(work, n))


def self_energy_patch(spots, scalars, carriers, occupation, screened, pieces, results):
    rows, width = screened.shape[1:]

    def kernel(*refs):
        refs = list(refs)
        scalar_refs = [refs.pop(0) for _ in scalars]
        occ_ref = refs.pop(0)
        carrier_refs = [refs.pop(0) for _ in carriers]
        screened_ref = refs.pop(0)
        table = refs.pop()
        notes = [lambda ref=ref: ref[:, :128].astype(jnp.int32) for ref in carrier_refs]
        for n in range(len(pieces)):
            piece_ref = refs.pop(0)
            if len(piece_ref.shape) == 3:
                table[n] = piece_ref[...]
            else:
                table[n, 0] = piece_ref[:rows]
                table[n, 1] = piece_ref[rows : 2 * rows]
                notes.append(
                    lambda ref=piece_ref: ref[2 * rows : 2 * rows + 16, :128].astype(jnp.int32)
                )
        places = spots(scalar_refs, notes)
        step = 16

        def strip(i, carry):
            at = pl.ds(pl.multiple_of(i * step, step), step)
            weights = [screened_ref[m, at, :].astype(F32) for m in range(MODES)]
            for n in range(results):
                for part in range(2):
                    total = None
                    for m in range(MODES):
                        above = table[places[n][m][0], part, at, :].astype(F32)
                        below = table[places[n][m][1], part, at, :].astype(F32)
                        term = weights[m] * (above + occ_ref[m] * below)
                        total = term if total is None else total + term
                    refs[n][part, at, :] = total.astype(BF)
            return carry

        lax.fori_loop(0, rows // step, strip, 0)

    return call(
        kernel,
        [block(2, rows, width)] * results,
        [*scalars, occupation],
        [*carriers, screened, *pieces],
        results * 2 * rows * width * 12,
        [pltpu.VMEM((len(pieces), 2, rows, width), BF)],
    )


def times_into(left, right, out):
    size = left.shape[1]
    tile = min(256, size)
    real, imag = right[0], right[1]
    for i in range(0, size, tile):
        lr, li = left[0, i : i + tile, :], left[1, i : i + tile, :]
        out[0, i : i + tile, :] = (dot(lr, real) - dot(li, imag)).astype(BF)
        out[1, i : i + tile, :] = (dot(lr, imag) + dot(li, real)).astype(BF)


def times(core, number, lefts, groups, places=None, after=(), tied=()):
    rows, width = groups[0][0].shape[1:]
    full = (2, rows * len(groups), width)
    counts = [len(group) for group in groups]
    scalars = [core] if places is None else [core, places]
    whole = counts == [1]

    def kernel(core_ref, *refs):
        refs = list(refs)
        places_ref = refs.pop(0) if places is not None else None
        left_refs = [refs.pop(0) for _ in range(2)]
        if whole:
            right, out_ref = refs
        else:
            right, out_ref = refs.pop(), refs.pop()
            for n, count in enumerate(counts):
                if places_ref is None:
                    at = slice(n * rows, (n + 1) * rows)
                else:
                    at = pl.ds(pl.multiple_of(places_ref[n] * rows, rows), rows)
                value = refs.pop(0)[...]
                for _ in range(count - 1):
                    value = value + refs.pop(0)[...]
                right[:, at, :] = value
        either(core_ref, number, lambda n: times_into(left_refs[n], right, out_ref))

    return call(
        kernel,
        [block(*full)],
        scalars,
        [*lefts, *sum(groups, [])],
        8 * full[1] * full[1] * width,
        [] if whole else [pltpu.VMEM(full, BF)],
        after,
        tied,
    )


def transfer_of(green, coupling, after=()):
    size = coupling.shape[0]

    def kernel(green_ref, coupling_ref, out_ref):
        for part in range(2):
            out_ref[part] = dot(green_ref[part], coupling_ref[...]).astype(BF)

    return call(kernel, [block(*green.shape)], [], [green, coupling], 4 * size**3, (), after)


def composed(wanted, left, groups, after=()):
    size = left.shape[1]

    def kernel(wanted_ref, left_ref, *refs):
        *right_refs, out_ref, right = refs

        @pl.when(wanted_ref[0] == 1)
        def _():
            value = right_refs[0][...]
            for ref in right_refs[1:]:
                value = value + ref[...]
            right[...] = value
            times_into(left_ref, right, out_ref)

        @pl.when(wanted_ref[0] != 1)
        def _():
            out_ref[...] = left_ref[...]

    return call(
        kernel,
        [block(*left.shape)],
        [wanted],
        [left, *groups],
        8 * size**3,
        [pltpu.VMEM(left.shape, BF)],
        after,
    )


def adjoint_into(mine, theirs, right, mine_at, theirs_at, to_at, store):
    size = right.shape[1]
    tile = min(256, size)
    a = [right[p, to_at, mine_at] for p in range(2)]
    b = [right[p, to_at, theirs_at] for p in range(2)]
    for i in range(0, size, tile):
        at = slice(i, i + tile)
        mr, mi = mine[0, at, :], mine[1, at, :]
        tr, ti = theirs[0, at, :], theirs[1, at, :]
        real = dot_t(mr, a[0]) + dot_t(mi, a[1]) + dot_t(tr, b[0]) + dot_t(ti, b[1])
        imag = dot_t(mi, a[0]) - dot_t(mr, a[1]) + dot_t(ti, b[0]) - dot_t(tr, b[1])
        store(at, real, imag)


def adjoint_half(core, number, mine, theirs, rights, summand=None, after=()):
    half = mine.shape[2]

    def kernel(core_ref, mine_ref, theirs_ref, *refs):
        out_ref = refs[-1]

        def store(at, real, imag):
            if summand is not None:
                real = real + refs[2][0, at, :].astype(F32)
                imag = imag + refs[2][1, at, :].astype(F32)
            out_ref[0, at, :] = real.astype(BF)
            out_ref[1, at, :] = imag.astype(BF)

        def work(n):
            held = number ^ n
            own, other = slice(held * half, (held + 1) * half), slice((1 - held) * half, (2 - held) * half)
            adjoint_into(mine_ref, theirs_ref, refs[n], own, other, own, store)

        either(core_ref, number, work)

    arrays = [mine, theirs, *rights] + ([] if summand is None else [summand])
    flops = 16 * mine.shape[1] * half * half
    return call(kernel, [block(*mine.shape)], [core], arrays, flops, (), after)


def adjoint_own(core, mines, theirs, right, sums, other_sums):
    half = mines[0].shape[2]
    size = mines[0].shape[1]

    def kernel(core_ref, right_ref, *refs):
        out_ref = refs[-1]

        def work(n):
            mine_ref, theirs_ref, sum_ref, other_ref = refs[n:-1:2]
            own, other = slice(n * half, (n + 1) * half), slice((1 - n) * half, (2 - n) * half)
            for to, summand in ((own, sum_ref), (other, other_ref)):

                def store(at, real, imag):
                    out_ref[0, at, to] = (real + summand[0, at, :].astype(F32)).astype(BF)
                    out_ref[1, at, to] = (imag + summand[1, at, :].astype(F32)).astype(BF)

                adjoint_into(mine_ref, theirs_ref, right_ref, own, other, to, store)

        either(core_ref, 0, work)

    arrays = [right, *mines, *theirs, *sums, *other_sums]
    return call(kernel, [block(2, size, size)], [core], arrays, 8 * size**3)


def on_device(left_green, coupling, previous_lesser, screened, offsets, occupation):
    energies, slabs = lax.axis_size("energy"), lax.axis_size("slab")
    me, slab = lax.axis_index("energy"), lax.axis_index("slab")
    pairs = energies // 2
    pair, core = me // 2, me % 2
    first = core == 0
    size = coupling.shape[1]
    half = size // 2
    core_s = core[None]

    def swap(value):
        return lax.ppermute(value, "energy", [(i, i ^ 1) for i in range(energies)])

    def to_even(value):
        return lax.ppermute(value, "energy", [(i + 1, i) for i in range(0, energies, 2)])

    def to_odd(value):
        return lax.ppermute(value, "energy", [(i, i + 1) for i in range(0, energies, 2)])

    def by_energy(own, other):
        return jnp.where(first, own, other), jnp.where(first, other, own)

    green = left_green[:, 0, 0]
    before = previous_lesser[:, 0, 0]
    own = transfer_of(green, coupling[0])

    def column_half(value):
        return lax.dynamic_slice_in_dim(value, core * half, half, value.ndim - 1)

    both = [before, swap(before)]
    two = jnp.concatenate([offsets, swap(offsets)])
    spread = pairs in (2, 4) and size % (16 * pairs) == 0
    if spread:
        rows = size // pairs

        def across(value, d):
            moves = [(i, i ^ (2 * d)) for i in range(energies)]
            return lax.ppermute(value, "energy", moves)

        def patch(value, which):
            corner = (0, which * rows, core * half)
            return lax.dynamic_slice(value, corner, (2, rows, half))

        notes = jnp.pad(two.reshape(2 * MODES, 1).astype(BF), ((0, 16 - 2 * MODES), (0, 0)))
        notes = jnp.broadcast_to(notes, (16, half))
        order = list(reversed(range(1, pairs)))
        pieces = [None] * energies
        carriers = [notes]
        pieces[0], pieces[1] = patch(both[0], pair), patch(both[1], pair)
        for d in order:
            pieces[2 * d] = across(patch(both[0], pair ^ d), d)
        for d in order:
            sent = patch(both[1], pair ^ d).reshape(2 * rows, half)
            pieces[2 * d + 1] = across(jnp.concatenate([sent, notes]), d)
        weights = patch(screened[:, 0], pair)
        places = pair ^ jnp.arange(pairs, dtype=jnp.int32)
        scalars = [me[None]]

        def spots(scalar_refs, carrier_refs):
            here = scalar_refs[0][0]
            found = [[None] * pairs for _ in range(2)]
            core_here = lax.rem(here, 2)
            for d in range(pairs):
                note = carrier_refs[d]()
                line = lax.broadcasted_iota(jnp.int32, note.shape, 0)
                for n in range(2):
                    holder = here ^ (2 * d) ^ (core_here ^ n)
                    at = []
                    for m in range(MODES):
                        wanted_line = MODES * (core_here ^ n) + m
                        o = jnp.max(jnp.where(line == wanted_line, note, 0))
                        higher = lax.rem(holder + o, energies) ^ here
                        lower = lax.rem(holder - o + energies, energies) ^ here
                        at.append((higher, lower))
                    found[n][d] = at
            return found[0] + found[1]
    else:
        near = (REACH + 1) // 2
        pieces = []
        for d in range(-near, near + 1):
            moves = [(i, (i - 2 * d) % energies) for i in range(energies)]
            for value in both:
                value = column_half(value)
                pieces.append(lax.ppermute(value, "energy", moves) if d else value)
        weights = column_half(screened[:, 0])
        places, carriers = None, []
        scalars = [core_s, two]

        def spots(scalar_refs, piece_refs):
            core_ref, two_ref = scalar_refs

            def place(away):
                away = away + 2 * near
                return 2 * lax.div(away, 2) + (lax.rem(away, 2) ^ core_ref[0])

            found = []
            for n in range(2):
                shift = [two_ref[core_ref[0] ^ n, m] for m in range(MODES)]
                found.append([(place(n + o), place(n - o)) for o in shift])
            return found

    def maps_before(span, own):
        found, moving = [], own
        for hop in range(span):
            moves = [
                (s + hop - 1, s + hop)
                for s in range(3 * span, slabs, 2 * span)
                if s + hop < slabs
            ]
            moving = lax.ppermute(moving, "slab", moves)
            found.append(moving)
        return found

    befores = maps_before(1, own) if slabs > 2 else []
    other_green = swap(green)
    lefts = (green, other_green)
    found = self_energy_patch(
        spots, scalars, carriers, occupation, weights, pieces, 2 * pairs if spread else 2
    )
    sums = []
    if spread:
        early, late = list(found[:pairs]), list(found[pairs:])
        for d in order:
            early[d] = across(early[d], d)
        product, *late[1:] = times(
            core_s, 0, lefts, [[part] for part in early], places, tied=late[1:]
        )
        for d in order:
            late[d] = across(late[d], d)
    else:
        product = times(core_s, 0, lefts, [[found[0]]])
        late = [found[1]]
    sums.append(adjoint_half(core_s, 0, product, swap(product), lefts, None, befores))
    product = times(core_s, 1, lefts, [[part] for part in late], places, after=sums)
    sums.append(adjoint_half(core_s, 1, product, swap(product), lefts))
    maps = (own, transfer_of(other_green, coupling[0], after=sums[1:]))

    def arrivals(span, value):
        cuts = 1 if span == 1 else CUTS
        high = size // cuts
        groups = []
        for cut in range(cuts):
            group, moving = [], value[:, cut * high : (cut + 1) * high]
            for hop in range(span):
                moves = [
                    (s + hop - 1, s + hop)
                    for s in range(span, slabs, 2 * span)
                    if s + hop < slabs
                ]
                moving = lax.ppermute(moving, "slab", moves)
                group.append(moving)
            groups.append(group)
        return groups

    span = 1
    groups = [arrivals(1, value) for value in sums] if slabs > 1 else []
    while 2 * span < slabs:
        wanted = lax.rem(slab // span, 2)[None]
        own = composed(wanted, own, befores, after=[sums[1], maps[1]])
        carried = times(core_s, 0, maps, groups[0], after=[own])
        early = adjoint_half(core_s, 0, carried, swap(carried), maps, sums[0])
        early_groups = arrivals(2 * span, early)
        heads = [group[0] for group in early_groups]
        carried = times(core_s, 1, maps, groups[1], after=[early, heads[0]])
        behind = heads[1:] + early_groups[0][1:2]
        late = adjoint_half(core_s, 1, carried, swap(carried), maps, sums[1], behind)
        sums, groups = [early, late], [early_groups, arrivals(2 * span, late)]
        maps = (own, swap(own))
        span *= 2
        if 2 * span < slabs:
            befores = maps_before(span, own)
    if slabs > 1:
        carried = [times(core_s, n, maps, groups[n]) for n in range(2)]
        theirs = [to_even(carried[0]), to_odd(carried[1])]
        others = [to_even(sums[0]), to_odd(sums[1])]
        result = adjoint_own(core_s, carried, theirs, maps[0], sums, others)
        return result[:, None, None]
    result = jnp.where(first, sums[0], sums[1])
    other = swap(jnp.where(first, sums[1], sums[0]))
    return jnp.concatenate(by_energy(result, other), axis=2)[:, None, None]


def solution(mesh):
    placed = (
        P(None, "energy", "slab", None, None),
        P("slab", None, None),
        P(None, "energy", "slab", None, None),
        P(None, "slab", None, None),
        P("energy", None),
        P(),
    )
    return jax.shard_map(
        on_device,
        mesh=mesh,
        in_specs=placed,
        out_specs=P(None, "energy", "slab", None, None),
        check_vma=False,
    )
```

time: 193 us -> 121 us (0.63)
  the two profiles are of different devices: /device:TPU:30 before, /device:TPU:25 now
where the time goes in v1:
time: 121 us; the launch traced here: 120 us
  waiting for transfers between devices  51 us (42%)
  starting transfers between devices  41.6 us (34%)
  Pallas kernels  20.6 us (17%)
  local copies, waits for them, and re-layouts  6.79 us (6%)
    ppermute x10, waiting for transfers between devices, arrivals(): moving = lax.ppermute(moving, 'slab', moves)  33 us
    pallas_call x15, Pallas kernels, call(): pl.pallas_call(body, out_shape=[*outs, *(jax.ShapeDtypeStruct(t.shape, t....  20.6 us
    ppermute x12, waiting for transfers between devices, across(): return lax.ppermute(value, 'energy', moves)  14.1 us
    ppermute x12, starting transfers between devices, across(): return lax.ppermute(value, 'energy', moves)  11 us
    ppermute x10, starting transfers between devices, arrivals(): moving = lax.ppermute(moving, 'slab', moves)  10.4 us
    ppermute x2, starting transfers between devices, to_even(): lax.ppermute(value, 'energy', [(i + 1, i) for i in range(0, energies, 2)])  8.66 us
    ppermute x8, starting transfers between devices, swap(): return lax.ppermute(value, 'energy', [(i, i ^ 1) for i in range(energies)])  7.57 us
    unnamed x20, local copies, waits for them, and re-layouts  3.45 us
  transfers between devices with their start and end apart: 35, of which 17 were waited for; matrix products, arithmetic and copies ran while one was open for 3% of the time, Pallas kernels for 11%

profile of v1, /device:TPU:25, one launch (start us, length us, event | category | flops | bytes accessed | tf_op | source)
XLA Modules:
  0.0 120.4 jit_solution(866631161009564826)
XLA Ops:
  1.4 1.9 %dynamic-slice_bitcast_fusion = (bf16[2,128,256]{2,1,0:T(8,128)(2,1)}, bf16[2,128,256]{2,1,0:T(8,128)(2,1)}, bf16[2,128,256]{2,1,0:T(8,128)(2,1)S(1)}, bf16[2,128,256]{2,1,0:T(8,128)(2,1)}) fusion(bf16[2,1,1,512,512]{4,3,2,1,0:T(8,128)(2,1)} %param.8, s32[]{:T(128)S(6)} %select_n.46, s32[]{:T(128)S(6)} %select_n.43, s32[]{:T(128)S(6)} %select_n.44, ...), kind=kLoop, calls=%fused_computation.3 | loop fusion | bytes 1048596 | tf_op jit(solution)/shard_map/dynamic_slice | solution.py:302
  8.0 1.3 %collective-permute-start = (bf16[2,512,512]{2,1,0:T(8,128)(2,1)S(1)}, bf16[2,512,512]{2,1,0:T(8,128)(2,1)S(1)}, u32[]{:S(2)}, u32[]{:S(2)}) collective-permute-start(bf16[2,512,512]{2,1,0:T(8,128)(2,1)S(1)} %shard_map.64.refs_1_.refs_3_), channel_id=1, source_target_pairs={{2,3},{6,7},{10,11},{14,15},{18,19},{22,23},{26,27},{30,31}} | collective-permute-start | bytes 3145736 | tf_op jit(solution)/shard_map/ppermute | solution.py:370
  13.6 1.4 %collective-permute-done.5.refs_7_ = bf16[272,256]{1,0:T(8,128)(2,1)S(1)} collective-permute-done((bf16[272,256]{1,0:T(8,128)(2,1)S(1)}, bf16[272,256]{1,0:T(8,128)(2,1)S(1)}, u32[]{:S(2)}, u32[]{:S(2)}) %collective-permute-start.5) | collective-permute-done | bytes 139296 | tf_op jit(solution)/shard_map/ppermute | solution.py:298
  16.0 2.5 %collective-permute-done.9.refs_11_ = bf16[272,256]{1,0:T(8,128)(2,1)S(1)} collective-permute-done((bf16[272,256]{1,0:T(8,128)(2,1)S(1)}, bf16[272,256]{1,0:T(8,128)(2,1)S(1)}, u32[]{:S(2)}, u32[]{:S(2)}) %collective-permute-start.9) | collective-permute-done | bytes 139296 | tf_op jit(solution)/shard_map/ppermute | solution.py:298
  19.2 2.1 %shard_map.65 = (bf16[2,128,256]{2,1,0:T(8,128)(2,1)S(1)}, bf16[2,128,256]{2,1,0:T(8,128)(2,1)S(1)}, bf16[2,128,256]{2,1,0:T(8,128)(2,1)S(1)}, bf16[2,128,256]{2...) custom-call(s32[1]{0:T(128)} %bitcast.4.refs_0_, ...), custom_call_target="tpu_custom_call" | custom-call | flops 6291456 | bytes 2260992 | tf_op jit(solution)/shard_map/pallas_call | solution.py:37
  21.3 1.7 %collective-permute-start.10 = (bf16[2,128,256]{2,1,0:T(8,128)(2,1)S(1)}, bf16[2,128,256]{2,1,0:T(8,128)(2,1)S(1)}, u32[]{:S(2)}, u32[]{:S(2)}) collective-permute-start(bf16[2,128,256]{2,1,0:T(8,128)(2,1)S(1)} %get-tuple-element.19), channel_id=1, source_target_pairs={{0,8},{4,12},{8,0},{12,4},{16,24},{20,28},{24,16},{28,20},{1,9},{5... | collective-permute-start | bytes 393224 | tf_op jit(solution)/shard_map/ppermute | solution.py:298
  24.3 1.4 %collective-permute-done.10.refs_5_ = bf16[2,128,256]{2,1,0:T(8,128)(2,1)S(1)} collective-permute-done((bf16[2,128,256]{2,1,0:T(8,128)(2,1)S(1)}, bf16[2,128,256]{2,1,0:T(8,128)(2,1)S(1)}, u32[]{:S(2)}, u32[]{:S(2)}) %collective-permute-start.10) | collective-permute-done | bytes 131104 | tf_op jit(solution)/shard_map/ppermute | solution.py:298
  25.6 2.8 %collective-permute-done.11.refs_6_ = bf16[2,128,256]{2,1,0:T(8,128)(2,1)S(1)} collective-permute-done((bf16[2,128,256]{2,1,0:T(8,128)(2,1)S(1)}, bf16[2,128,256]{2,1,0:T(8,128)(2,1)S(1)}, u32[]{:S(2)}, u32[]{:S(2)}) %collective-permute-start.11) | collective-permute-done | bytes 131104 | tf_op jit(solution)/shard_map/ppermute | solution.py:298
  28.4 1.3 %shard_map.66 = (bf16[2,512,256]{2,1,0:T(8,128)(2,1)S(1)}, bf16[2,128,256]{2,1,0:T(8,128)(2,1)S(1)}, bf16[2,128,256]{2,1,0:T(8,128)(2,1)S(1)}, bf16[2,128,256]{2,1,0:T(8,128)(2,1)S(1)}) custom-call(s32[1]{0:T(128)} %bitcast.refs_0_, s32[4]{0:T(128)S(1)} %iota_xor_fusion.refs_1_, ...), custom_call_target="tpu_custom_call", output_to_operand_aliasing={{1}: (8, {}), {2}: (9, {}), {3}: (10, {})} | custom-call | flops 536870912 | bytes 3145728 | tf_op jit(solution)/shard_map/pallas_call | solution.py:37
  29.7 3.4 %collective-permute-start.16 = (bf16[2,512,256]{2,1,0:T(8,128)(2,1)S(1)}, bf16[2,512,256]{2,1,0:T(8,128)(2,1)S(1)}, u32[]{:S(2)}, u32[]{:S(2)}) collective-permute-start(bf16[2,512,256]{2,1,0:T(8,128)(2,1)S(1)} %get-tuple-element.28.refs_1_), channel_id=1, source_target_pairs={{0,4},{4,0},{8,12},{12,8},{16,20},{20,16},{24,28},{28,24},{1,5},{5... | collective-permute-start | bytes 1572872 | tf_op jit(solution)/shard_map/ppermute | solution.py:272
  35.8 1.6 %shard_map.67.refs_8_.refs_5_ = bf16[2,512,256]{2,1,0:T(8,128)(2,1)} custom-call(s32[1]{0:T(128)} %bitcast.refs_0_, bf16[2,512,256]{2,1,0:T(8,128)(2,1)S(1)} %get-tuple-element.28.refs_1_, bf16[2,512,256]{2,1,0:T(8,128)(2,1)S(1)} %collective-permute-done.16.refs_2_, bf16[2,512,512]{2,1,0:T(8,128)(2,1)S(1)} %bitcast.27, ...), custom_call_target="tpu_custom_call" | custom-call | flops 536870912 | bytes 3670016 | tf_op jit(solution)/shard_map/pallas_call | solution.py:37
  39.0 3.0 %collective-permute-done.15.refs_7_ = bf16[2,128,256]{2,1,0:T(8,128)(2,1)S(1)} collective-permute-done((bf16[2,128,256]{2,1,0:T(8,128)(2,1)S(1)}, bf16[2,128,256]{2,1,0:T(8,128)(2,1)S(1)}, u32[]{:S(2)}, u32[]{:S(2)}) %collective-permute-start.15) | collective-permute-done | bytes 131104 | tf_op jit(solution)/shard_map/ppermute | solution.py:298
  42.0 2.1 %shard_map.68.refs_1_ = bf16[2,512,256]{2,1,0:T(8,128)(2,1)} custom-call(s32[1]{0:T(128)} %bitcast.refs_0_, s32[4]{0:T(128)S(1)} %iota_xor_fusion.refs_1_, bf16[2,512,512]{2,1,0:T(8,128)(2,1)S(1)} %bitcast.28, bf16[2,512,512]{2,1,0:T(8,128)(2,1)S(1)} %collective-permute-done.1.refs_3_.refs_4_.refs_0_, bf16[2,128,256]{2,1,0:T(8,128)(2,1)S(1)} %get-tuple-element.17.refs_4_, ...), custom_call_target="tpu_custom_call" | custom-call | flops 536870912 | bytes 3145728 | tf_op jit(solution)/shard_map/pallas_call | solution.py:37
  48.2 2.0 %shard_map.69.refs_2_.refs_3_.refs_5_ = bf16[2,512,256]{2,1,0:T(8,128)(2,1)S(1)} custom-call(s32[1]{0:T(128)} %bitcast.refs_0_, bf16[2,512,256]{2,1,0:T(8,128)(2,1)} %shard_map.68.refs_1_, bf16[2,512,256]{2,1,0:T(8,128)(2,1)} %collective-permute-done.17.refs_2_, bf16[2,512,512]{2,1,0:T(8,128)(2,1)S(1)} %bitcast.29, ...), custom_call_target="tpu_custom_call" | custom-call | flops 536870912 | bytes 3670016 | tf_op jit(solution)/shard_map/pallas_call | solution.py:37
  51.5 1.3 %shard_map.71.refs_4_.refs_1_ = bf16[2,512,512]{2,1,0:T(8,128)(2,1)S(1)} custom-call(s32[1]{0:T(128)} %bitcast.1.refs_0_, bf16[2,512,512]{2,1,0:T(8,128)(2,1)S(1)} %shard_map.64.refs_1_.refs_3_, bf16[2,512,512]{2,1,0:T(8,128)(2,1)S(1)} %copy-done.5, bf16[2,512,256]{2,1,0:T(8,128)(2,1)S(1)} %shard_map.69.refs_2_.refs_3_.refs_5_, ...), custom_call_target="tpu_custom_call" | custom-call | flops 1073741824 | bytes 3145728 | tf_op jit(solution)/shard_map/pallas_call | solution.py:37
  52.8 8.2 %collective-permute-done.19.refs_3_ = bf16[2,512,256]{2,1,0:T(8,128)(2,1)} collective-permute-done((bf16[2,512,256]{2,1,0:T(8,128)(2,1)}, bf16[2,512,256]{2,1,0:T(8,128)(2,1)}, u32[]{:S(2)}, u32[]{:S(2)}) %collective-permute-start.19) | collective-permute-done | bytes 524320 | tf_op jit(solution)/shard_map/ppermute | solution.py:410
  60.9 1.7 %shard_map.72.refs_1_ = bf16[2,512,256]{2,1,0:T(8,128)(2,1)S(1)} custom-call(s32[1]{0:T(128)} %bitcast.refs_0_, bf16[2,512,512]{2,1,0:T(8,128)(2,1)S(1)} %shard_map.64.refs_1_.refs_3_, bf16[2,512,512]{2,1,0:T(8,128)(2,1)S(1)} %shard_map.70.refs_4_.refs_2_, bf16[2,512,256]{2,1,0:T(8,128)(2,1)} %collective-permute-done.19.refs_3_, ...), custom_call_target="tpu_custom_call" | custom-call | flops 536870912 | bytes 3145728 | tf_op jit(solution)/shard_map/pallas_call | solution.py:37
  65.0 1.8 %shard_map.73.refs_4_.refs_6_ = bf16[2,512,256]{2,1,0:T(8,128)(2,1)S(1)} custom-call(s32[1]{0:T(128)} %bitcast.refs_0_, bf16[2,512,256]{2,1,0:T(8,128)(2,1)S(1)} %shard_map.72.refs_1_, bf16[2,512,256]{2,1,0:T(8,128)(2,1)S(1)} %collective-permute-done.20.refs_2_, bf16[2,512,512]{2,1,0:T(8,128)(2,1)S(1)} %shard_map.64.refs_1_.refs_3_, ...), custom_call_target="tpu_custom_call" | custom-call | flops 536870912 | bytes 4194304 | tf_op jit(solution)/shard_map/pallas_call | solution.py:37
  67.6 11.3 %collective-permute-done.25.refs_3_ = bf16[2,512,256]{2,1,0:T(8,128)(2,1)S(1)} collective-permute-done((bf16[2,512,256]{2,1,0:T(8,128)(2,1)S(1)}, bf16[2,512,256]{2,1,0:T(8,128)(2,1)S(1)}, u32[]{:S(2)}, u32[]{:S(2)}) %collective-permute-start.25) | collective-permute-done | bytes 524320 | tf_op jit(solution)/shard_map/ppermute | solution.py:410
  81.3 1.3 %collective-permute-start.22 = (bf16[2,256,256]{2,1,0:T(8,128)(2,1)S(1)}, bf16[2,256,256]{2,1,0:T(8,128)(2,1)S(1)}, u32[]{:S(2)}, u32[]{:S(2)}) collective-permute-start(bf16[2,256,256]{2,1,0:T(8,128)(2,1)S(1)} %collective-permute-done.21.refs_3_.refs_5_), channel_id=1, source_target_pairs={{2,3},{6,7},{10,11},{14,15},{18,19},{22,23},{26,27},{30,31}} | collective-permute-start | bytes 786440 | tf_op jit(solution)/shard_map/ppermute | solution.py:410
  82.6 8.0 %collective-permute-done.22.refs_4_.refs_7_ = bf16[2,256,256]{2,1,0:T(8,128)(2,1)S(1)} collective-permute-done((bf16[2,256,256]{2,1,0:T(8,128)(2,1)S(1)}, bf16[2,256,256]{2,1,0:T(8,128)(2,1)S(1)}, u32[]{:S(2)}, u32[]{:S(2)}) %collective-permute-start.22) | collective-permute-done | bytes 262176 | tf_op jit(solution)/shard_map/ppermute | solution.py:410
  92.8 1.3 %collective-permute-start.24 = (bf16[2,256,256]{2,1,0:T(8,128)(2,1)S(1)}, bf16[2,256,256]{2,1,0:T(8,128)(2,1)S(1)}, u32[]{:S(2)}, u32[]{:S(2)}) collective-permute-start(bf16[2,256,256]{2,1,0:T(8,128)(2,1)S(1)} %collective-permute-done.23.refs_5_.refs_6_), channel_id=1, source_target_pairs={{2,3},{6,7},{10,11},{14,15},{18,19},{22,23},{26,27},{30,31}} | collective-permute-start | bytes 786440 | tf_op jit(solution)/shard_map/ppermute | solution.py:410
  94.1 1.3 %collective-permute-start.28 = (bf16[2,256,256]{2,1,0:T(8,128)(2,1)S(1)}, bf16[2,256,256]{2,1,0:T(8,128)(2,1)S(1)}, u32[]{:S(2)}, u32[]{:S(2)}) collective-permute-start(bf16[2,256,256]{2,1,0:T(8,128)(2,1)S(1)} %collective-permute-done.27.refs_3_), channel_id=1, source_target_pairs={{2,3},{6,7},{10,11},{14,15},{18,19},{22,23},{26,27},{30,31}} | collective-permute-start | bytes 786440 | tf_op jit(solution)/shard_map/ppermute | solution.py:410
  95.4 1.3 %collective-permute-start.30 = (bf16[2,256,256]{2,1,0:T(8,128)(2,1)S(1)}, bf16[2,256,256]{2,1,0:T(8,128)(2,1)S(1)}, u32[]{:S(2)}, u32[]{:S(2)}) collective-permute-start(bf16[2,256,256]{2,1,0:T(8,128)(2,1)S(1)} %collective-permute-done.29.refs_5_), channel_id=1, source_target_pairs={{2,3},{6,7},{10,11},{14,15},{18,19},{22,23},{26,27},{30,31}} | collective-permute-start | bytes 786440 | tf_op jit(solution)/shard_map/ppermute | solution.py:410
  96.7 3.2 %collective-permute-start.33 = (bf16[2,512,256]{2,1,0:T(8,128)(2,1)S(1)}, bf16[2,512,256]{2,1,0:T(8,128)(2,1)S(1)}, u32[]{:S(2)}, u32[]{:S(2)}) collective-permute-start(bf16[2,512,256]{2,1,0:T(8,128)(2,1)S(1)} %shard_map.73.refs_4_.refs_6_), channel_id=1, source_target_pairs={{4,0},{12,8},{20,16},{28,24},{5,1},{13,9},{21,17},{29,25},{6,2},{1... | collective-permute-start | bytes 1572872 | tf_op jit(solution)/shard_map/ppermute | solution.py:275
  99.9 1.3 %collective-permute-done.24.refs_6_ = bf16[2,256,256]{2,1,0:T(8,128)(2,1)S(1)} collective-permute-done((bf16[2,256,256]{2,1,0:T(8,128)(2,1)S(1)}, bf16[2,256,256]{2,1,0:T(8,128)(2,1)S(1)}, u32[]{:S(2)}, u32[]{:S(2)}) %collective-permute-start.24) | collective-permute-done | bytes 262176 | tf_op jit(solution)/shard_map/ppermute | solution.py:410
  102.0 5.5 %collective-permute-start.31 = (bf16[2,512,256]{2,1,0:T(8,128)(2,1)S(1)}, bf16[2,512,256]{2,1,0:T(8,128)(2,1)S(1)}, u32[]{:S(2)}, u32[]{:S(2)}) collective-permute-start(bf16[2,512,256]{2,1,0:T(8,128)(2,1)S(1)} %shard_map.74.refs_2_), channel_id=1, source_target_pairs={{4,0},{12,8},{20,16},{28,24},{5,1},{13,9},{21,17},{29,25},{6,2},{1... | collective-permute-start | bytes 1572872 | tf_op jit(solution)/shard_map/ppermute | solution.py:275
  107.4 1.3 %collective-permute-start.34 = (bf16[2,512,256]{2,1,0:T(8,128)(2,1)S(1)}, bf16[2,512,256]{2,1,0:T(8,128)(2,1)S(1)}, u32[]{:S(2)}, u32[]{:S(2)}) collective-permute-start(bf16[2,512,256]{2,1,0:T(8,128)(2,1)S(1)} %shard_map.76.refs_7_), channel_id=1, source_target_pairs={{0,4},{8,12},{16,20},{24,28},{1,5},{9,13},{17,21},{25,29},{2,6},{1... | collective-permute-start | bytes 1572872 | tf_op jit(solution)/shard_map/ppermute | solution.py:278
  108.8 4.2 %collective-permute-done.30.refs_6_ = bf16[2,256,256]{2,1,0:T(8,128)(2,1)S(1)} collective-permute-done((bf16[2,256,256]{2,1,0:T(8,128)(2,1)S(1)}, bf16[2,256,256]{2,1,0:T(8,128)(2,1)S(1)}, u32[]{:S(2)}, u32[]{:S(2)}) %collective-permute-start.30) | collective-permute-done | bytes 262176 | tf_op jit(solution)/shard_map/ppermute | solution.py:410
  113.7 1.3 %collective-permute-start.32 = (bf16[2,512,256]{2,1,0:T(8,128)(2,1)S(1)}, bf16[2,512,256]{2,1,0:T(8,128)(2,1)S(1)}, u32[]{:S(2)}, u32[]{:S(2)}) collective-permute-start(bf16[2,512,256]{2,1,0:T(8,128)(2,1)S(1)} %shard_map.77.refs_3_), channel_id=1, source_target_pairs={{0,4},{8,12},{16,20},{24,28},{1,5},{9,13},{17,21},{25,29},{2,6},{1... | collective-permute-start | bytes 1572872 | tf_op jit(solution)/shard_map/ppermute | solution.py:278
  115.0 3.1 %collective-permute-done.32.refs_5_ = bf16[2,512,256]{2,1,0:T(8,128)(2,1)S(1)} collective-permute-done((bf16[2,512,256]{2,1,0:T(8,128)(2,1)S(1)}, bf16[2,512,256]{2,1,0:T(8,128)(2,1)S(1)}, u32[]{:S(2)}, u32[]{:S(2)}) %collective-permute-start.32) | collective-permute-done | bytes 524320 | tf_op jit(solution)/shard_map/ppermute | solution.py:278
  118.1 2.3 %shard_map.78 = bf16[2,512,512]{2,1,0:T(8,128)(2,1)} custom-call(s32[1]{0:T(128)} %bitcast.refs_0_, bf16[2,512,512]{2,1,0:T(8,128)(2,1)S(1)} %shard_map.71.refs_4_.refs_1_, bf16[2,512,256]{2,1,0:T(8,128)(2,1)S(1)} %shard_map.74.refs_2_, bf16[2,512,256]{2,1,0:T(8,128)(2,1)S(1)} %shard_map.77.refs_3_, ...), custom_call_target="tpu_custom_call" | custom-call | flops 1073741824 | bytes 6291456 | tf_op jit(solution)/shard_map/pallas_call | solution.py:37
  (86 shorter events, 32.0 us)
Async XLA Ops:
  0.0 8.0 %collective-permute-start.3 = (bf16[2,512,512]{2,1,0:T(8,128)(2,1)}, bf16[2,512,512]{2,1,0:T(8,128)(2,1)}, u32[]{:S(2)}, u32[]{:S(2)}) collective-permute-start(bf16[2,512,512]{2,1,0:T(8,128)(2,1)} %bitcast.35), channel_id=1, source_target_pairs={{0,4},{4,0},{8,12},{12,8},{16,20},{20,16},{24,28},{28,24},{1,5},{5... | collective-permute-start | bytes 3145736 | tf_op jit(solution)/shard_map/ppermute | solution.py:272
  0.7 23.6 %collective-permute-start.1 = (bf16[2,512,512]{2,1,0:T(8,128)(2,1)}, bf16[2,512,512]{2,1,0:T(8,128)(2,1)S(1)}, u32[]{:S(2)}, u32[]{:S(2)}) collective-permute-start(bf16[2,512,512]{2,1,0:T(8,128)(2,1)} %bitcast.24), channel_id=1, source_target_pairs={{0,4},{4,0},{8,12},{12,8},{16,20},{20,16},{24,28},{28,24},{1,5},{5... | collective-permute-start | bytes 3145736 | tf_op jit(solution)/shard_map/ppermute | solution.py:272
  0.8 6.8 %collective-permute-start.2 = (s32[1,2]{1,0:T(1,128)S(1)}, s32[1,2]{1,0:T(1,128)S(1)}, u32[]{:S(2)}, u32[]{:S(2)}) collective-permute-start(s32[1,2]{1,0:T(1,128)S(1)} %copy-done.9), channel_id=1, source_target_pairs={{0,4},{4,0},{8,12},{12,8},{16,20},{20,16},{24,28},{28,24},{1,5},{5... | collective-permute-start | bytes 32 | tf_op jit(solution)/shard_map/ppermute | solution.py:272
  3.4 7.2 %collective-permute-start.4 = (bf16[2,128,256]{2,1,0:T(8,128)(2,1)}, bf16[2,128,256]{2,1,0:T(8,128)(2,1)S(1)}, u32[]{:S(2)}, u32[]{:S(2)}) collective-permute-start(bf16[2,128,256]{2,1,0:T(8,128)(2,1)} %get-tuple-element.34), channel_id=1, source_target_pairs={{0,8},{4,12},{8,0},{12,4},{16,24},{20,28},{24,16},{28,20},{1,9},{5... | collective-permute-start | bytes 393224 | tf_op jit(solution)/shard_map/ppermute | solution.py:298
  4.6 7.3 %collective-permute-start.6 = (bf16[2,128,256]{2,1,0:T(8,128)(2,1)}, bf16[2,128,256]{2,1,0:T(8,128)(2,1)S(1)}, u32[]{:S(2)}, u32[]{:S(2)}) collective-permute-start(bf16[2,128,256]{2,1,0:T(8,128)(2,1)} %get-tuple-element.36), channel_id=1, source_target_pairs={{0,16},{4,20},{8,24},{12,28},{16,0},{20,4},{24,8},{28,12},{1,17},{... | collective-permute-start | bytes 393224 | tf_op jit(solution)/shard_map/ppermute | solution.py:298
  7.6 5.8 %collective-permute-start.8 = (bf16[2,128,256]{2,1,0:T(8,128)(2,1)}, bf16[2,128,256]{2,1,0:T(8,128)(2,1)}, u32[]{:S(2)}, u32[]{:S(2)}) collective-permute-start(bf16[2,128,256]{2,1,0:T(8,128)(2,1)} %get-tuple-element.33), channel_id=1, source_target_pairs={{0,24},{4,28},{8,16},{12,20},{16,8},{20,12},{24,0},{28,4},{1,25},{... | collective-permute-start | bytes 393224 | tf_op jit(solution)/shard_map/ppermute | solution.py:298
  8.0 27.8 %collective-permute-start = (bf16[2,512,512]{2,1,0:T(8,128)(2,1)S(1)}, bf16[2,512,512]{2,1,0:T(8,128)(2,1)S(1)}, u32[]{:S(2)}, u32[]{:S(2)}) collective-permute-start(bf16[2,512,512]{2,1,0:T(8,128)(2,1)S(1)} %shard_map.64.refs_1_.refs_3_), channel_id=1, source_target_pairs={{2,3},{6,7},{10,11},{14,15},{18,19},{22,23},{26,27},{30,31}} | collective-permute-start | bytes 3145736 | tf_op jit(solution)/shard_map/ppermute | solution.py:370
  10.5 4.4 %collective-permute-start.5 = (bf16[272,256]{1,0:T(8,128)(2,1)S(1)}, bf16[272,256]{1,0:T(8,128)(2,1)S(1)}, u32[]{:S(2)}, u32[]{:S(2)}) collective-permute-start(bf16[272,256]{1,0:T(8,128)(2,1)S(1)} %get-tuple-element.43), channel_id=1, source_target_pairs={{0,8},{4,12},{8,0},{12,4},{16,24},{20,28},{24,16},{28,20},{1,9},{5... | collective-permute-start | bytes 417800 | tf_op jit(solution)/shard_map/ppermute | solution.py:298
  11.8 4.2 %collective-permute-start.7 = (bf16[272,256]{1,0:T(8,128)(2,1)S(1)}, bf16[272,256]{1,0:T(8,128)(2,1)S(1)}, u32[]{:S(2)}, u32[]{:S(2)}) collective-permute-start(bf16[272,256]{1,0:T(8,128)(2,1)S(1)} %get-tuple-element.42), channel_id=1, source_target_pairs={{0,16},{4,20},{8,24},{12,28},{16,0},{20,4},{24,8},{28,12},{1,17},{... | collective-permute-start | bytes 417800 | tf_op jit(solution)/shard_map/ppermute | solution.py:298
  13.4 5.2 %collective-permute-start.9 = (bf16[272,256]{1,0:T(8,128)(2,1)S(1)}, bf16[272,256]{1,0:T(8,128)(2,1)S(1)}, u32[]{:S(2)}, u32[]{:S(2)}) collective-permute-start(bf16[272,256]{1,0:T(8,128)(2,1)S(1)} %get-tuple-element.41), channel_id=1, source_target_pairs={{0,24},{4,28},{8,16},{12,20},{16,8},{20,12},{24,0},{28,4},{1,25},{... | collective-permute-start | bytes 417800 | tf_op jit(solution)/shard_map/ppermute | solution.py:298
  21.3 4.3 %collective-permute-start.10 = (bf16[2,128,256]{2,1,0:T(8,128)(2,1)S(1)}, bf16[2,128,256]{2,1,0:T(8,128)(2,1)S(1)}, u32[]{:S(2)}, u32[]{:S(2)}) collective-permute-start(bf16[2,128,256]{2,1,0:T(8,128)(2,1)S(1)} %get-tuple-element.19), channel_id=1, source_target_pairs={{0,8},{4,12},{8,0},{12,4},{16,24},{20,28},{24,16},{28,20},{1,9},{5... | collective-permute-start | bytes 393224 | tf_op jit(solution)/shard_map/ppermute | solution.py:298
  23.0 5.4 %collective-permute-start.11 = (bf16[2,128,256]{2,1,0:T(8,128)(2,1)S(1)}, bf16[2,128,256]{2,1,0:T(8,128)(2,1)S(1)}, u32[]{:S(2)}, u32[]{:S(2)}) collective-permute-start(bf16[2,128,256]{2,1,0:T(8,128)(2,1)S(1)} %get-tuple-element.20), channel_id=1, source_target_pairs={{0,16},{4,20},{8,24},{12,28},{16,0},{20,4},{24,8},{28,12},{1,17},{... | collective-permute-start | bytes 393224 | tf_op jit(solution)/shard_map/ppermute | solution.py:298
  23.2 5.2 %collective-permute-start.12 = (bf16[2,128,256]{2,1,0:T(8,128)(2,1)S(1)}, bf16[2,128,256]{2,1,0:T(8,128)(2,1)S(1)}, u32[]{:S(2)}, u32[]{:S(2)}) collective-permute-start(bf16[2,128,256]{2,1,0:T(8,128)(2,1)S(1)} %get-tuple-element.21), channel_id=1, source_target_pairs={{0,24},{4,28},{8,16},{12,20},{16,8},{20,12},{24,0},{28,4},{1,25},{... | collective-permute-start | bytes 393224 | tf_op jit(solution)/shard_map/ppermute | solution.py:298
  29.7 6.0 %collective-permute-start.16 = (bf16[2,512,256]{2,1,0:T(8,128)(2,1)S(1)}, bf16[2,512,256]{2,1,0:T(8,128)(2,1)S(1)}, u32[]{:S(2)}, u32[]{:S(2)}) collective-permute-start(bf16[2,512,256]{2,1,0:T(8,128)(2,1)S(1)} %get-tuple-element.28.refs_1_), channel_id=1, source_target_pairs={{0,4},{4,0},{8,12},{12,8},{16,20},{20,16},{24,28},{28,24},{1,5},{5... | collective-permute-start | bytes 1572872 | tf_op jit(solution)/shard_map/ppermute | solution.py:272
  33.1 5.1 %collective-permute-start.13 = (bf16[2,128,256]{2,1,0:T(8,128)(2,1)S(1)}, bf16[2,128,256]{2,1,0:T(8,128)(2,1)S(1)}, u32[]{:S(2)}, u32[]{:S(2)}) collective-permute-start(bf16[2,128,256]{2,1,0:T(8,128)(2,1)S(1)} %get-tuple-element.25), channel_id=1, source_target_pairs={{0,8},{4,12},{8,0},{12,4},{16,24},{20,28},{24,16},{28,20},{1,9},{5... | collective-permute-start | bytes 393224 | tf_op jit(solution)/shard_map/ppermute | solution.py:298
  34.2 4.7 %collective-permute-start.14 = (bf16[2,128,256]{2,1,0:T(8,128)(2,1)S(1)}, bf16[2,128,256]{2,1,0:T(8,128)(2,1)S(1)}, u32[]{:S(2)}, u32[]{:S(2)}) collective-permute-start(bf16[2,128,256]{2,1,0:T(8,128)(2,1)S(1)} %get-tuple-element.26), channel_id=1, source_target_pairs={{0,16},{4,20},{8,24},{12,28},{16,0},{20,4},{24,8},{28,12},{1,17},{... | collective-permute-start | bytes 393224 | tf_op jit(solution)/shard_map/ppermute | solution.py:298
  34.7 7.3 %collective-permute-start.15 = (bf16[2,128,256]{2,1,0:T(8,128)(2,1)S(1)}, bf16[2,128,256]{2,1,0:T(8,128)(2,1)S(1)}, u32[]{:S(2)}, u32[]{:S(2)}) collective-permute-start(bf16[2,128,256]{2,1,0:T(8,128)(2,1)S(1)} %get-tuple-element.27), channel_id=1, source_target_pairs={{0,24},{4,28},{8,16},{12,20},{16,8},{20,12},{24,0},{28,4},{1,25},{... | collective-permute-start | bytes 393224 | tf_op jit(solution)/shard_map/ppermute | solution.py:298
  44.1 2.9 %collective-permute-start.17 = (bf16[2,512,256]{2,1,0:T(8,128)(2,1)}, bf16[2,512,256]{2,1,0:T(8,128)(2,1)}, u32[]{:S(2)}, u32[]{:S(2)}) collective-permute-start(bf16[2,512,256]{2,1,0:T(8,128)(2,1)} %shard_map.68.refs_1_), channel_id=1, source_target_pairs={{0,4},{4,0},{8,12},{12,8},{16,20},{20,16},{24,28},{28,24},{1,5},{5... | collective-permute-start | bytes 1572872 | tf_op jit(solution)/shard_map/ppermute | solution.py:272
  45.1 15.8 %collective-permute-start.19 = (bf16[2,512,256]{2,1,0:T(8,128)(2,1)}, bf16[2,512,256]{2,1,0:T(8,128)(2,1)}, u32[]{:S(2)}, u32[]{:S(2)}) collective-permute-start(bf16[2,512,256]{2,1,0:T(8,128)(2,1)} %shard_map.67.refs_8_.refs_5_), channel_id=1, source_target_pairs={{0,1},{2,3},{4,5},{6,7},{8,9},{10,11},{12,13},{14,15},{16,17},{18,... | collective-permute-start | bytes 1572872 | tf_op jit(solution)/shard_map/ppermute | solution.py:410
  63.5 15.4 %collective-permute-start.25 = (bf16[2,512,256]{2,1,0:T(8,128)(2,1)S(1)}, bf16[2,512,256]{2,1,0:T(8,128)(2,1)S(1)}, u32[]{:S(2)}, u32[]{:S(2)}) collective-permute-start(bf16[2,512,256]{2,1,0:T(8,128)(2,1)S(1)} %shard_map.69.refs_2_.refs_3_.refs_5_), channel_id=1, source_target_pairs={{0,1},{2,3},{4,5},{6,7},{8,9},{10,11},{12,13},{14,15},{16,17},{18,... | collective-permute-start | bytes 1572872 | tf_op jit(solution)/shard_map/ppermute | solution.py:410
  66.9 12.0 %collective-permute-start.21 = (bf16[2,256,256]{2,1,0:T(8,128)(2,1)S(1)}, bf16[2,256,256]{2,1,0:T(8,128)(2,1)S(1)}, u32[]{:S(2)}, u32[]{:S(2)}) collective-permute-start(bf16[2,256,256]{2,1,0:T(8,128)(2,1)S(1)} %get-tuple-element.40), channel_id=1, source_target_pairs={{1,2},{5,6},{9,10},{13,14},{17,18},{21,22},{25,26},{29,30}} | collective-permute-start | bytes 786440 | tf_op jit(solution)/shard_map/ppermute | solution.py:410
  79.6 11.0 %collective-permute-start.26 = (bf16[2,512,256]{2,1,0:T(8,128)(2,1)S(1)}, bf16[2,512,256]{2,1,0:T(8,128)(2,1)S(1)}, u32[]{:S(2)}, u32[]{:S(2)}) collective-permute-start(bf16[2,512,256]{2,1,0:T(8,128)(2,1)S(1)} %shard_map.75.refs_1_), channel_id=1, source_target_pairs={{0,4},{4,0},{8,12},{12,8},{16,20},{20,16},{24,28},{28,24},{1,5},{5... | collective-permute-start | bytes 1572872 | tf_op jit(solution)/shard_map/ppermute | solution.py:272
  80.5 19.4 %collective-permute-start.18 = (bf16[2,512,512]{2,1,0:T(8,128)(2,1)S(1)}, bf16[2,512,512]{2,1,0:T(8,128)(2,1)S(1)}, u32[]{:S(2)}, u32[]{:S(2)}) collective-permute-start(bf16[2,512,512]{2,1,0:T(8,128)(2,1)S(1)} %shard_map.71.refs_4_.refs_1_), channel_id=1, source_target_pairs={{0,4},{4,0},{8,12},{12,8},{16,20},{20,16},{24,28},{28,24},{1,5},{5... | collective-permute-start | bytes 3145736 | tf_op jit(solution)/shard_map/ppermute | solution.py:272
  81.3 9.3 %collective-permute-start.22 = (bf16[2,256,256]{2,1,0:T(8,128)(2,1)S(1)}, bf16[2,256,256]{2,1,0:T(8,128)(2,1)S(1)}, u32[]{:S(2)}, u32[]{:S(2)}) collective-permute-start(bf16[2,256,256]{2,1,0:T(8,128)(2,1)S(1)} %collective-permute-done.21.refs_3_.refs_5_), channel_id=1, source_target_pairs={{2,3},{6,7},{10,11},{14,15},{18,19},{22,23},{26,27},{30,31}} | collective-permute-start | bytes 786440 | tf_op jit(solution)/shard_map/ppermute | solution.py:410
  92.1 3.3 %collective-permute-start.29 = (bf16[2,256,256]{2,1,0:T(8,128)(2,1)S(1)}, bf16[2,256,256]{2,1,0:T(8,128)(2,1)S(1)}, u32[]{:S(2)}, u32[]{:S(2)}) collective-permute-start(bf16[2,256,256]{2,1,0:T(8,128)(2,1)S(1)} %get-tuple-element.37), channel_id=1, source_target_pairs={{1,2},{5,6},{9,10},{13,14},{17,18},{21,22},{25,26},{29,30}} | collective-permute-start | bytes 786440 | tf_op jit(solution)/shard_map/ppermute | solution.py:410
  92.8 8.4 %collective-permute-start.24 = (bf16[2,256,256]{2,1,0:T(8,128)(2,1)S(1)}, bf16[2,256,256]{2,1,0:T(8,128)(2,1)S(1)}, u32[]{:S(2)}, u32[]{:S(2)}) collective-permute-start(bf16[2,256,256]{2,1,0:T(8,128)(2,1)S(1)} %collective-permute-done.23.refs_5_.refs_6_), channel_id=1, source_target_pairs={{2,3},{6,7},{10,11},{14,15},{18,19},{22,23},{26,27},{30,31}} | collective-permute-start | bytes 786440 | tf_op jit(solution)/shard_map/ppermute | solution.py:410
  94.1 14.7 %collective-permute-start.28 = (bf16[2,256,256]{2,1,0:T(8,128)(2,1)S(1)}, bf16[2,256,256]{2,1,0:T(8,128)(2,1)S(1)}, u32[]{:S(2)}, u32[]{:S(2)}) collective-permute-start(bf16[2,256,256]{2,1,0:T(8,128)(2,1)S(1)} %collective-permute-done.27.refs_3_), channel_id=1, source_target_pairs={{2,3},{6,7},{10,11},{14,15},{18,19},{22,23},{26,27},{30,31}} | collective-permute-start | bytes 786440 | tf_op jit(solution)/shard_map/ppermute | solution.py:410
  95.4 17.5 %collective-permute-start.30 = (bf16[2,256,256]{2,1,0:T(8,128)(2,1)S(1)}, bf16[2,256,256]{2,1,0:T(8,128)(2,1)S(1)}, u32[]{:S(2)}, u32[]{:S(2)}) collective-permute-start(bf16[2,256,256]{2,1,0:T(8,128)(2,1)S(1)} %collective-permute-done.29.refs_5_), channel_id=1, source_target_pairs={{2,3},{6,7},{10,11},{14,15},{18,19},{22,23},{26,27},{30,31}} | collective-permute-start | bytes 786440 | tf_op jit(solution)/shard_map/ppermute | solution.py:410
  96.7 18.3 %collective-permute-start.33 = (bf16[2,512,256]{2,1,0:T(8,128)(2,1)S(1)}, bf16[2,512,256]{2,1,0:T(8,128)(2,1)S(1)}, u32[]{:S(2)}, u32[]{:S(2)}) collective-permute-start(bf16[2,512,256]{2,1,0:T(8,128)(2,1)S(1)} %shard_map.73.refs_4_.refs_6_), channel_id=1, source_target_pairs={{4,0},{12,8},{20,16},{28,24},{5,1},{13,9},{21,17},{29,25},{6,2},{1... | collective-permute-start | bytes 1572872 | tf_op jit(solution)/shard_map/ppermute | solution.py:275
  102.0 13.0 %collective-permute-start.31 = (bf16[2,512,256]{2,1,0:T(8,128)(2,1)S(1)}, bf16[2,512,256]{2,1,0:T(8,128)(2,1)S(1)}, u32[]{:S(2)}, u32[]{:S(2)}) collective-permute-start(bf16[2,512,256]{2,1,0:T(8,128)(2,1)S(1)} %shard_map.74.refs_2_), channel_id=1, source_target_pairs={{4,0},{12,8},{20,16},{28,24},{5,1},{13,9},{21,17},{29,25},{6,2},{1... | collective-permute-start | bytes 1572872 | tf_op jit(solution)/shard_map/ppermute | solution.py:275
  107.4 7.6 %collective-permute-start.34 = (bf16[2,512,256]{2,1,0:T(8,128)(2,1)S(1)}, bf16[2,512,256]{2,1,0:T(8,128)(2,1)S(1)}, u32[]{:S(2)}, u32[]{:S(2)}) collective-permute-start(bf16[2,512,256]{2,1,0:T(8,128)(2,1)S(1)} %shard_map.76.refs_7_), channel_id=1, source_target_pairs={{0,4},{8,12},{16,20},{24,28},{1,5},{9,13},{17,21},{25,29},{2,6},{1... | collective-permute-start | bytes 1572872 | tf_op jit(solution)/shard_map/ppermute | solution.py:278
  113.7 4.4 %collective-permute-start.32 = (bf16[2,512,256]{2,1,0:T(8,128)(2,1)S(1)}, bf16[2,512,256]{2,1,0:T(8,128)(2,1)S(1)}, u32[]{:S(2)}, u32[]{:S(2)}) collective-permute-start(bf16[2,512,256]{2,1,0:T(8,128)(2,1)S(1)} %shard_map.77.refs_3_), channel_id=1, source_target_pairs={{0,4},{8,12},{16,20},{24,28},{1,5},{9,13},{17,21},{25,29},{2,6},{1... | collective-permute-start | bytes 1572872 | tf_op jit(solution)/shard_map/ppermute | solution.py:278
  (13 other events, 51.4 us)

commit v2 on v1

v2 whole, which is shorter than its diff:
```python
import functools

import jax
import jax.numpy as jnp
from jax import lax
from jax.experimental import pallas as pl
from jax.experimental.pallas import tpu as pltpu
from jax.sharding import PartitionSpec as P

MODES = 2
REACH = 3
BF = jnp.bfloat16
F32 = jnp.float32
CUTS = 2
PARTS = 1
AHEAD = 0

VMEM = pl.BlockSpec(memory_space=pltpu.VMEM)
SMEM = pl.BlockSpec(memory_space=pltpu.SMEM)
ANY = pl.BlockSpec(memory_space=pl.ANY)


def dot(left, right):
    return jnp.dot(left, right, preferred_element_type=F32)


def dot_t(left, right):
    return lax.dot_general(left, right, (((1,), (1,)), ((), ())), preferred_element_type=F32)


def call(kernel, outs, scalars, arrays, flops, scratch=(), after=(), tied=()):
    moved = sum(a.size * a.dtype.itemsize for a in [*arrays, *outs])
    inputs = len(scalars) + len(arrays)

    def body(*refs):
        tied_refs = refs[inputs : inputs + len(tied)]
        rest = refs[inputs + len(tied) + len(after) :]
        kernel(*refs[:inputs], *rest[: len(outs)], *rest[len(outs) + len(tied) :])
        for source, target in zip(tied_refs, rest[len(outs) :]):
            target[...] = source[...]

    found = pl.pallas_call(
        body,
        out_shape=[*outs, *(jax.ShapeDtypeStruct(t.shape, t.dtype) for t in tied)],
        in_specs=[SMEM] * len(scalars)
        + [VMEM] * (len(arrays) + len(tied))
        + [ANY] * len(after),
        out_specs=[VMEM] * (len(outs) + len(tied)),
        scratch_shapes=list(scratch),
        compiler_params=pltpu.CompilerParams(vmem_limit_bytes=16 * 2**20),
        cost_estimate=pl.CostEstimate(flops=flops, bytes_accessed=moved, transcendentals=0),
    )(*scalars, *arrays, *tied, *after)
    return found[0] if len(found) == 1 else list(found)


def block(*shape):
    return jax.ShapeDtypeStruct(shape, BF)


def either(core_ref, number, work):
    for n in range(2):
        pl.when(core_ref[0] == (number ^ n))(functools.partial(work, n))


def self_energy_patch(spots, scalars, above_by, below_by, pieces, results):
    rows, width = above_by.shape[1:]

    def kernel(*refs):
        refs = list(refs)
        scalar_refs = [refs.pop(0) for _ in scalars]
        above_ref, below_ref = refs.pop(0), refs.pop(0)
        table = refs.pop()
        notes = []
        for n in range(len(pieces)):
            piece_ref = refs.pop(0)
            for each in range(4):
                table[2 * n + each // 2, each % 2] = piece_ref[each * rows : (each + 1) * rows]
            if pieces[n].shape[0] > 4 * rows:
                notes.append(piece_ref[4 * rows : 4 * rows + 16, :128].astype(jnp.int32))
        places = spots(scalar_refs, notes)
        step = 16

        def strip(i, carry):
            at = pl.ds(pl.multiple_of(i * step, step), step)
            factors = [
                (above_ref[m, at, :], below_ref[m, at, :]) for m in range(MODES)
            ]
            for n in range(results):
                for part in range(2):
                    total = None
                    for m in range(MODES):
                        for place, factor in zip(places[n][m], factors[m]):
                            term = factor * table[place, part, at, :].astype(F32)
                            total = term if total is None else total + term
                    refs[n][part, at, :] = total.astype(BF)
            return carry

        lax.fori_loop(0, rows // step, strip, 0)

    return call(
        kernel,
        [block(2, rows, width)] * results,
        scalars,
        [above_by, below_by, *pieces],
        results * 2 * rows * width * 12,
        [pltpu.VMEM((2 * len(pieces), 2, rows, width), BF)],
    )


def rows_at(pieces, part, i, tile):
    n, at = divmod(i, pieces[0].shape[1])
    return pieces[n], (part, slice(at, at + tile), slice(None))


def rows_in(pieces, part, i, tile):
    ref, at = rows_at(pieces, part, i, tile)
    return ref[at]


def put_rows(pieces, part, i, tile, value):
    ref, at = rows_at(pieces, part, i, tile)
    ref[at] = value.astype(BF)


def times_into(left, right, outs):
    size = left.shape[1]
    tile = min(256, outs[0].shape[1])
    real, imag = right[0], right[1]
    for i in range(0, size, tile):
        lr, li = left[0, i : i + tile, :], left[1, i : i + tile, :]
        put_rows(outs, 0, i, tile, dot(lr, real) - dot(li, imag))
        put_rows(outs, 1, i, tile, dot(lr, imag) + dot(li, real))


def times(core, number, lefts, groups, places=None, after=(), tied=()):
    size = lefts[0].shape[1]
    rows, width = groups[0][0].shape[1:]
    full = (2, rows * len(groups), width)
    counts = [len(group) for group in groups]
    scalars = [core] if places is None else [core, places]
    whole = counts == [1]

    def kernel(core_ref, *refs):
        refs = list(refs)
        places_ref = refs.pop(0) if places is not None else None
        left_refs = [refs.pop(0) for _ in range(2)]
        if whole:
            right, *out_refs = refs
        else:
            right = refs.pop()
            out_refs = refs[-CUTS:]
            for n, count in enumerate(counts):
                if places_ref is None:
                    at = slice(n * rows, (n + 1) * rows)
                else:
                    at = pl.ds(pl.multiple_of(places_ref[n] * rows, rows), rows)
                value = refs.pop(0)[...]
                for _ in range(count - 1):
                    value = value + refs.pop(0)[...]
                right[:, at, :] = value
        either(core_ref, number, lambda n: times_into(left_refs[n], right, out_refs))

    return call(
        kernel,
        [block(2, size // CUTS, width)] * CUTS,
        scalars,
        [*lefts, *sum(groups, [])],
        8 * size * size * width,
        [] if whole else [pltpu.VMEM(full, BF)],
        after,
        tied,
    )


def transfer_of(green, coupling, copies=1, after=()):
    size = coupling.shape[0]

    def kernel(green_ref, coupling_ref, *out_refs):
        for part in range(2):
            value = dot(green_ref[part], coupling_ref[...]).astype(BF)
            for out_ref in out_refs:
                out_ref[part] = value

    outs = [block(*green.shape)] * copies
    return call(kernel, outs, [], [green, coupling], 4 * size**3, (), after)


def composed(wanted, left, groups, after=()):
    size = left.shape[1]

    def kernel(wanted_ref, left_ref, *refs):
        *right_refs, out_ref, right = refs

        @pl.when(wanted_ref[0] == 1)
        def _():
            value = right_refs[0][...]
            for ref in right_refs[1:]:
                value = value + ref[...]
            right[...] = value
            times_into(left_ref, right, [out_ref])

        @pl.when(wanted_ref[0] != 1)
        def _():
            out_ref[...] = left_ref[...]

    return call(
        kernel,
        [block(*left.shape)],
        [wanted],
        [left, *groups],
        8 * size**3,
        [pltpu.VMEM(left.shape, BF)],
        after,
    )


def adjoint_into(mine, theirs, right, mine_at, theirs_at, to_at, store):
    size = right.shape[1]
    tile = min(256, mine[0].shape[1])
    a = [right[p, to_at, mine_at] for p in range(2)]
    b = [right[p, to_at, theirs_at] for p in range(2)]
    for i in range(0, size, tile):
        mr, mi = (rows_in(mine, part, i, tile) for part in range(2))
        tr, ti = (rows_in(theirs, part, i, tile) for part in range(2))
        real = dot_t(mr, a[0]) + dot_t(mi, a[1]) + dot_t(tr, b[0]) + dot_t(ti, b[1])
        imag = dot_t(mi, a[0]) - dot_t(mr, a[1]) + dot_t(ti, b[0]) - dot_t(tr, b[1])
        store(i, tile, real, imag)


def split(refs, *counts):
    refs, found = list(refs), []
    for count in counts:
        found.append(refs[:count])
        refs = refs[count:]
    return *found, refs


def adjoint_half(core, number, mine, theirs, rights, summand=(), cuts=1, after=()):
    half, size = mine[0].shape[2], rights[0].shape[1]

    def kernel(core_ref, *refs):
        mine_refs, theirs_refs, right_refs, sum_refs, out_refs = split(
            refs, len(mine), len(theirs), 2, len(summand)
        )

        def store(i, tile, *values):
            for part, value in enumerate(values):
                if sum_refs:
                    value = value + rows_in(sum_refs, part, i, tile).astype(F32)
                put_rows(out_refs, part, i, tile, value)

        def work(n):
            held = number ^ n
            own = slice(held * half, (held + 1) * half)
            other = slice((1 - held) * half, (2 - held) * half)
            adjoint_into(mine_refs, theirs_refs, right_refs[n], own, other, own, store)

        either(core_ref, number, work)

    arrays = [*mine, *theirs, *rights, *summand]
    found = call(
        kernel, [block(2, size // cuts, half)] * cuts, [core], arrays, 16 * size * half * half, (), after
    )
    return [found] if cuts == 1 else list(found)


def adjoint_own(core, mines, theirs, right, sums, other_sums):
    half, size = mines[0][0].shape[2], right.shape[1]
    lists = [*mines, *theirs, *sums, *other_sums]

    def kernel(core_ref, right_ref, *refs):
        *groups, (out_ref,) = split(refs, *(len(each) for each in lists))

        def work(n):
            mine_refs, theirs_refs, sum_refs, other_refs = groups[n::2]
            own, other = slice(n * half, (n + 1) * half), slice((1 - n) * half, (2 - n) * half)
            for to, summand in ((own, sum_refs), (other, other_refs)):

                def store(i, tile, *values):
                    for part, value in enumerate(values):
                        value = value + rows_in(summand, part, i, tile).astype(F32)
                        out_ref[part, i : i + tile, to] = value.astype(BF)

                adjoint_into(mine_refs, theirs_refs, right_ref, own, other, to, store)

        either(core_ref, 0, work)

    out = jax.ShapeDtypeStruct((2, size, size), BF)
    return call(kernel, [out], [core], [right, *sum(lists, [])], 8 * size**3)


def on_device(left_green, coupling, previous_lesser, screened, offsets, occupation):
    energies, slabs = lax.axis_size("energy"), lax.axis_size("slab")
    me, slab = lax.axis_index("energy"), lax.axis_index("slab")
    pairs = energies // 2
    pair, core = me // 2, me % 2
    first = core == 0
    size = coupling.shape[1]
    half = size // 2
    core_s = core[None]

    def swap(value):
        return lax.ppermute(value, "energy", [(i, i ^ 1) for i in range(energies)])

    def to_even(value):
        return lax.ppermute(value, "energy", [(i + 1, i) for i in range(0, energies, 2)])

    def to_odd(value):
        return lax.ppermute(value, "energy", [(i, i + 1) for i in range(0, energies, 2)])

    def by_energy(own, other):
        return jnp.where(first, own, other), jnp.where(first, other, own)

    green = left_green[:, 0, 0]
    before = previous_lesser[:, 0, 0]

    def column_half(value):
        return lax.dynamic_slice_in_dim(value, core * half, half, value.ndim - 1)

    both = [before, swap(before)]
    two = jnp.concatenate([offsets, swap(offsets)])
    spread = pairs in (2, 4) and size % (16 * pairs) == 0
    if spread:
        rows = size // pairs

        def across(value, d):
            moves = [(i, i ^ (2 * d)) for i in range(energies)]
            return lax.ppermute(value, "energy", moves)

        def patch(value, which):
            corner = (0, which * rows, core * half)
            return lax.dynamic_slice(value, corner, (2, rows, half))

        notes = jnp.pad(two.reshape(2 * MODES, 1).astype(BF), ((0, 16 - 2 * MODES), (0, 0)))
        notes = jnp.broadcast_to(notes, (16, half))
        order = list(reversed(range(1, pairs)))

        def patches(which):
            return jnp.concatenate(
                [patch(value, which).reshape(2 * rows, half) for value in both] + [notes]
            )

        sent = [patches(pair ^ d) for d in range(pairs)]
        pieces = sent[:1] + [None] * (pairs - 1)
        for d in order:
            pieces[d] = across(sent[d], d)
        first_sent = sent[1:]
        weights = patch(screened[:, 0], pair)
        places = pair ^ jnp.arange(pairs, dtype=jnp.int32)
        scalars = [me[None]]

        def spots(scalar_refs, carrier_refs):
            here = scalar_refs[0][0]
            found = [[None] * pairs for _ in range(2)]
            core_here = lax.rem(here, 2)
            for d in range(pairs):
                note = carrier_refs[d]
                line = lax.broadcasted_iota(jnp.int32, note.shape, 0)
                for n in range(2):
                    holder = here ^ (2 * d) ^ (core_here ^ n)
                    at = []
                    for m in range(MODES):
                        wanted_line = MODES * (core_here ^ n) + m
                        o = jnp.max(jnp.where(line == wanted_line, note, 0))
                        higher = lax.rem(holder + o, energies) ^ here
                        lower = lax.rem(holder - o + energies, energies) ^ here
                        at.append((higher, lower))
                    found[n][d] = at
            return found[0] + found[1]
    else:
        near = (REACH + 1) // 2
        pieces = []
        for d in range(-near, near + 1):
            moves = [(i, (i - 2 * d) % energies) for i in range(energies)]
            value = jnp.concatenate([column_half(v).reshape(2 * size, half) for v in both])
            pieces.append(lax.ppermute(value, "energy", moves) if d else value)
        weights = column_half(screened[:, 0])
        places, first_sent = None, []
        scalars = [core_s, two]

        def spots(scalar_refs, piece_refs):
            core_ref, two_ref = scalar_refs

            def place(away):
                away = away + 2 * near
                return 2 * lax.div(away, 2) + (lax.rem(away, 2) ^ core_ref[0])

            found = []
            for n in range(2):
                shift = [two_ref[core_ref[0] ^ n, m] for m in range(MODES)]
                found.append([(place(n + o), place(n - o)) for o in shift])
            return found

    own, own_sent = transfer_of(green, coupling[0], 2, first_sent)

    def maps_before(span, own):
        found, moving = [], own
        for hop in range(span):
            moves = [
                (s + hop - 1, s + hop)
                for s in range(3 * span, slabs, 2 * span)
                if s + hop < slabs
            ]
            moving = lax.ppermute(moving, "slab", moves)
            found.append(moving)
        return found

    def swap_all(values):
        return [swap(value) for value in values]

    def arrivals(span, values):
        groups = []
        for moving in values:
            group = []
            for hop in range(span):
                moves = [
                    (s + hop - 1, s + hop)
                    for s in range(span, slabs, 2 * span)
                    if s + hop < slabs
                ]
                moving = lax.ppermute(moving, "slab", moves)
                group.append(moving)
            groups.append(group)
        return groups

    other_green = swap(green)
    lefts = (green, other_green)
    above_by = weights.astype(F32)
    below_by = above_by * occupation[:, None, None]
    found = self_energy_patch(
        spots, scalars, above_by, below_by, pieces, 2 * pairs if spread else 2
    )
    maps = (own, transfer_of(other_green, coupling[0], 1, found[:1]))
    befores = maps_before(1, own_sent) if slabs > 2 else []
    if spread:
        early, late = list(found[:pairs]), list(found[pairs:])
        for d in order:
            early[d] = across(early[d], d)
        early = [[part] for part in early]
        *product, late[1], late[2:] = (
            lambda out: (*out[:CUTS], out[CUTS], list(out[CUTS + 1 :]))
        )(times(core_s, 0, lefts, early, places, maps[1:], late[1:]))
        for d in order:
            late[d] = across(late[d], d)
    else:
        product = times(core_s, 0, lefts, [[found[0]]], None, maps[1:])
        late = [found[1]]
    sums = [adjoint_half(core_s, 0, product, swap_all(product), lefts, (), 1, befores)]
    groups = [arrivals(1, sums[0])]
    product = times(core_s, 1, lefts, [[part] for part in late], places, sums[0])
    sums.append(adjoint_half(core_s, 1, product, swap_all(product), lefts))
    groups.append(arrivals(1, sums[1]))

    span = 1
    while 2 * span < slabs:
        carried = times(core_s, 0, maps, groups[0])
        early = adjoint_half(core_s, 0, carried, swap_all(carried), maps, sums[0], PARTS)
        early_groups = arrivals(2 * span, early)
        wanted = lax.rem(slab // span, 2)[None]
        own = composed(wanted, own, befores, after=early)
        ahead = [group[0] for group in early_groups]
        carried = times(core_s, 1, maps, groups[1], None, [own, *early, *ahead[:AHEAD]])
        behind = ahead[AHEAD:]
        late = adjoint_half(core_s, 1, carried, swap_all(carried), maps, sums[1], 2, behind)
        sums, groups = [early, late], [early_groups, arrivals(2 * span, late)]
        maps = (own, swap(own))
        span *= 2
        if 2 * span < slabs:
            befores = maps_before(span, own)
    if slabs > 1:
        others = [swap_all(value) for value in sums]
        carried = [times(core_s, n, maps, groups[n]) for n in range(2)]
        theirs = [swap_all(value) for value in carried]
        result = adjoint_own(core_s, carried, theirs, maps[0], sums, others)
        return result[:, None, None]
    sums = [value[0] for value in sums]
    result = jnp.where(first, sums[0], sums[1])
    other = swap(jnp.where(first, sums[1], sums[0]))
    return jnp.concatenate(by_energy(result, other), axis=2)[:, None, None]


def solution(mesh):
    placed = (
        P(None, "energy", "slab", None, None),
        P("slab", None, None),
        P(None, "energy", "slab", None, None),
        P(None, "slab", None, None),
        P("energy", None),
        P(),
    )
    return jax.shard_map(
        on_device,
        mesh=mesh,
        in_specs=placed,
        out_specs=P(None, "energy", "slab", None, None),
        check_vma=False,
    )
```

time: 121 us -> 110 us (0.909)
  waiting for transfers between devices: 51 us -> 42.6 us
  local copies, waits for them, and re-layouts: 6.79 us -> 3.83 us
  other arithmetic: 0.05 us -> 2.21 us
  starting transfers between devices: 41.6 us -> 40.2 us
    ppermute x8 -> x19, starting transfers between devices: 7.57 us -> 21.6 us  [swap(): return lax.ppermute(value, 'energy', [(i, i ^ 1) for i in range(energies)])]
    ppermute x10 -> x8, waiting for transfers between devices: 33 us -> 19 us  [arrivals(): moving = lax.ppermute(moving, 'slab', moves)]
    ppermute x4 -> x0, starting transfers between devices: 11.2 us -> none  [the longest x2 8.66 us: to_even(): lax.ppermute(value, 'energy', [(i + 1, i) for i in range(0, energies, 2)])]
    ppermute x12 -> x9, waiting for transfers between devices: 14.1 us -> 20 us  [across(): return lax.ppermute(value, 'energy', moves)]
    ppermute x4 -> x0, waiting for transfers between devices: 3.08 us -> none  [the longest x2 3.07 us: to_odd(): lax.ppermute(value, 'energy', [(i, i + 1) for i in range(0, energies, 2)])]
    ppermute x12 -> x9, starting transfers between devices: 11 us -> 8.14 us  [across(): return lax.ppermute(value, 'energy', moves)]
    ppermute x8 -> x19, waiting for transfers between devices: 0.85 us -> 3.59 us  [swap(): return lax.ppermute(value, 'energy', [(i, i ^ 1) for i in range(energies)])]
    dynamic_slice x3 -> x2, local copies, waits for them, and re-layouts: 3.1 us -> 1.18 us  [patch(): return lax.dynamic_slice(value, corner, (2, rows, half))]
  transfers between devices with their start and end apart: 35 -> 37, of which waited for: 17 -> 19; matrix products, arithmetic and copies ran while one was open for 3% -> 3% of each run, Pallas kernels for 11% -> 15%
where the time goes in v2:
time: 110 us
  waiting for transfers between devices  42.6 us (39%)
  starting transfers between devices  40.2 us (37%)
  Pallas kernels  20.6 us (19%)
  local copies, waits for them, and re-layouts  3.83 us (3%)
  other arithmetic  2.21 us (2%)
    ppermute x19, starting transfers between devices, swap(): return lax.ppermute(value, 'energy', [(i, i ^ 1) for i in range(energies)])  21.6 us
    pallas_call x15, Pallas kernels, call(): pl.pallas_call(body, out_shape=[*outs, *(jax.ShapeDtypeStruct(t.shape, t....  20.6 us
    ppermute x9, waiting for transfers between devices, across(): return lax.ppermute(value, 'energy', moves)  20 us
    ppermute x8, waiting for transfers between devices, arrivals(): moving = lax.ppermute(moving, 'slab', moves)  19 us
    ppermute x8, starting transfers between devices, arrivals(): moving = lax.ppermute(moving, 'slab', moves)  9.24 us
    ppermute x9, starting transfers between devices, across(): return lax.ppermute(value, 'energy', moves)  8.14 us
    ppermute x19, waiting for transfers between devices, swap(): return lax.ppermute(value, 'energy', [(i, i ^ 1) for i in range(energies)])  3.59 us
    unnamed x12, local copies, waits for them, and re-layouts  2.55 us
  transfers between devices with their start and end apart: 37, of which 19 were waited for; matrix products, arithmetic and copies ran while one was open for 3% of the time, Pallas kernels for 15%

profile of v2, /device:TPU:25, one launch (start us, length us, event | category | flops | bytes accessed | tf_op | source)
XLA Modules:
  0.0 109.8 jit_solution(9692123774815375704)
XLA Ops:
  5.3 1.3 %collective-permute-start.2 = (bf16[2,512,512]{2,1,0:T(8,128)(2,1)S(1)}, bf16[2,512,512]{2,1,0:T(8,128)(2,1)S(1)}, u32[]{:S(2)}, u32[]{:S(2)}) collective-permute-start(bf16[2,512,512]{2,1,0:T(8,128)(2,1)S(1)} %get-tuple-element.33), channel_id=1, source_target_pairs={{2,3},{6,7},{10,11},{14,15},{18,19},{22,23},{26,27},{30,31}} | collective-permute-start | bytes 3145736 | tf_op jit(solution)/shard_map/ppermute | solution.py:404
  6.6 1.3 %collective-permute-start.5 = (bf16[528,256]{1,0:T(8,128)(2,1)S(1)}, bf16[528,256]{1,0:T(8,128)(2,1)S(1)}, u32[]{:S(2)}, u32[]{:S(2)}) collective-permute-start(bf16[528,256]{1,0:T(8,128)(2,1)S(1)} %get-tuple-element.68.refs_3_), channel_id=1, source_target_pairs={{0,16},{4,20},{8,24},{12,28},{16,0},{20,4},{24,8},{28,12},{1,17},{... | collective-permute-start | bytes 811016 | tf_op jit(solution)/shard_map/ppermute | solution.py:328
  11.3 8.9 %collective-permute-done.5.refs_5_ = bf16[528,256]{1,0:T(8,128)(2,1)S(1)} collective-permute-done((bf16[528,256]{1,0:T(8,128)(2,1)S(1)}, bf16[528,256]{1,0:T(8,128)(2,1)S(1)}, u32[]{:S(2)}, u32[]{:S(2)}) %collective-permute-start.5) | collective-permute-done | bytes 270368 | tf_op jit(solution)/shard_map/ppermute | solution.py:328
  22.3 1.3 %collective-permute-start.7 = (bf16[2,128,256]{2,1,0:T(8,128)(2,1)S(1)}, bf16[2,128,256]{2,1,0:T(8,128)(2,1)S(1)}, u32[]{:S(2)}, u32[]{:S(2)}) collective-permute-start(bf16[2,128,256]{2,1,0:T(8,128)(2,1)S(1)} %get-tuple-element.35), channel_id=1, source_target_pairs={{0,8},{4,12},{8,0},{12,4},{16,24},{20,28},{24,16},{28,20},{1,9},{5... | collective-permute-start | bytes 393224 | tf_op jit(solution)/shard_map/ppermute | solution.py:328
  27.7 2.9 %collective-permute-done.9.refs_7_ = bf16[2,128,256]{2,1,0:T(8,128)(2,1)S(1)} collective-permute-done((bf16[2,128,256]{2,1,0:T(8,128)(2,1)S(1)}, bf16[2,128,256]{2,1,0:T(8,128)(2,1)S(1)}, u32[]{:S(2)}, u32[]{:S(2)}) %collective-permute-start.9) | collective-permute-done | bytes 131104 | tf_op jit(solution)/shard_map/ppermute | solution.py:328
  30.6 1.3 %shard_map.67 = (bf16[2,256,256]{2,1,0:T(8,128)(2,1)S(1)}, bf16[2,256,256]{2,1,0:T(8,128)(2,1)S(1)}, bf16[2,128,256]{2,1,0:T(8,128)(2,1)S(1)}, bf16[2,128,256]{2,1,0:T(8,128)(2,1)S(1)}, bf16[2,128,256]{2,1,0:T(8,128)(2,1)S(1)}) custom-call(s32[1]{0:T(128)} %bitcast.refs_0_, s32[4]{0:T(128)S(1)} %iota_xor_fusion.refs_1_, bf16[2,512,512]{2,1,0:T(8,128)(2,1)S(1)} %bitcast.27, ...), custom_call_target="tpu_custom_call" | custom-call | flops 536870912 | bytes 3145728 | tf_op jit(solution)/shard_map/pallas_call | solution.py:42
  31.9 2.5 %collective-permute-start.10 = (bf16[2,256,256]{2,1,0:T(8,128)(2,1)S(1)}, bf16[2,256,256]{2,1,0:T(8,128)(2,1)S(1)}, u32[]{:S(2)}, u32[]{:S(2)}) collective-permute-start(bf16[2,256,256]{2,1,0:T(8,128)(2,1)S(1)} %get-tuple-element.41.refs_1_), channel_id=1, source_target_pairs={{0,4},{4,0},{8,12},{12,8},{16,20},{20,16},{24,28},{28,24},{1,5},{5... | collective-permute-start | bytes 786440 | tf_op jit(solution)/shard_map/ppermute | solution.py:303
  37.0 1.3 %collective-permute-start.12 = (bf16[2,512,256]{2,1,0:T(8,128)(2,1)S(1)}, bf16[2,512,256]{2,1,0:T(8,128)(2,1)S(1)}, u32[]{:S(2)}, u32[]{:S(2)}) collective-permute-start(bf16[2,512,256]{2,1,0:T(8,128)(2,1)S(1)} %shard_map.68.refs_7_.refs_8_), channel_id=1, source_target_pairs={{0,1},{2,3},{4,5},{6,7},{8,9},{10,11},{12,13},{14,15},{16,17},{18,... | collective-permute-start | bytes 1572872 | tf_op jit(solution)/shard_map/ppermute | solution.py:421
  39.1 1.8 %collective-permute-start.20 = (bf16[2,128,256]{2,1,0:T(8,128)(2,1)S(1)}, bf16[2,128,256]{2,1,0:T(8,128)(2,1)S(1)}, u32[]{:S(2)}, u32[]{:S(2)}) collective-permute-start(bf16[2,128,256]{2,1,0:T(8,128)(2,1)S(1)} %get-tuple-element.50), channel_id=1, source_target_pairs={{0,24},{4,28},{8,16},{12,20},{16,8},{20,12},{24,0},{28,4},{1,25},{... | collective-permute-start | bytes 393224 | tf_op jit(solution)/shard_map/ppermute | solution.py:328
  41.0 2.1 %collective-permute-done.18.refs_5_ = bf16[2,128,256]{2,1,0:T(8,128)(2,1)S(1)} collective-permute-done((bf16[2,128,256]{2,1,0:T(8,128)(2,1)S(1)}, bf16[2,128,256]{2,1,0:T(8,128)(2,1)S(1)}, u32[]{:S(2)}, u32[]{:S(2)}) %collective-permute-start.18) | collective-permute-done | bytes 131104 | tf_op jit(solution)/shard_map/ppermute | solution.py:328
  43.0 3.3 %collective-permute-done.20.refs_7_ = bf16[2,128,256]{2,1,0:T(8,128)(2,1)S(1)} collective-permute-done((bf16[2,128,256]{2,1,0:T(8,128)(2,1)S(1)}, bf16[2,128,256]{2,1,0:T(8,128)(2,1)S(1)}, u32[]{:S(2)}, u32[]{:S(2)}) %collective-permute-start.20) | collective-permute-done | bytes 131104 | tf_op jit(solution)/shard_map/ppermute | solution.py:328
  46.3 1.3 %shard_map.73 = (bf16[2,256,256]{2,1,0:T(8,128)(2,1)S(1)}, bf16[2,256,256]{2,1,0:T(8,128)(2,1)S(1)}) custom-call(s32[1]{0:T(128)} %bitcast.refs_0_, s32[4]{0:T(128)S(1)} %iota_xor_fusion.refs_1_, bf16[2,512,512]{2,1,0:T(8,128)(2,1)S(1)} %bitcast.29, bf16[2,512,512]{2,1,0:T(8,128)(2,1)S(1)} %collective-permute-done.3.refs_0_.refs_3_.refs_6_, ...), custom_call_target="tpu_custom_call" | custom-call | flops 536870912 | bytes 3145728 | tf_op jit(solution)/shard_map/pallas_call | solution.py:42
  47.6 1.3 %collective-permute-start.21 = (bf16[2,256,256]{2,1,0:T(8,128)(2,1)S(1)}, bf16[2,256,256]{2,1,0:T(8,128)(2,1)S(1)}, u32[]{:S(2)}, u32[]{:S(2)}) collective-permute-start(bf16[2,256,256]{2,1,0:T(8,128)(2,1)S(1)} %get-tuple-element.51.refs_1_), channel_id=1, source_target_pairs={{0,4},{4,0},{8,12},{12,8},{16,20},{20,16},{24,28},{28,24},{1,5},{5... | collective-permute-start | bytes 786440 | tf_op jit(solution)/shard_map/ppermute | solution.py:303
  48.9 3.1 %collective-permute-done.12.refs_3_ = bf16[2,512,256]{2,1,0:T(8,128)(2,1)S(1)} collective-permute-done((bf16[2,512,256]{2,1,0:T(8,128)(2,1)S(1)}, bf16[2,512,256]{2,1,0:T(8,128)(2,1)S(1)}, u32[]{:S(2)}, u32[]{:S(2)}) %collective-permute-start.12) | collective-permute-done | bytes 524320 | tf_op jit(solution)/shard_map/ppermute | solution.py:421
  52.7 1.3 %collective-permute-start.13 = (bf16[2,256,256]{2,1,0:T(8,128)(2,1)S(1)}, bf16[2,256,256]{2,1,0:T(8,128)(2,1)S(1)}, u32[]{:S(2)}, u32[]{:S(2)}) collective-permute-start(bf16[2,256,256]{2,1,0:T(8,128)(2,1)S(1)} %get-tuple-element.43.refs_1_), channel_id=1, source_target_pairs={{0,4},{4,0},{8,12},{12,8},{16,20},{20,16},{24,28},{28,24},{1,5},{5... | collective-permute-start | bytes 786440 | tf_op jit(solution)/shard_map/ppermute | solution.py:303
  54.1 1.5 %shard_map.74.refs_7_ = bf16[2,512,256]{2,1,0:T(8,128)(2,1)} custom-call(s32[1]{0:T(128)} %bitcast.refs_0_, bf16[2,256,256]{2,1,0:T(8,128)(2,1)S(1)} %get-tuple-element.51.refs_1_, bf16[2,256,256]{2,1,0:T(8,128)(2,1)S(1)} %get-tuple-element.52.refs_2_, bf16[2,256,256]{2,1,0:T(8,128)(2,1)S(1)} %collective-permute-done.21.refs_3_, ...), custom_call_target="tpu_custom_call" | custom-call | flops 536870912 | bytes 3670016 | tf_op jit(solution)/shard_map/pallas_call | solution.py:42
  55.6 1.3 %collective-permute-start.23 = (bf16[2,512,256]{2,1,0:T(8,128)(2,1)}, bf16[2,512,256]{2,1,0:T(8,128)(2,1)}, u32[]{:S(2)}, u32[]{:S(2)}) collective-permute-start(bf16[2,512,256]{2,1,0:T(8,128)(2,1)} %shard_map.74.refs_7_), channel_id=1, source_target_pairs={{0,1},{2,3},{4,5},{6,7},{8,9},{10,11},{12,13},{14,15},{16,17},{18,... | collective-permute-start | bytes 1572872 | tf_op jit(solution)/shard_map/ppermute | solution.py:421
  56.9 1.6 %shard_map.70.refs_3_.refs_5_.refs_10_ = bf16[2,512,256]{2,1,0:T(8,128)(2,1)} custom-call(s32[1]{0:T(128)} %bitcast.refs_0_, bf16[2,256,256]{2,1,0:T(8,128)(2,1)S(1)} %get-tuple-element.43.refs_1_, bf16[2,256,256]{2,1,0:T(8,128)(2,1)S(1)} %get-tuple-element.44.refs_2_, bf16[2,256,256]{2,1,0:T(8,128)(2,1)S(1)} %collective-permute-done.13.refs_3_, ...), custom_call_target="tpu_custom_call" | custom-call | flops 536870912 | bytes 4194304 | tf_op jit(solution)/shard_map/pallas_call | solution.py:42
  58.5 1.5 %collective-permute-start.16 = (bf16[2,512,256]{2,1,0:T(8,128)(2,1)}, bf16[2,512,256]{2,1,0:T(8,128)(2,1)}, u32[]{:S(2)}, u32[]{:S(2)}) collective-permute-start(bf16[2,512,256]{2,1,0:T(8,128)(2,1)} %shard_map.70.refs_3_.refs_5_.refs_10_), channel_id=1, source_target_pairs={{1,2},{5,6},{9,10},{13,14},{17,18},{21,22},{25,26},{29,30}} | collective-permute-start | bytes 1572872 | tf_op jit(solution)/shard_map/ppermute | solution.py:421
  62.9 7.9 %collective-permute-done.23.refs_3_ = bf16[2,512,256]{2,1,0:T(8,128)(2,1)} collective-permute-done((bf16[2,512,256]{2,1,0:T(8,128)(2,1)}, bf16[2,512,256]{2,1,0:T(8,128)(2,1)}, u32[]{:S(2)}, u32[]{:S(2)}) %collective-permute-start.23) | collective-permute-done | bytes 524320 | tf_op jit(solution)/shard_map/ppermute | solution.py:421
  70.9 1.8 %shard_map.75 = (bf16[2,256,256]{2,1,0:T(8,128)(2,1)S(1)}, bf16[2,256,256]{2,1,0:T(8,128)(2,1)S(1)}) custom-call(s32[1]{0:T(128)} %bitcast.refs_0_, bf16[2,512,512]{2,1,0:T(8,128)(2,1)S(1)} %get-tuple-element.32.refs_1_.refs_5_, bf16[2,512,512]{2,1,0:T(8,128)(2,1)S(1)} %shard_map.66.refs_11_.refs_2_.refs_6_, ...), custom_call_target="tpu_custom_call" | custom-call | flops 536870912 | bytes 3145728 | tf_op jit(solution)/shard_map/pallas_call | solution.py:42
  72.6 1.3 %collective-permute-start.24 = (bf16[2,256,256]{2,1,0:T(8,128)(2,1)S(1)}, bf16[2,256,256]{2,1,0:T(8,128)(2,1)S(1)}, u32[]{:S(2)}, u32[]{:S(2)}) collective-permute-start(bf16[2,256,256]{2,1,0:T(8,128)(2,1)S(1)} %get-tuple-element.53.refs_1_), channel_id=1, source_target_pairs={{0,4},{4,0},{8,12},{12,8},{16,20},{20,16},{24,28},{28,24},{1,5},{5... | collective-permute-start | bytes 786440 | tf_op jit(solution)/shard_map/ppermute | solution.py:303
  74.1 1.3 %collective-permute-start.17 = (bf16[2,512,256]{2,1,0:T(8,128)(2,1)}, bf16[2,512,256]{2,1,0:T(8,128)(2,1)S(1)}, u32[]{:S(2)}, u32[]{:S(2)}) collective-permute-start(bf16[2,512,256]{2,1,0:T(8,128)(2,1)} %collective-permute-done.16.refs_3_.refs_8_), channel_id=1, source_target_pairs={{2,3},{6,7},{10,11},{14,15},{18,19},{22,23},{26,27},{30,31}} | collective-permute-start | bytes 1572872 | tf_op jit(solution)/shard_map/ppermute | solution.py:421
  75.5 1.8 %shard_map.76 = (bf16[2,256,256]{2,1,0:T(8,128)(2,1)S(1)}, bf16[2,256,256]{2,1,0:T(8,128)(2,1)S(1)}) custom-call(s32[1]{0:T(128)} %bitcast.refs_0_, bf16[2,256,256]{2,1,0:T(8,128)(2,1)S(1)} %get-tuple-element.53.refs_1_, bf16[2,256,256]{2,1,0:T(8,128)(2,1)S(1)} %get-tuple-element.54.refs_2_, bf16[2,256,256]{2,1,0:T(8,128)(2,1)S(1)} %collective-permute-done.24.refs_3_, ...), custom_call_target="tpu_custom_call" | custom-call | flops 536870912 | bytes 4194304 | tf_op jit(solution)/shard_map/pallas_call | solution.py:42
  79.1 1.3 %collective-permute-start.27 = (bf16[2,256,256]{2,1,0:T(8,128)(2,1)S(1)}, bf16[2,256,256]{2,1,0:T(8,128)(2,1)S(1)}, u32[]{:S(2)}, u32[]{:S(2)}) collective-permute-start(bf16[2,256,256]{2,1,0:T(8,128)(2,1)S(1)} %collective-permute-done.26.refs_3_), channel_id=1, source_target_pairs={{2,3},{6,7},{10,11},{14,15},{18,19},{22,23},{26,27},{30,31}} | collective-permute-start | bytes 786440 | tf_op jit(solution)/shard_map/ppermute | solution.py:421
  80.4 1.3 %collective-permute-start.29 = (bf16[2,256,256]{2,1,0:T(8,128)(2,1)S(1)}, bf16[2,256,256]{2,1,0:T(8,128)(2,1)S(1)}, u32[]{:S(2)}, u32[]{:S(2)}) collective-permute-start(bf16[2,256,256]{2,1,0:T(8,128)(2,1)S(1)} %collective-permute-done.28.refs_5_), channel_id=1, source_target_pairs={{2,3},{6,7},{10,11},{14,15},{18,19},{22,23},{26,27},{30,31}} | collective-permute-start | bytes 786440 | tf_op jit(solution)/shard_map/ppermute | solution.py:421
  81.7 6.7 %collective-permute-done.17.refs_4_ = bf16[2,512,256]{2,1,0:T(8,128)(2,1)S(1)} collective-permute-done((bf16[2,512,256]{2,1,0:T(8,128)(2,1)}, bf16[2,512,256]{2,1,0:T(8,128)(2,1)S(1)}, u32[]{:S(2)}, u32[]{:S(2)}) %collective-permute-start.17) | collective-permute-done | bytes 524320 | tf_op jit(solution)/shard_map/ppermute | solution.py:421
  88.4 2.3 %collective-permute-start.35 = (bf16[2,256,256]{2,1,0:T(8,128)(2,1)S(1)}, bf16[2,256,256]{2,1,0:T(8,128)(2,1)S(1)}, u32[]{:S(2)}, u32[]{:S(2)}) collective-permute-start(bf16[2,256,256]{2,1,0:T(8,128)(2,1)S(1)} %get-tuple-element.55.refs_11_), channel_id=1, source_target_pairs={{0,4},{4,0},{8,12},{12,8},{16,20},{20,16},{24,28},{28,24},{1,5},{5... | collective-permute-start | bytes 786440 | tf_op jit(solution)/shard_map/ppermute | solution.py:303
  90.7 1.8 %shard_map.72 = (bf16[2,256,256]{2,1,0:T(8,128)(2,1)S(1)}, bf16[2,256,256]{2,1,0:T(8,128)(2,1)S(1)}) custom-call(s32[1]{0:T(128)} %bitcast.refs_0_, bf16[2,512,512]{2,1,0:T(8,128)(2,1)S(1)} %shard_map.71.refs_1_.refs_4_, bf16[2,512,512]{2,1,0:T(8,128)(2,1)S(1)} %collective-permute-done.15.refs_2_, ...), custom_call_target="tpu_custom_call" | custom-call | flops 536870912 | bytes 3670016 | tf_op jit(solution)/shard_map/pallas_call | solution.py:42
  92.7 7.3 %collective-permute-start.30 = (bf16[2,256,256]{2,1,0:T(8,128)(2,1)S(1)}, bf16[2,256,256]{2,1,0:T(8,128)(2,1)S(1)}, u32[]{:S(2)}, u32[]{:S(2)}) collective-permute-start(bf16[2,256,256]{2,1,0:T(8,128)(2,1)S(1)} %get-tuple-element.45.refs_2_), channel_id=1, source_target_pairs={{0,4},{4,0},{8,12},{12,8},{16,20},{20,16},{24,28},{28,24},{1,5},{5... | collective-permute-start | bytes 786440 | tf_op jit(solution)/shard_map/ppermute | solution.py:303
  101.2 2.4 %collective-permute-start.31 = (bf16[2,256,256]{2,1,0:T(8,128)(2,1)S(1)}, bf16[2,256,256]{2,1,0:T(8,128)(2,1)S(1)}, u32[]{:S(2)}, u32[]{:S(2)}) collective-permute-start(bf16[2,256,256]{2,1,0:T(8,128)(2,1)S(1)} %get-tuple-element.46.refs_3_), channel_id=1, source_target_pairs={{0,4},{4,0},{8,12},{12,8},{16,20},{20,16},{24,28},{28,24},{1,5},{5... | collective-permute-start | bytes 786440 | tf_op jit(solution)/shard_map/ppermute | solution.py:303
  106.4 3.3 %shard_map.78 = bf16[2,512,512]{2,1,0:T(8,128)(2,1)} custom-call(s32[1]{0:T(128)} %bitcast.refs_0_, bf16[2,512,512]{2,1,0:T(8,128)(2,1)S(1)} %shard_map.71.refs_1_.refs_4_, bf16[2,256,256]{2,1,0:T(8,128)(2,1)S(1)} %get-tuple-element.45.refs_2_, bf16[2,256,256]{2,1,0:T(8,128)(2,1)S(1)} %get-tuple-element.46.refs_3_, ...), custom_call_target="tpu_custom_call" | custom-call | flops 1073741824 | bytes 6291456 | tf_op jit(solution)/shard_map/pallas_call | solution.py:42
  (81 shorter events, 28.2 us)
Async XLA Ops:
  0.0 3.2 %collective-permute-start = (bf16[2,512,512]{2,1,0:T(8,128)(2,1)}, bf16[2,512,512]{2,1,0:T(8,128)(2,1)S(1)}, u32[]{:S(2)}, u32[]{:S(2)}) collective-permute-start(bf16[2,512,512]{2,1,0:T(8,128)(2,1)} %bitcast.41), channel_id=1, source_target_pairs={{0,4},{4,0},{8,12},{12,8},{16,20},{20,16},{24,28},{28,24},{1,5},{5... | collective-permute-start | bytes 3145736 | tf_op jit(solution)/shard_map/ppermute | solution.py:303
  0.7 2.3 %collective-permute-start.1 = (s32[1,2]{1,0:T(1,128)S(1)}, s32[1,2]{1,0:T(1,128)S(1)}, u32[]{:S(2)}, u32[]{:S(2)}) collective-permute-start(s32[1,2]{1,0:T(1,128)S(1)} %copy-done.5), channel_id=1, source_target_pairs={{0,4},{4,0},{8,12},{12,8},{16,20},{20,16},{24,28},{28,24},{1,5},{5... | collective-permute-start | bytes 32 | tf_op jit(solution)/shard_map/ppermute | solution.py:303
  1.3 23.7 %collective-permute-start.3 = (bf16[2,512,512]{2,1,0:T(8,128)(2,1)}, bf16[2,512,512]{2,1,0:T(8,128)(2,1)S(1)}, u32[]{:S(2)}, u32[]{:S(2)}) collective-permute-start(bf16[2,512,512]{2,1,0:T(8,128)(2,1)} %bitcast.25), channel_id=1, source_target_pairs={{0,4},{4,0},{8,12},{12,8},{16,20},{20,16},{24,28},{28,24},{1,5},{5... | collective-permute-start | bytes 3145736 | tf_op jit(solution)/shard_map/ppermute | solution.py:303
  5.3 30.7 %collective-permute-start.2 = (bf16[2,512,512]{2,1,0:T(8,128)(2,1)S(1)}, bf16[2,512,512]{2,1,0:T(8,128)(2,1)S(1)}, u32[]{:S(2)}, u32[]{:S(2)}) collective-permute-start(bf16[2,512,512]{2,1,0:T(8,128)(2,1)S(1)} %get-tuple-element.33), channel_id=1, source_target_pairs={{2,3},{6,7},{10,11},{14,15},{18,19},{22,23},{26,27},{30,31}} | collective-permute-start | bytes 3145736 | tf_op jit(solution)/shard_map/ppermute | solution.py:404
  6.6 13.6 %collective-permute-start.5 = (bf16[528,256]{1,0:T(8,128)(2,1)S(1)}, bf16[528,256]{1,0:T(8,128)(2,1)S(1)}, u32[]{:S(2)}, u32[]{:S(2)}) collective-permute-start(bf16[528,256]{1,0:T(8,128)(2,1)S(1)} %get-tuple-element.68.refs_3_), channel_id=1, source_target_pairs={{0,16},{4,20},{8,24},{12,28},{16,0},{20,4},{24,8},{28,12},{1,17},{... | collective-permute-start | bytes 811016 | tf_op jit(solution)/shard_map/ppermute | solution.py:328
  7.9 12.3 %collective-permute-start.6 = (bf16[528,256]{1,0:T(8,128)(2,1)S(1)}, bf16[528,256]{1,0:T(8,128)(2,1)S(1)}, u32[]{:S(2)}, u32[]{:S(2)}) collective-permute-start(bf16[528,256]{1,0:T(8,128)(2,1)S(1)} %get-tuple-element.69.refs_4_), channel_id=1, source_target_pairs={{0,24},{4,28},{8,16},{12,20},{16,8},{20,12},{24,0},{28,4},{1,25},{... | collective-permute-start | bytes 811016 | tf_op jit(solution)/shard_map/ppermute | solution.py:328
  9.1 12.1 %collective-permute-start.4 = (bf16[528,256]{1,0:T(8,128)(2,1)S(1)}, bf16[528,256]{1,0:T(8,128)(2,1)S(1)}, u32[]{:S(2)}, u32[]{:S(2)}) collective-permute-start(bf16[528,256]{1,0:T(8,128)(2,1)S(1)} %get-tuple-element.70.refs_2_), channel_id=1, source_target_pairs={{0,8},{4,12},{8,0},{12,4},{16,24},{20,28},{24,16},{28,20},{1,9},{5... | collective-permute-start | bytes 811016 | tf_op jit(solution)/shard_map/ppermute | solution.py:328
  22.3 4.2 %collective-permute-start.7 = (bf16[2,128,256]{2,1,0:T(8,128)(2,1)S(1)}, bf16[2,128,256]{2,1,0:T(8,128)(2,1)S(1)}, u32[]{:S(2)}, u32[]{:S(2)}) collective-permute-start(bf16[2,128,256]{2,1,0:T(8,128)(2,1)S(1)} %get-tuple-element.35), channel_id=1, source_target_pairs={{0,8},{4,12},{8,0},{12,4},{16,24},{20,28},{24,16},{28,20},{1,9},{5... | collective-permute-start | bytes 393224 | tf_op jit(solution)/shard_map/ppermute | solution.py:328
  23.6 4.1 %collective-permute-start.8 = (bf16[2,128,256]{2,1,0:T(8,128)(2,1)S(1)}, bf16[2,128,256]{2,1,0:T(8,128)(2,1)S(1)}, u32[]{:S(2)}, u32[]{:S(2)}) collective-permute-start(bf16[2,128,256]{2,1,0:T(8,128)(2,1)S(1)} %get-tuple-element.36), channel_id=1, source_target_pairs={{0,16},{4,20},{8,24},{12,28},{16,0},{20,4},{24,8},{28,12},{1,17},{... | collective-permute-start | bytes 393224 | tf_op jit(solution)/shard_map/ppermute | solution.py:328
  24.8 5.8 %collective-permute-start.9 = (bf16[2,128,256]{2,1,0:T(8,128)(2,1)S(1)}, bf16[2,128,256]{2,1,0:T(8,128)(2,1)S(1)}, u32[]{:S(2)}, u32[]{:S(2)}) collective-permute-start(bf16[2,128,256]{2,1,0:T(8,128)(2,1)S(1)} %get-tuple-element.37), channel_id=1, source_target_pairs={{0,24},{4,28},{8,16},{12,20},{16,8},{20,12},{24,0},{28,4},{1,25},{... | collective-permute-start | bytes 393224 | tf_op jit(solution)/shard_map/ppermute | solution.py:328
  31.9 3.7 %collective-permute-start.10 = (bf16[2,256,256]{2,1,0:T(8,128)(2,1)S(1)}, bf16[2,256,256]{2,1,0:T(8,128)(2,1)S(1)}, u32[]{:S(2)}, u32[]{:S(2)}) collective-permute-start(bf16[2,256,256]{2,1,0:T(8,128)(2,1)S(1)} %get-tuple-element.41.refs_1_), channel_id=1, source_target_pairs={{0,4},{4,0},{8,12},{12,8},{16,20},{20,16},{24,28},{28,24},{1,5},{5... | collective-permute-start | bytes 786440 | tf_op jit(solution)/shard_map/ppermute | solution.py:303
  37.0 15.0 %collective-permute-start.12 = (bf16[2,512,256]{2,1,0:T(8,128)(2,1)S(1)}, bf16[2,512,256]{2,1,0:T(8,128)(2,1)S(1)}, u32[]{:S(2)}, u32[]{:S(2)}) collective-permute-start(bf16[2,512,256]{2,1,0:T(8,128)(2,1)S(1)} %shard_map.68.refs_7_.refs_8_), channel_id=1, source_target_pairs={{0,1},{2,3},{4,5},{6,7},{8,9},{10,11},{12,13},{14,15},{16,17},{18,... | collective-permute-start | bytes 1572872 | tf_op jit(solution)/shard_map/ppermute | solution.py:421
  38.3 4.8 %collective-permute-start.18 = (bf16[2,128,256]{2,1,0:T(8,128)(2,1)S(1)}, bf16[2,128,256]{2,1,0:T(8,128)(2,1)S(1)}, u32[]{:S(2)}, u32[]{:S(2)}) collective-permute-start(bf16[2,128,256]{2,1,0:T(8,128)(2,1)S(1)} %get-tuple-element.48), channel_id=1, source_target_pairs={{0,8},{4,12},{8,0},{12,4},{16,24},{20,28},{24,16},{28,20},{1,9},{5... | collective-permute-start | bytes 393224 | tf_op jit(solution)/shard_map/ppermute | solution.py:328
  38.6 4.5 %collective-permute-start.19 = (bf16[2,128,256]{2,1,0:T(8,128)(2,1)S(1)}, bf16[2,128,256]{2,1,0:T(8,128)(2,1)S(1)}, u32[]{:S(2)}, u32[]{:S(2)}) collective-permute-start(bf16[2,128,256]{2,1,0:T(8,128)(2,1)S(1)} %get-tuple-element.49), channel_id=1, source_target_pairs={{0,16},{4,20},{8,24},{12,28},{16,0},{20,4},{24,8},{28,12},{1,17},{... | collective-permute-start | bytes 393224 | tf_op jit(solution)/shard_map/ppermute | solution.py:328
  39.1 7.2 %collective-permute-start.20 = (bf16[2,128,256]{2,1,0:T(8,128)(2,1)S(1)}, bf16[2,128,256]{2,1,0:T(8,128)(2,1)S(1)}, u32[]{:S(2)}, u32[]{:S(2)}) collective-permute-start(bf16[2,128,256]{2,1,0:T(8,128)(2,1)S(1)} %get-tuple-element.50), channel_id=1, source_target_pairs={{0,24},{4,28},{8,16},{12,20},{16,8},{20,12},{24,0},{28,4},{1,25},{... | collective-permute-start | bytes 393224 | tf_op jit(solution)/shard_map/ppermute | solution.py:328
  47.6 6.5 %collective-permute-start.21 = (bf16[2,256,256]{2,1,0:T(8,128)(2,1)S(1)}, bf16[2,256,256]{2,1,0:T(8,128)(2,1)S(1)}, u32[]{:S(2)}, u32[]{:S(2)}) collective-permute-start(bf16[2,256,256]{2,1,0:T(8,128)(2,1)S(1)} %get-tuple-element.51.refs_1_), channel_id=1, source_target_pairs={{0,4},{4,0},{8,12},{12,8},{16,20},{20,16},{24,28},{28,24},{1,5},{5... | collective-permute-start | bytes 786440 | tf_op jit(solution)/shard_map/ppermute | solution.py:303
  48.9 5.2 %collective-permute-start.22 = (bf16[2,256,256]{2,1,0:T(8,128)(2,1)S(1)}, bf16[2,256,256]{2,1,0:T(8,128)(2,1)S(1)}, u32[]{:S(2)}, u32[]{:S(2)}) collective-permute-start(bf16[2,256,256]{2,1,0:T(8,128)(2,1)S(1)} %get-tuple-element.52.refs_2_), channel_id=1, source_target_pairs={{0,4},{4,0},{8,12},{12,8},{16,20},{20,16},{24,28},{28,24},{1,5},{5... | collective-permute-start | bytes 786440 | tf_op jit(solution)/shard_map/ppermute | solution.py:303
  52.7 4.2 %collective-permute-start.13 = (bf16[2,256,256]{2,1,0:T(8,128)(2,1)S(1)}, bf16[2,256,256]{2,1,0:T(8,128)(2,1)S(1)}, u32[]{:S(2)}, u32[]{:S(2)}) collective-permute-start(bf16[2,256,256]{2,1,0:T(8,128)(2,1)S(1)} %get-tuple-element.43.refs_1_), channel_id=1, source_target_pairs={{0,4},{4,0},{8,12},{12,8},{16,20},{20,16},{24,28},{28,24},{1,5},{5... | collective-permute-start | bytes 786440 | tf_op jit(solution)/shard_map/ppermute | solution.py:303
  54.0 2.9 %collective-permute-start.14 = (bf16[2,256,256]{2,1,0:T(8,128)(2,1)S(1)}, bf16[2,256,256]{2,1,0:T(8,128)(2,1)S(1)}, u32[]{:S(2)}, u32[]{:S(2)}) collective-permute-start(bf16[2,256,256]{2,1,0:T(8,128)(2,1)S(1)} %get-tuple-element.44.refs_2_), channel_id=1, source_target_pairs={{0,4},{4,0},{8,12},{12,8},{16,20},{20,16},{24,28},{28,24},{1,5},{5... | collective-permute-start | bytes 786440 | tf_op jit(solution)/shard_map/ppermute | solution.py:303
  55.6 15.3 %collective-permute-start.23 = (bf16[2,512,256]{2,1,0:T(8,128)(2,1)}, bf16[2,512,256]{2,1,0:T(8,128)(2,1)}, u32[]{:S(2)}, u32[]{:S(2)}) collective-permute-start(bf16[2,512,256]{2,1,0:T(8,128)(2,1)} %shard_map.74.refs_7_), channel_id=1, source_target_pairs={{0,1},{2,3},{4,5},{6,7},{8,9},{10,11},{12,13},{14,15},{16,17},{18,... | collective-permute-start | bytes 1572872 | tf_op jit(solution)/shard_map/ppermute | solution.py:421
  58.5 15.6 %collective-permute-start.16 = (bf16[2,512,256]{2,1,0:T(8,128)(2,1)}, bf16[2,512,256]{2,1,0:T(8,128)(2,1)}, u32[]{:S(2)}, u32[]{:S(2)}) collective-permute-start(bf16[2,512,256]{2,1,0:T(8,128)(2,1)} %shard_map.70.refs_3_.refs_5_.refs_10_), channel_id=1, source_target_pairs={{1,2},{5,6},{9,10},{13,14},{17,18},{21,22},{25,26},{29,30}} | collective-permute-start | bytes 1572872 | tf_op jit(solution)/shard_map/ppermute | solution.py:421
  62.5 28.3 %collective-permute-start.15 = (bf16[2,512,512]{2,1,0:T(8,128)(2,1)S(1)}, bf16[2,512,512]{2,1,0:T(8,128)(2,1)S(1)}, u32[]{:S(2)}, u32[]{:S(2)}) collective-permute-start(bf16[2,512,512]{2,1,0:T(8,128)(2,1)S(1)} %shard_map.71.refs_1_.refs_4_), channel_id=1, source_target_pairs={{0,4},{4,0},{8,12},{12,8},{16,20},{20,16},{24,28},{28,24},{1,5},{5... | collective-permute-start | bytes 3145736 | tf_op jit(solution)/shard_map/ppermute | solution.py:303
  72.6 2.7 %collective-permute-start.24 = (bf16[2,256,256]{2,1,0:T(8,128)(2,1)S(1)}, bf16[2,256,256]{2,1,0:T(8,128)(2,1)S(1)}, u32[]{:S(2)}, u32[]{:S(2)}) collective-permute-start(bf16[2,256,256]{2,1,0:T(8,128)(2,1)S(1)} %get-tuple-element.53.refs_1_), channel_id=1, source_target_pairs={{0,4},{4,0},{8,12},{12,8},{16,20},{20,16},{24,28},{28,24},{1,5},{5... | collective-permute-start | bytes 786440 | tf_op jit(solution)/shard_map/ppermute | solution.py:303
  74.1 14.3 %collective-permute-start.17 = (bf16[2,512,256]{2,1,0:T(8,128)(2,1)}, bf16[2,512,256]{2,1,0:T(8,128)(2,1)S(1)}, u32[]{:S(2)}, u32[]{:S(2)}) collective-permute-start(bf16[2,512,256]{2,1,0:T(8,128)(2,1)} %collective-permute-done.16.refs_3_.refs_8_), channel_id=1, source_target_pairs={{2,3},{6,7},{10,11},{14,15},{18,19},{22,23},{26,27},{30,31}} | collective-permute-start | bytes 1572872 | tf_op jit(solution)/shard_map/ppermute | solution.py:421
  78.0 2.4 %collective-permute-start.28 = (bf16[2,256,256]{2,1,0:T(8,128)(2,1)S(1)}, bf16[2,256,256]{2,1,0:T(8,128)(2,1)S(1)}, u32[]{:S(2)}, u32[]{:S(2)}) collective-permute-start(bf16[2,256,256]{2,1,0:T(8,128)(2,1)S(1)} %get-tuple-element.56.refs_12_), channel_id=1, source_target_pairs={{1,2},{5,6},{9,10},{13,14},{17,18},{21,22},{25,26},{29,30}} | collective-permute-start | bytes 786440 | tf_op jit(solution)/shard_map/ppermute | solution.py:421
  78.7 25.8 %collective-permute-start.34 = (bf16[2,512,256]{2,1,0:T(8,128)(2,1)}, bf16[2,512,256]{2,1,0:T(8,128)(2,1)S(1)}, u32[]{:S(2)}, u32[]{:S(2)}) collective-permute-start(bf16[2,512,256]{2,1,0:T(8,128)(2,1)} %shard_map.70.refs_3_.refs_5_.refs_10_), channel_id=1, source_target_pairs={{0,4},{4,0},{8,12},{12,8},{16,20},{20,16},{24,28},{28,24},{1,5},{5... | collective-permute-start | bytes 1572872 | tf_op jit(solution)/shard_map/ppermute | solution.py:303
  79.1 13.6 %collective-permute-start.27 = (bf16[2,256,256]{2,1,0:T(8,128)(2,1)S(1)}, bf16[2,256,256]{2,1,0:T(8,128)(2,1)S(1)}, u32[]{:S(2)}, u32[]{:S(2)}) collective-permute-start(bf16[2,256,256]{2,1,0:T(8,128)(2,1)S(1)} %collective-permute-done.26.refs_3_), channel_id=1, source_target_pairs={{2,3},{6,7},{10,11},{14,15},{18,19},{22,23},{26,27},{30,31}} | collective-permute-start | bytes 786440 | tf_op jit(solution)/shard_map/ppermute | solution.py:421
  80.4 20.8 %collective-permute-start.29 = (bf16[2,256,256]{2,1,0:T(8,128)(2,1)S(1)}, bf16[2,256,256]{2,1,0:T(8,128)(2,1)S(1)}, u32[]{:S(2)}, u32[]{:S(2)}) collective-permute-start(bf16[2,256,256]{2,1,0:T(8,128)(2,1)S(1)} %collective-permute-done.28.refs_5_), channel_id=1, source_target_pairs={{2,3},{6,7},{10,11},{14,15},{18,19},{22,23},{26,27},{30,31}} | collective-permute-start | bytes 786440 | tf_op jit(solution)/shard_map/ppermute | solution.py:421
  88.4 16.1 %collective-permute-start.35 = (bf16[2,256,256]{2,1,0:T(8,128)(2,1)S(1)}, bf16[2,256,256]{2,1,0:T(8,128)(2,1)S(1)}, u32[]{:S(2)}, u32[]{:S(2)}) collective-permute-start(bf16[2,256,256]{2,1,0:T(8,128)(2,1)S(1)} %get-tuple-element.55.refs_11_), channel_id=1, source_target_pairs={{0,4},{4,0},{8,12},{12,8},{16,20},{20,16},{24,28},{28,24},{1,5},{5... | collective-permute-start | bytes 786440 | tf_op jit(solution)/shard_map/ppermute | solution.py:303
  90.7 14.3 %collective-permute-start.36 = (bf16[2,256,256]{2,1,0:T(8,128)(2,1)S(1)}, bf16[2,256,256]{2,1,0:T(8,128)(2,1)S(1)}, u32[]{:S(2)}, u32[]{:S(2)}) collective-permute-start(bf16[2,256,256]{2,1,0:T(8,128)(2,1)S(1)} %get-tuple-element.56.refs_12_), channel_id=1, source_target_pairs={{0,4},{4,0},{8,12},{12,8},{16,20},{20,16},{24,28},{28,24},{1,5},{5... | collective-permute-start | bytes 786440 | tf_op jit(solution)/shard_map/ppermute | solution.py:303
  92.7 12.3 %collective-permute-start.30 = (bf16[2,256,256]{2,1,0:T(8,128)(2,1)S(1)}, bf16[2,256,256]{2,1,0:T(8,128)(2,1)S(1)}, u32[]{:S(2)}, u32[]{:S(2)}) collective-permute-start(bf16[2,256,256]{2,1,0:T(8,128)(2,1)S(1)} %get-tuple-element.45.refs_2_), channel_id=1, source_target_pairs={{0,4},{4,0},{8,12},{12,8},{16,20},{20,16},{24,28},{28,24},{1,5},{5... | collective-permute-start | bytes 786440 | tf_op jit(solution)/shard_map/ppermute | solution.py:303
  101.2 3.8 %collective-permute-start.31 = (bf16[2,256,256]{2,1,0:T(8,128)(2,1)S(1)}, bf16[2,256,256]{2,1,0:T(8,128)(2,1)S(1)}, u32[]{:S(2)}, u32[]{:S(2)}) collective-permute-start(bf16[2,256,256]{2,1,0:T(8,128)(2,1)S(1)} %get-tuple-element.46.refs_3_), channel_id=1, source_target_pairs={{0,4},{4,0},{8,12},{12,8},{16,20},{20,16},{24,28},{28,24},{1,5},{5... | collective-permute-start | bytes 786440 | tf_op jit(solution)/shard_map/ppermute | solution.py:303
  (11 other events, 14.8 us)

commit v3 on v2

--- a/solution.py
+++ b/solution.py
@@ -28,7 +28,7 @@
     return lax.dot_general(left, right, (((1,), (1,)), ((), ())), preferred_element_type=F32)
 
 
-def call(kernel, outs, scalars, arrays, flops, scratch=(), after=(), tied=()):
+def call(kernel, outs, scalars, arrays, flops, scratch=(), after=(), tied=(), to_hbm=False):
     moved = sum(a.size * a.dtype.itemsize for a in [*arrays, *outs])
     inputs = len(scalars) + len(arrays)
 
@@ -45,7 +45,7 @@
         in_specs=[SMEM] * len(scalars)
         + [VMEM] * (len(arrays) + len(tied))
         + [ANY] * len(after),
-        out_specs=[VMEM] * (len(outs) + len(tied)),
+        out_specs=[ANY if to_hbm else VMEM] * (len(outs) + len(tied)),
         scratch_shapes=list(scratch),
         compiler_params=pltpu.CompilerParams(vmem_limit_bytes=16 * 2**20),
         cost_estimate=pl.CostEstimate(flops=flops, bytes_accessed=moved, transcendentals=0),
@@ -214,12 +214,12 @@
     )
 
 
-def adjoint_into(mine, theirs, right, mine_at, theirs_at, to_at, store):
+def adjoint_into(mine, theirs, right, mine_at, theirs_at, to_at, store, span=None):
     size = right.shape[1]
     tile = min(256, mine[0].shape[1])
     a = [right[p, to_at, mine_at] for p in range(2)]
     b = [right[p, to_at, theirs_at] for p in range(2)]
-    for i in range(0, size, tile):
+    for i in range(*(span or (0, size)), tile):
         mr, mi = (rows_in(mine, part, i, tile) for part in range(2))
         tr, ti = (rows_in(theirs, part, i, tile) for part in range(2))
         real = dot_t(mr, a[0]) + dot_t(mi, a[1]) + dot_t(tr, b[0]) + dot_t(ti, b[1])
@@ -235,7 +235,7 @@
     return *found, refs
 
 
-def adjoint_half(core, number, mine, theirs, rights, summand=(), cuts=1, after=()):
+def adjoint_half(core, number, mine, theirs, rights, summand=(), cuts=1, after=(), copies=1):
     half, size = mine[0].shape[2], rights[0].shape[1]
 
     def kernel(core_ref, *refs):
@@ -247,7 +247,8 @@
             for part, value in enumerate(values):
                 if sum_refs:
                     value = value + rows_in(sum_refs, part, i, tile).astype(F32)
-                put_rows(out_refs, part, i, tile, value)
+                for n in range(copies):
+                    put_rows(out_refs[n * cuts : (n + 1) * cuts], part, i, tile, value)
 
         def work(n):
             held = number ^ n
@@ -259,8 +260,16 @@
 
     arrays = [*mine, *theirs, *rights, *summand]
     found = call(
-        kernel, [block(2, size // cuts, half)] * cuts, [core], arrays, 16 * size * half * half, (), after
-    )
+        kernel,
+        [block(2, size // cuts, half)] * (cuts * copies),
+        [core],
+        arrays,
+        16 * size * half * half,
+        (),
+        after,
+    )
+    if copies == 2:
+        return found[:cuts], found[cuts:]
     return [found] if cuts == 1 else list(found)
 
 
@@ -269,24 +278,39 @@
     lists = [*mines, *theirs, *sums, *other_sums]
 
     def kernel(core_ref, right_ref, *refs):
-        *groups, (out_ref,) = split(refs, *(len(each) for each in lists))
+        *groups, (out_ref, held, sem) = split(refs, *(len(each) for each in lists))
+        tile = min(256, mines[0][0].shape[1])
+
+        def moved(i):
+            at = slice(i, i + tile)
+            return pltpu.make_async_copy(
+                held.at[:, at, :], out_ref.at[:, at, :], sem.at[i // tile]
+            )
 
         def work(n):
             mine_refs, theirs_refs, sum_refs, other_refs = groups[n::2]
             own, other = slice(n * half, (n + 1) * half), slice((1 - n) * half, (2 - n) * half)
-            for to, summand in ((own, sum_refs), (other, other_refs)):
-
-                def store(i, tile, *values):
-                    for part, value in enumerate(values):
-                        value = value + rows_in(summand, part, i, tile).astype(F32)
-                        out_ref[part, i : i + tile, to] = value.astype(BF)
-
-                adjoint_into(mine_refs, theirs_refs, right_ref, own, other, to, store)
+            for i in range(0, size, tile):
+                for to, summand in ((own, sum_refs), (other, other_refs)):
+
+                    def store(i, tile, *values):
+                        for part, value in enumerate(values):
+                            value = value + rows_in(summand, part, i, tile).astype(F32)
+                            held[part, i : i + tile, to] = value.astype(BF)
+
+                    adjoint_into(mine_refs, theirs_refs, right_ref, own, other, to, store, (i, i + tile))
+                moved(i).start()
 
         either(core_ref, 0, work)
+        for i in range(0, size, tile):
+            moved(i).wait()
 
     out = jax.ShapeDtypeStruct((2, size, size), BF)
-    return call(kernel, [out], [core], [right, *sum(lists, [])], 8 * size**3)
+    steps = size // min(256, mines[0][0].shape[1])
+    scratch = [pltpu.VMEM(out.shape, BF), pltpu.SemaphoreType.DMA((steps,))]
+    return call(
+        kernel, [out], [core], [right, *sum(lists, [])], 8 * size**3, scratch, to_hbm=True
+    )
 
 
 def on_device(left_green, coupling, previous_lesser, screened, offsets, occupation):
@@ -448,14 +472,19 @@
     sums = [adjoint_half(core_s, 0, product, swap_all(product), lefts, (), 1, befores)]
     groups = [arrivals(1, sums[0])]
     product = times(core_s, 1, lefts, [[part] for part in late], places, sums[0])
-    sums.append(adjoint_half(core_s, 1, product, swap_all(product), lefts))
-    groups.append(arrivals(1, sums[1]))
+    source, source_sent = adjoint_half(
+        core_s, 1, product, swap_all(product), lefts, copies=2
+    )
+    sums.append(source)
+    groups.append(arrivals(1, source_sent))
 
     span = 1
     while 2 * span < slabs:
-        carried = times(core_s, 0, maps, groups[0])
-        early = adjoint_half(core_s, 0, carried, swap_all(carried), maps, sums[0], PARTS)
-        early_groups = arrivals(2 * span, early)
+        carried = times(core_s, 0, maps, groups[0], None, sums[1])
+        early, early_sent = adjoint_half(
+            core_s, 0, carried, swap_all(carried), maps, sums[0], PARTS, copies=2
+        )
+        early_groups = arrivals(2 * span, early_sent)
         wanted = lax.rem(slab // span, 2)[None]
         own = composed(wanted, own, befores, after=early)
         ahead = [group[0] for group in early_groups]

time: 110 us -> 106 us (0.964)
  Pallas kernels: 20.6 us -> 17.3 us
    pallas_call x15, Pallas kernels: 20.6 us -> 17.3 us  [call(): pl.pallas_call(body, out_shape=[*outs, *(jax.ShapeDtypeStruct(t.shape, t....]
    ppermute x19, waiting for transfers between devices: 3.59 us -> 5.2 us  [swap(): return lax.ppermute(value, 'energy', [(i, i ^ 1) for i in range(energies)])]
    ppermute x8, waiting for transfers between devices: 19 us -> 17.6 us  [arrivals(): moving = lax.ppermute(moving, 'slab', moves)]
    unnamed x12 -> x16, local copies, waits for them, and re-layouts: 2.55 us -> 2.62 us
  transfers between devices with their start and end apart: 37 -> 37, of which waited for: 19 -> 21; matrix products, arithmetic and copies ran while one was open for 3% -> 3% of each run, Pallas kernels for 15% -> 13%
where the time goes in v3:
time: 106 us
  waiting for transfers between devices  42.8 us (40%)
  starting transfers between devices  39.4 us (37%)
  Pallas kernels  17.3 us (16%)
  local copies, waits for them, and re-layouts  3.9 us (4%)
  other arithmetic  2.21 us (2%)
    ppermute x19, starting transfers between devices, swap(): return lax.ppermute(value, 'energy', [(i, i ^ 1) for i in range(energies)])  21.5 us
    ppermute x9, waiting for transfers between devices, across(): return lax.ppermute(value, 'energy', moves)  20 us
    ppermute x8, waiting for transfers between devices, arrivals(): moving = lax.ppermute(moving, 'slab', moves)  17.6 us
    pallas_call x15, Pallas kernels, call(): pl.pallas_call(body, out_shape=[*outs, *(jax.ShapeDtypeStruct(t.shape, t....  17.3 us
    ppermute x8, starting transfers between devices, arrivals(): moving = lax.ppermute(moving, 'slab', moves)  8.45 us
    ppermute x9, starting transfers between devices, across(): return lax.ppermute(value, 'energy', moves)  8.14 us
    ppermute x19, waiting for transfers between devices, swap(): return lax.ppermute(value, 'energy', [(i, i ^ 1) for i in range(energies)])  5.2 us
    unnamed x16, local copies, waits for them, and re-layouts  2.62 us
  transfers between devices with their start and end apart: 37, of which 21 were waited for; matrix products, arithmetic and copies ran while one was open for 3% of the time, Pallas kernels for 13%

profile of v3, /device:TPU:25, one launch (start us, length us, event | category | flops | bytes accessed | tf_op | source)
XLA Modules:
  0.0 106.1 jit_solution(3400322373488144276)
XLA Ops:
  5.3 1.3 %collective-permute-start.2 = (bf16[2,512,512]{2,1,0:T(8,128)(2,1)S(1)}, bf16[2,512,512]{2,1,0:T(8,128)(2,1)S(1)}, u32[]{:S(2)}, u32[]{:S(2)}) collective-permute-start(bf16[2,512,512]{2,1,0:T(8,128)(2,1)S(1)} %get-tuple-element.37), channel_id=1, source_target_pairs={{2,3},{6,7},{10,11},{14,15},{18,19},{22,23},{26,27},{30,31}} | collective-permute-start | bytes 3145736 | tf_op jit(solution)/shard_map/ppermute | solution.py:428
  6.6 1.3 %collective-permute-start.5 = (bf16[528,256]{1,0:T(8,128)(2,1)S(1)}, bf16[528,256]{1,0:T(8,128)(2,1)S(1)}, u32[]{:S(2)}, u32[]{:S(2)}) collective-permute-start(bf16[528,256]{1,0:T(8,128)(2,1)S(1)} %get-tuple-element.76.refs_3_), channel_id=1, source_target_pairs={{0,16},{4,20},{8,24},{12,28},{16,0},{20,4},{24,8},{28,12},{1,17},{... | collective-permute-start | bytes 811016 | tf_op jit(solution)/shard_map/ppermute | solution.py:352
  11.3 8.9 %collective-permute-done.5.refs_5_ = bf16[528,256]{1,0:T(8,128)(2,1)S(1)} collective-permute-done((bf16[528,256]{1,0:T(8,128)(2,1)S(1)}, bf16[528,256]{1,0:T(8,128)(2,1)S(1)}, u32[]{:S(2)}, u32[]{:S(2)}) %collective-permute-start.5) | collective-permute-done | bytes 270368 | tf_op jit(solution)/shard_map/ppermute | solution.py:352
  21.1 1.2 %shard_map.65 = (bf16[2,128,256]{2,1,0:T(8,128)(2,1)S(1)}, bf16[2,128,256]{2,1,0:T(8,128)(2,1)S(1)}, bf16[2,128,256]{2,1,0:T(8,128)(2,1)S(1)}, bf16[2,128,256]{2...) custom-call(s32[1]{0:T(128)} %bitcast.12.refs_0_, ...), custom_call_target="tpu_custom_call" | custom-call | flops 6291456 | bytes 2654208 | tf_op jit(solution)/shard_map/pallas_call | solution.py:42
  22.3 1.3 %collective-permute-start.7 = (bf16[2,128,256]{2,1,0:T(8,128)(2,1)S(1)}, bf16[2,128,256]{2,1,0:T(8,128)(2,1)S(1)}, u32[]{:S(2)}, u32[]{:S(2)}) collective-permute-start(bf16[2,128,256]{2,1,0:T(8,128)(2,1)S(1)} %get-tuple-element.39), channel_id=1, source_target_pairs={{0,8},{4,12},{8,0},{12,4},{16,24},{20,28},{24,16},{28,20},{1,9},{5... | collective-permute-start | bytes 393224 | tf_op jit(solution)/shard_map/ppermute | solution.py:352
  23.6 1.2 %collective-permute-start.8 = (bf16[2,128,256]{2,1,0:T(8,128)(2,1)S(1)}, bf16[2,128,256]{2,1,0:T(8,128)(2,1)S(1)}, u32[]{:S(2)}, u32[]{:S(2)}) collective-permute-start(bf16[2,128,256]{2,1,0:T(8,128)(2,1)S(1)} %get-tuple-element.40), channel_id=1, source_target_pairs={{0,16},{4,20},{8,24},{12,28},{16,0},{20,4},{24,8},{28,12},{1,17},{... | collective-permute-start | bytes 393224 | tf_op jit(solution)/shard_map/ppermute | solution.py:352
  27.7 2.9 %collective-permute-done.9.refs_7_ = bf16[2,128,256]{2,1,0:T(8,128)(2,1)S(1)} collective-permute-done((bf16[2,128,256]{2,1,0:T(8,128)(2,1)S(1)}, bf16[2,128,256]{2,1,0:T(8,128)(2,1)S(1)}, u32[]{:S(2)}, u32[]{:S(2)}) %collective-permute-start.9) | collective-permute-done | bytes 131104 | tf_op jit(solution)/shard_map/ppermute | solution.py:352
  30.6 1.3 %shard_map.67 = (bf16[2,256,256]{2,1,0:T(8,128)(2,1)S(1)}, bf16[2,256,256]{2,1,0:T(8,128)(2,1)S(1)}, bf16[2,128,256]{2,1,0:T(8,128)(2,1)S(1)}, bf16[2,128,256]{2,1,0:T(8,128)(2,1)S(1)}, bf16[2,128,256]{2,1,0:T(8,128)(2,1)S(1)}) custom-call(s32[1]{0:T(128)} %bitcast.refs_0_, s32[4]{0:T(128)S(1)} %iota_xor_fusion.refs_1_, bf16[2,512,512]{2,1,0:T(8,128)(2,1)S(1)} %bitcast.27, ...), custom_call_target="tpu_custom_call" | custom-call | flops 536870912 | bytes 3145728 | tf_op jit(solution)/shard_map/pallas_call | solution.py:42
  31.9 2.5 %collective-permute-start.10 = (bf16[2,256,256]{2,1,0:T(8,128)(2,1)S(1)}, bf16[2,256,256]{2,1,0:T(8,128)(2,1)S(1)}, u32[]{:S(2)}, u32[]{:S(2)}) collective-permute-start(bf16[2,256,256]{2,1,0:T(8,128)(2,1)S(1)} %get-tuple-element.45.refs_1_), channel_id=1, source_target_pairs={{0,4},{4,0},{8,12},{12,8},{16,20},{20,16},{24,28},{28,24},{1,5},{5... | collective-permute-start | bytes 786440 | tf_op jit(solution)/shard_map/ppermute | solution.py:327
  37.0 1.3 %collective-permute-start.12 = (bf16[2,512,256]{2,1,0:T(8,128)(2,1)S(1)}, bf16[2,512,256]{2,1,0:T(8,128)(2,1)S(1)}, u32[]{:S(2)}, u32[]{:S(2)}) collective-permute-start(bf16[2,512,256]{2,1,0:T(8,128)(2,1)S(1)} %shard_map.68.refs_8_.refs_7_), channel_id=1, source_target_pairs={{0,1},{2,3},{4,5},{6,7},{8,9},{10,11},{12,13},{14,15},{16,17},{18,... | collective-permute-start | bytes 1572872 | tf_op jit(solution)/shard_map/ppermute | solution.py:445
  39.1 1.8 %collective-permute-start.15 = (bf16[2,128,256]{2,1,0:T(8,128)(2,1)S(1)}, bf16[2,128,256]{2,1,0:T(8,128)(2,1)S(1)}, u32[]{:S(2)}, u32[]{:S(2)}) collective-permute-start(bf16[2,128,256]{2,1,0:T(8,128)(2,1)S(1)} %get-tuple-element.50), channel_id=1, source_target_pairs={{0,24},{4,28},{8,16},{12,20},{16,8},{20,12},{24,0},{28,4},{1,25},{... | collective-permute-start | bytes 393224 | tf_op jit(solution)/shard_map/ppermute | solution.py:352
  41.0 2.1 %collective-permute-done.13.refs_5_ = bf16[2,128,256]{2,1,0:T(8,128)(2,1)S(1)} collective-permute-done((bf16[2,128,256]{2,1,0:T(8,128)(2,1)S(1)}, bf16[2,128,256]{2,1,0:T(8,128)(2,1)S(1)}, u32[]{:S(2)}, u32[]{:S(2)}) %collective-permute-start.13) | collective-permute-done | bytes 131104 | tf_op jit(solution)/shard_map/ppermute | solution.py:352
  43.0 3.3 %collective-permute-done.15.refs_7_ = bf16[2,128,256]{2,1,0:T(8,128)(2,1)S(1)} collective-permute-done((bf16[2,128,256]{2,1,0:T(8,128)(2,1)S(1)}, bf16[2,128,256]{2,1,0:T(8,128)(2,1)S(1)}, u32[]{:S(2)}, u32[]{:S(2)}) %collective-permute-start.15) | collective-permute-done | bytes 131104 | tf_op jit(solution)/shard_map/ppermute | solution.py:352
  46.3 1.3 %shard_map.69 = (bf16[2,256,256]{2,1,0:T(8,128)(2,1)S(1)}, bf16[2,256,256]{2,1,0:T(8,128)(2,1)S(1)}) custom-call(s32[1]{0:T(128)} %bitcast.refs_0_, s32[4]{0:T(128)S(1)} %iota_xor_fusion.refs_1_, bf16[2,512,512]{2,1,0:T(8,128)(2,1)S(1)} %bitcast.29, bf16[2,512,512]{2,1,0:T(8,128)(2,1)S(1)} %collective-permute-done.3.refs_0_.refs_3_.refs_6_, ...), custom_call_target="tpu_custom_call" | custom-call | flops 536870912 | bytes 3145728 | tf_op jit(solution)/shard_map/pallas_call | solution.py:42
  47.6 1.3 %collective-permute-start.16 = (bf16[2,256,256]{2,1,0:T(8,128)(2,1)S(1)}, bf16[2,256,256]{2,1,0:T(8,128)(2,1)S(1)}, u32[]{:S(2)}, u32[]{:S(2)}) collective-permute-start(bf16[2,256,256]{2,1,0:T(8,128)(2,1)S(1)} %get-tuple-element.51.refs_1_), channel_id=1, source_target_pairs={{0,4},{4,0},{8,12},{12,8},{16,20},{20,16},{24,28},{28,24},{1,5},{5... | collective-permute-start | bytes 786440 | tf_op jit(solution)/shard_map/ppermute | solution.py:327
  50.4 1.6 %shard_map.70 = (bf16[2,512,256]{2,1,0:T(8,128)(2,1)S(1)}, bf16[2,512,256]{2,1,0:T(8,128)(2,1)}) custom-call(s32[1]{0:T(128)} %bitcast.refs_0_, bf16[2,256,256]{2,1,0:T(8,128)(2,1)S(1)} %get-tuple-element.51.refs_1_, bf16[2,256,256]{2,1,0:T(8,128)(2,1)S(1)} %get-tuple-element.52.refs_2_, bf16[2,256,256]{2,1,0:T(8,128)(2,1)S(1)} %collective-permute-done.16.refs_3_, ...), custom_call_target="tpu_custom_call" | custom-call | flops 536870912 | bytes 4194304 | tf_op jit(solution)/shard_map/pallas_call | solution.py:42
  52.8 1.2 %collective-permute-start.18 = (bf16[2,256,256]{2,1,0:T(8,128)(2,1)S(1)}, bf16[2,256,256]{2,1,0:T(8,128)(2,1)S(1)}, u32[]{:S(2)}, u32[]{:S(2)}) collective-permute-start(bf16[2,256,256]{2,1,0:T(8,128)(2,1)S(1)} %get-tuple-element.54.refs_1_), channel_id=1, source_target_pairs={{0,4},{4,0},{8,12},{12,8},{16,20},{20,16},{24,28},{28,24},{1,5},{5... | collective-permute-start | bytes 786440 | tf_op jit(solution)/shard_map/ppermute | solution.py:327
  54.1 1.3 %collective-permute-start.23 = (bf16[2,512,256]{2,1,0:T(8,128)(2,1)}, bf16[2,512,256]{2,1,0:T(8,128)(2,1)}, u32[]{:S(2)}, u32[]{:S(2)}) collective-permute-start(bf16[2,512,256]{2,1,0:T(8,128)(2,1)} %get-tuple-element.60), channel_id=1, source_target_pairs={{0,1},{2,3},{4,5},{6,7},{8,9},{10,11},{12,13},{14,15},{16,17},{18,... | collective-permute-start | bytes 1572872 | tf_op jit(solution)/shard_map/ppermute | solution.py:445
  55.5 1.5 %shard_map.72 = (bf16[2,512,256]{2,1,0:T(8,128)(2,1)S(1)}, bf16[2,512,256]{2,1,0:T(8,128)(2,1)}) custom-call(s32[1]{0:T(128)} %bitcast.refs_0_, bf16[2,256,256]{2,1,0:T(8,128)(2,1)S(1)} %get-tuple-element.54.refs_1_, bf16[2,256,256]{2,1,0:T(8,128)(2,1)S(1)} %get-tuple-element.55.refs_2_, bf16[2,256,256]{2,1,0:T(8,128)(2,1)S(1)} %collective-permute-done.18.refs_3_, ...), custom_call_target="tpu_custom_call" | custom-call | flops 536870912 | bytes 4718592 | tf_op jit(solution)/shard_map/pallas_call | solution.py:42
  57.8 1.2 %copy-done.5 = bf16[2,512,512]{2,1,0:T(8,128)(2,1)S(1)} copy-done((bf16[2,512,512]{2,1,0:T(8,128)(2,1)S(1)}, bf16[2,512,512]{2,1,0:T(8,128)(2,1)}, u32[]{:S(2)}) %copy-start.5) | copy-done | bytes 1048600
  59.0 1.3 %shard_map.73.refs_1_.refs_4_ = bf16[2,512,512]{2,1,0:T(8,128)(2,1)S(1)} custom-call(s32[1]{0:T(128)} %bitcast.1.refs_0_, bf16[2,512,512]{2,1,0:T(8,128)(2,1)S(1)} %get-tuple-element.36.refs_1_.refs_5_, bf16[2,512,512]{2,1,0:T(8,128)(2,1)S(1)} %copy-done.5, bf16[2,512,256]{2,1,0:T(8,128)(2,1)S(1)} %get-tuple-element.56.refs_3_.refs_5_.refs_10_), custom_call_target="tpu_custom_call" | custom-call | flops 1073741824 | bytes 3145728 | tf_op jit(solution)/shard_map/pallas_call | solution.py:42
  60.7 8.6 %collective-permute-done.23.refs_3_ = bf16[2,512,256]{2,1,0:T(8,128)(2,1)} collective-permute-done((bf16[2,512,256]{2,1,0:T(8,128)(2,1)}, bf16[2,512,256]{2,1,0:T(8,128)(2,1)}, u32[]{:S(2)}, u32[]{:S(2)}) %collective-permute-start.23) | collective-permute-done | bytes 524320 | tf_op jit(solution)/shard_map/ppermute | solution.py:445
  69.3 1.8 %shard_map.75 = (bf16[2,256,256]{2,1,0:T(8,128)(2,1)S(1)}, bf16[2,256,256]{2,1,0:T(8,128)(2,1)S(1)}) custom-call(s32[1]{0:T(128)} %bitcast.refs_0_, bf16[2,512,512]{2,1,0:T(8,128)(2,1)S(1)} %get-tuple-element.36.refs_1_.refs_5_, bf16[2,512,512]{2,1,0:T(8,128)(2,1)S(1)} %shard_map.66.refs_11_.refs_2_.refs_6_, ...), custom_call_target="tpu_custom_call" | custom-call | flops 536870912 | bytes 3145728 | tf_op jit(solution)/shard_map/pallas_call | solution.py:42
  71.1 1.3 %collective-permute-start.24 = (bf16[2,256,256]{2,1,0:T(8,128)(2,1)S(1)}, bf16[2,256,256]{2,1,0:T(8,128)(2,1)S(1)}, u32[]{:S(2)}, u32[]{:S(2)}) collective-permute-start(bf16[2,256,256]{2,1,0:T(8,128)(2,1)S(1)} %get-tuple-element.61.refs_1_), channel_id=1, source_target_pairs={{0,4},{4,0},{8,12},{12,8},{16,20},{20,16},{24,28},{28,24},{1,5},{5... | collective-permute-start | bytes 786440 | tf_op jit(solution)/shard_map/ppermute | solution.py:327
  72.5 1.3 %collective-permute-start.22 = (bf16[2,512,256]{2,1,0:T(8,128)(2,1)S(1)}, bf16[2,512,256]{2,1,0:T(8,128)(2,1)S(1)}, u32[]{:S(2)}, u32[]{:S(2)}) collective-permute-start(bf16[2,512,256]{2,1,0:T(8,128)(2,1)S(1)} %collective-permute-done.21.refs_3_.refs_8_), channel_id=1, source_target_pairs={{2,3},{6,7},{10,11},{14,15},{18,19},{22,23},{26,27},{30,31}} | collective-permute-start | bytes 1572872 | tf_op jit(solution)/shard_map/ppermute | solution.py:445
  76.5 1.3 %collective-permute-start.27 = (bf16[2,256,256]{2,1,0:T(8,128)(2,1)S(1)}, bf16[2,256,256]{2,1,0:T(8,128)(2,1)S(1)}, u32[]{:S(2)}, u32[]{:S(2)}) collective-permute-start(bf16[2,256,256]{2,1,0:T(8,128)(2,1)S(1)} %collective-permute-done.26.refs_3_), channel_id=1, source_target_pairs={{2,3},{6,7},{10,11},{14,15},{18,19},{22,23},{26,27},{30,31}} | collective-permute-start | bytes 786440 | tf_op jit(solution)/shard_map/ppermute | solution.py:445
  77.8 1.3 %collective-permute-start.29 = (bf16[2,256,256]{2,1,0:T(8,128)(2,1)S(1)}, bf16[2,256,256]{2,1,0:T(8,128)(2,1)S(1)}, u32[]{:S(2)}, u32[]{:S(2)}) collective-permute-start(bf16[2,256,256]{2,1,0:T(8,128)(2,1)S(1)} %collective-permute-done.28.refs_5_), channel_id=1, source_target_pairs={{2,3},{6,7},{10,11},{14,15},{18,19},{22,23},{26,27},{30,31}} | collective-permute-start | bytes 786440 | tf_op jit(solution)/shard_map/ppermute | solution.py:445
  79.1 7.4 %collective-permute-done.22.refs_4_ = bf16[2,512,256]{2,1,0:T(8,128)(2,1)S(1)} collective-permute-done((bf16[2,512,256]{2,1,0:T(8,128)(2,1)S(1)}, bf16[2,512,256]{2,1,0:T(8,128)(2,1)S(1)}, u32[]{:S(2)}, u32[]{:S(2)}) %collective-permute-start.22) | collective-permute-done | bytes 524320 | tf_op jit(solution)/shard_map/ppermute | solution.py:445
  86.5 3.2 %collective-permute-start.35 = (bf16[2,256,256]{2,1,0:T(8,128)(2,1)S(1)}, bf16[2,256,256]{2,1,0:T(8,128)(2,1)S(1)}, u32[]{:S(2)}, u32[]{:S(2)}) collective-permute-start(bf16[2,256,256]{2,1,0:T(8,128)(2,1)S(1)} %get-tuple-element.63.refs_11_), channel_id=1, source_target_pairs={{0,4},{4,0},{8,12},{12,8},{16,20},{20,16},{24,28},{28,24},{1,5},{5... | collective-permute-start | bytes 786440 | tf_op jit(solution)/shard_map/ppermute | solution.py:327
  90.9 6.5 %collective-permute-start.30 = (bf16[2,256,256]{2,1,0:T(8,128)(2,1)S(1)}, bf16[2,256,256]{2,1,0:T(8,128)(2,1)S(1)}, u32[]{:S(2)}, u32[]{:S(2)}) collective-permute-start(bf16[2,256,256]{2,1,0:T(8,128)(2,1)S(1)} %get-tuple-element.58.refs_2_), channel_id=1, source_target_pairs={{0,4},{4,0},{8,12},{12,8},{16,20},{20,16},{24,28},{28,24},{1,5},{5... | collective-permute-start | bytes 786440 | tf_op jit(solution)/shard_map/ppermute | solution.py:327
  98.6 2.4 %collective-permute-start.31 = (bf16[2,256,256]{2,1,0:T(8,128)(2,1)S(1)}, bf16[2,256,256]{2,1,0:T(8,128)(2,1)S(1)}, u32[]{:S(2)}, u32[]{:S(2)}) collective-permute-start(bf16[2,256,256]{2,1,0:T(8,128)(2,1)S(1)} %get-tuple-element.59.refs_3_), channel_id=1, source_target_pairs={{0,4},{4,0},{8,12},{12,8},{16,20},{20,16},{24,28},{28,24},{1,5},{5... | collective-permute-start | bytes 786440 | tf_op jit(solution)/shard_map/ppermute | solution.py:327
  103.8 2.1 %shard_map.78 = bf16[2,512,512]{2,1,0:T(8,128)(2,1)} custom-call(s32[1]{0:T(128)} %bitcast.refs_0_, bf16[2,512,512]{2,1,0:T(8,128)(2,1)S(1)} %shard_map.73.refs_1_.refs_4_, bf16[2,256,256]{2,1,0:T(8,128)(2,1)S(1)} %get-tuple-element.58.refs_2_, bf16[2,256,256]{2,1,0:T(8,128)(2,1)S(1)} %get-tuple-element.59.refs_3_, ...), custom_call_target="tpu_custom_call" | custom-call | flops 1073741824 | bytes 6291456 | tf_op jit(solution)/shard_map/pallas_call | solution.py:42
  (85 shorter events, 27.4 us)
Async XLA Ops:
  0.0 3.2 %collective-permute-start = (bf16[2,512,512]{2,1,0:T(8,128)(2,1)}, bf16[2,512,512]{2,1,0:T(8,128)(2,1)S(1)}, u32[]{:S(2)}, u32[]{:S(2)}) collective-permute-start(bf16[2,512,512]{2,1,0:T(8,128)(2,1)} %bitcast.41), channel_id=1, source_target_pairs={{0,4},{4,0},{8,12},{12,8},{16,20},{20,16},{24,28},{28,24},{1,5},{5... | collective-permute-start | bytes 3145736 | tf_op jit(solution)/shard_map/ppermute | solution.py:327
  0.7 2.3 %collective-permute-start.1 = (s32[1,2]{1,0:T(1,128)S(1)}, s32[1,2]{1,0:T(1,128)S(1)}, u32[]{:S(2)}, u32[]{:S(2)}) collective-permute-start(s32[1,2]{1,0:T(1,128)S(1)} %copy-done.7), channel_id=1, source_target_pairs={{0,4},{4,0},{8,12},{12,8},{16,20},{20,16},{24,28},{28,24},{1,5},{5... | collective-permute-start | bytes 32 | tf_op jit(solution)/shard_map/ppermute | solution.py:327
  1.3 23.7 %collective-permute-start.3 = (bf16[2,512,512]{2,1,0:T(8,128)(2,1)}, bf16[2,512,512]{2,1,0:T(8,128)(2,1)S(1)}, u32[]{:S(2)}, u32[]{:S(2)}) collective-permute-start(bf16[2,512,512]{2,1,0:T(8,128)(2,1)} %bitcast.25), channel_id=1, source_target_pairs={{0,4},{4,0},{8,12},{12,8},{16,20},{20,16},{24,28},{28,24},{1,5},{5... | collective-permute-start | bytes 3145736 | tf_op jit(solution)/shard_map/ppermute | solution.py:327
  5.3 30.7 %collective-permute-start.2 = (bf16[2,512,512]{2,1,0:T(8,128)(2,1)S(1)}, bf16[2,512,512]{2,1,0:T(8,128)(2,1)S(1)}, u32[]{:S(2)}, u32[]{:S(2)}) collective-permute-start(bf16[2,512,512]{2,1,0:T(8,128)(2,1)S(1)} %get-tuple-element.37), channel_id=1, source_target_pairs={{2,3},{6,7},{10,11},{14,15},{18,19},{22,23},{26,27},{30,31}} | collective-permute-start | bytes 3145736 | tf_op jit(solution)/shard_map/ppermute | solution.py:428
  6.6 13.6 %collective-permute-start.5 = (bf16[528,256]{1,0:T(8,128)(2,1)S(1)}, bf16[528,256]{1,0:T(8,128)(2,1)S(1)}, u32[]{:S(2)}, u32[]{:S(2)}) collective-permute-start(bf16[528,256]{1,0:T(8,128)(2,1)S(1)} %get-tuple-element.76.refs_3_), channel_id=1, source_target_pairs={{0,16},{4,20},{8,24},{12,28},{16,0},{20,4},{24,8},{28,12},{1,17},{... | collective-permute-start | bytes 811016 | tf_op jit(solution)/shard_map/ppermute | solution.py:352
  7.9 12.3 %collective-permute-start.6 = (bf16[528,256]{1,0:T(8,128)(2,1)S(1)}, bf16[528,256]{1,0:T(8,128)(2,1)S(1)}, u32[]{:S(2)}, u32[]{:S(2)}) collective-permute-start(bf16[528,256]{1,0:T(8,128)(2,1)S(1)} %get-tuple-element.77.refs_4_), channel_id=1, source_target_pairs={{0,24},{4,28},{8,16},{12,20},{16,8},{20,12},{24,0},{28,4},{1,25},{... | collective-permute-start | bytes 811016 | tf_op jit(solution)/shard_map/ppermute | solution.py:352
  9.1 12.1 %collective-permute-start.4 = (bf16[528,256]{1,0:T(8,128)(2,1)S(1)}, bf16[528,256]{1,0:T(8,128)(2,1)S(1)}, u32[]{:S(2)}, u32[]{:S(2)}) collective-permute-start(bf16[528,256]{1,0:T(8,128)(2,1)S(1)} %get-tuple-element.78.refs_2_), channel_id=1, source_target_pairs={{0,8},{4,12},{8,0},{12,4},{16,24},{20,28},{24,16},{28,20},{1,9},{5... | collective-permute-start | bytes 811016 | tf_op jit(solution)/shard_map/ppermute | solution.py:352
  22.3 4.2 %collective-permute-start.7 = (bf16[2,128,256]{2,1,0:T(8,128)(2,1)S(1)}, bf16[2,128,256]{2,1,0:T(8,128)(2,1)S(1)}, u32[]{:S(2)}, u32[]{:S(2)}) collective-permute-start(bf16[2,128,256]{2,1,0:T(8,128)(2,1)S(1)} %get-tuple-element.39), channel_id=1, source_target_pairs={{0,8},{4,12},{8,0},{12,4},{16,24},{20,28},{24,16},{28,20},{1,9},{5... | collective-permute-start | bytes 393224 | tf_op jit(solution)/shard_map/ppermute | solution.py:352
  23.6 4.1 %collective-permute-start.8 = (bf16[2,128,256]{2,1,0:T(8,128)(2,1)S(1)}, bf16[2,128,256]{2,1,0:T(8,128)(2,1)S(1)}, u32[]{:S(2)}, u32[]{:S(2)}) collective-permute-start(bf16[2,128,256]{2,1,0:T(8,128)(2,1)S(1)} %get-tuple-element.40), channel_id=1, source_target_pairs={{0,16},{4,20},{8,24},{12,28},{16,0},{20,4},{24,8},{28,12},{1,17},{... | collective-permute-start | bytes 393224 | tf_op jit(solution)/shard_map/ppermute | solution.py:352
  24.8 5.8 %collective-permute-start.9 = (bf16[2,128,256]{2,1,0:T(8,128)(2,1)S(1)}, bf16[2,128,256]{2,1,0:T(8,128)(2,1)S(1)}, u32[]{:S(2)}, u32[]{:S(2)}) collective-permute-start(bf16[2,128,256]{2,1,0:T(8,128)(2,1)S(1)} %get-tuple-element.41), channel_id=1, source_target_pairs={{0,24},{4,28},{8,16},{12,20},{16,8},{20,12},{24,0},{28,4},{1,25},{... | collective-permute-start | bytes 393224 | tf_op jit(solution)/shard_map/ppermute | solution.py:352
  31.9 3.7 %collective-permute-start.10 = (bf16[2,256,256]{2,1,0:T(8,128)(2,1)S(1)}, bf16[2,256,256]{2,1,0:T(8,128)(2,1)S(1)}, u32[]{:S(2)}, u32[]{:S(2)}) collective-permute-start(bf16[2,256,256]{2,1,0:T(8,128)(2,1)S(1)} %get-tuple-element.45.refs_1_), channel_id=1, source_target_pairs={{0,4},{4,0},{8,12},{12,8},{16,20},{20,16},{24,28},{28,24},{1,5},{5... | collective-permute-start | bytes 786440 | tf_op jit(solution)/shard_map/ppermute | solution.py:327
  37.0 15.0 %collective-permute-start.12 = (bf16[2,512,256]{2,1,0:T(8,128)(2,1)S(1)}, bf16[2,512,256]{2,1,0:T(8,128)(2,1)S(1)}, u32[]{:S(2)}, u32[]{:S(2)}) collective-permute-start(bf16[2,512,256]{2,1,0:T(8,128)(2,1)S(1)} %shard_map.68.refs_8_.refs_7_), channel_id=1, source_target_pairs={{0,1},{2,3},{4,5},{6,7},{8,9},{10,11},{12,13},{14,15},{16,17},{18,... | collective-permute-start | bytes 1572872 | tf_op jit(solution)/shard_map/ppermute | solution.py:445
  38.3 4.8 %collective-permute-start.13 = (bf16[2,128,256]{2,1,0:T(8,128)(2,1)S(1)}, bf16[2,128,256]{2,1,0:T(8,128)(2,1)S(1)}, u32[]{:S(2)}, u32[]{:S(2)}) collective-permute-start(bf16[2,128,256]{2,1,0:T(8,128)(2,1)S(1)} %get-tuple-element.48), channel_id=1, source_target_pairs={{0,8},{4,12},{8,0},{12,4},{16,24},{20,28},{24,16},{28,20},{1,9},{5... | collective-permute-start | bytes 393224 | tf_op jit(solution)/shard_map/ppermute | solution.py:352
  38.6 4.5 %collective-permute-start.14 = (bf16[2,128,256]{2,1,0:T(8,128)(2,1)S(1)}, bf16[2,128,256]{2,1,0:T(8,128)(2,1)S(1)}, u32[]{:S(2)}, u32[]{:S(2)}) collective-permute-start(bf16[2,128,256]{2,1,0:T(8,128)(2,1)S(1)} %get-tuple-element.49), channel_id=1, source_target_pairs={{0,16},{4,20},{8,24},{12,28},{16,0},{20,4},{24,8},{28,12},{1,17},{... | collective-permute-start | bytes 393224 | tf_op jit(solution)/shard_map/ppermute | solution.py:352
  39.1 7.2 %collective-permute-start.15 = (bf16[2,128,256]{2,1,0:T(8,128)(2,1)S(1)}, bf16[2,128,256]{2,1,0:T(8,128)(2,1)S(1)}, u32[]{:S(2)}, u32[]{:S(2)}) collective-permute-start(bf16[2,128,256]{2,1,0:T(8,128)(2,1)S(1)} %get-tuple-element.50), channel_id=1, source_target_pairs={{0,24},{4,28},{8,16},{12,20},{16,8},{20,12},{24,0},{28,4},{1,25},{... | collective-permute-start | bytes 393224 | tf_op jit(solution)/shard_map/ppermute | solution.py:352
  47.6 2.4 %collective-permute-start.16 = (bf16[2,256,256]{2,1,0:T(8,128)(2,1)S(1)}, bf16[2,256,256]{2,1,0:T(8,128)(2,1)S(1)}, u32[]{:S(2)}, u32[]{:S(2)}) collective-permute-start(bf16[2,256,256]{2,1,0:T(8,128)(2,1)S(1)} %get-tuple-element.51.refs_1_), channel_id=1, source_target_pairs={{0,4},{4,0},{8,12},{12,8},{16,20},{20,16},{24,28},{28,24},{1,5},{5... | collective-permute-start | bytes 786440 | tf_op jit(solution)/shard_map/ppermute | solution.py:327
  52.8 2.6 %collective-permute-start.18 = (bf16[2,256,256]{2,1,0:T(8,128)(2,1)S(1)}, bf16[2,256,256]{2,1,0:T(8,128)(2,1)S(1)}, u32[]{:S(2)}, u32[]{:S(2)}) collective-permute-start(bf16[2,256,256]{2,1,0:T(8,128)(2,1)S(1)} %get-tuple-element.54.refs_1_), channel_id=1, source_target_pairs={{0,4},{4,0},{8,12},{12,8},{16,20},{20,16},{24,28},{28,24},{1,5},{5... | collective-permute-start | bytes 786440 | tf_op jit(solution)/shard_map/ppermute | solution.py:327
  54.1 15.3 %collective-permute-start.23 = (bf16[2,512,256]{2,1,0:T(8,128)(2,1)}, bf16[2,512,256]{2,1,0:T(8,128)(2,1)}, u32[]{:S(2)}, u32[]{:S(2)}) collective-permute-start(bf16[2,512,256]{2,1,0:T(8,128)(2,1)} %get-tuple-element.60), channel_id=1, source_target_pairs={{0,1},{2,3},{4,5},{6,7},{8,9},{10,11},{12,13},{14,15},{16,17},{18,... | collective-permute-start | bytes 1572872 | tf_op jit(solution)/shard_map/ppermute | solution.py:445
  57.1 15.4 %collective-permute-start.21 = (bf16[2,512,256]{2,1,0:T(8,128)(2,1)}, bf16[2,512,256]{2,1,0:T(8,128)(2,1)S(1)}, u32[]{:S(2)}, u32[]{:S(2)}) collective-permute-start(bf16[2,512,256]{2,1,0:T(8,128)(2,1)} %get-tuple-element.57), channel_id=1, source_target_pairs={{1,2},{5,6},{9,10},{13,14},{17,18},{21,22},{25,26},{29,30}} | collective-permute-start | bytes 1572872 | tf_op jit(solution)/shard_map/ppermute | solution.py:445
  60.3 29.4 %collective-permute-start.20 = (bf16[2,512,512]{2,1,0:T(8,128)(2,1)S(1)}, bf16[2,512,512]{2,1,0:T(8,128)(2,1)S(1)}, u32[]{:S(2)}, u32[]{:S(2)}) collective-permute-start(bf16[2,512,512]{2,1,0:T(8,128)(2,1)S(1)} %shard_map.73.refs_1_.refs_4_), channel_id=1, source_target_pairs={{0,4},{4,0},{8,12},{12,8},{16,20},{20,16},{24,28},{28,24},{1,5},{5... | collective-permute-start | bytes 3145736 | tf_op jit(solution)/shard_map/ppermute | solution.py:327
  71.1 2.7 %collective-permute-start.24 = (bf16[2,256,256]{2,1,0:T(8,128)(2,1)S(1)}, bf16[2,256,256]{2,1,0:T(8,128)(2,1)S(1)}, u32[]{:S(2)}, u32[]{:S(2)}) collective-permute-start(bf16[2,256,256]{2,1,0:T(8,128)(2,1)S(1)} %get-tuple-element.61.refs_1_), channel_id=1, source_target_pairs={{0,4},{4,0},{8,12},{12,8},{16,20},{20,16},{24,28},{28,24},{1,5},{5... | collective-permute-start | bytes 786440 | tf_op jit(solution)/shard_map/ppermute | solution.py:327
  72.5 14.0 %collective-permute-start.22 = (bf16[2,512,256]{2,1,0:T(8,128)(2,1)S(1)}, bf16[2,512,256]{2,1,0:T(8,128)(2,1)S(1)}, u32[]{:S(2)}, u32[]{:S(2)}) collective-permute-start(bf16[2,512,256]{2,1,0:T(8,128)(2,1)S(1)} %collective-permute-done.21.refs_3_.refs_8_), channel_id=1, source_target_pairs={{2,3},{6,7},{10,11},{14,15},{18,19},{22,23},{26,27},{30,31}} | collective-permute-start | bytes 1572872 | tf_op jit(solution)/shard_map/ppermute | solution.py:445
  74.7 1.8 %collective-permute-start.26 = (bf16[2,256,256]{2,1,0:T(8,128)(2,1)S(1)}, bf16[2,256,256]{2,1,0:T(8,128)(2,1)S(1)}, u32[]{:S(2)}, u32[]{:S(2)}) collective-permute-start(bf16[2,256,256]{2,1,0:T(8,128)(2,1)S(1)} %get-tuple-element.63.refs_11_), channel_id=1, source_target_pairs={{1,2},{5,6},{9,10},{13,14},{17,18},{21,22},{25,26},{29,30}} | collective-permute-start | bytes 786440 | tf_op jit(solution)/shard_map/ppermute | solution.py:445
  75.4 2.4 %collective-permute-start.28 = (bf16[2,256,256]{2,1,0:T(8,128)(2,1)S(1)}, bf16[2,256,256]{2,1,0:T(8,128)(2,1)S(1)}, u32[]{:S(2)}, u32[]{:S(2)}) collective-permute-start(bf16[2,256,256]{2,1,0:T(8,128)(2,1)S(1)} %get-tuple-element.64.refs_12_), channel_id=1, source_target_pairs={{1,2},{5,6},{9,10},{13,14},{17,18},{21,22},{25,26},{29,30}} | collective-permute-start | bytes 786440 | tf_op jit(solution)/shard_map/ppermute | solution.py:445
  76.1 25.7 %collective-permute-start.34 = (bf16[2,512,256]{2,1,0:T(8,128)(2,1)S(1)}, bf16[2,512,256]{2,1,0:T(8,128)(2,1)S(1)}, u32[]{:S(2)}, u32[]{:S(2)}) collective-permute-start(bf16[2,512,256]{2,1,0:T(8,128)(2,1)S(1)} %get-tuple-element.56.refs_3_.refs_5_.refs_10_), channel_id=1, source_target_pairs={{0,4},{4,0},{8,12},{12,8},{16,20},{20,16},{24,28},{28,24},{1,5},{5... | collective-permute-start | bytes 1572872 | tf_op jit(solution)/shard_map/ppermute | solution.py:327
  76.5 14.4 %collective-permute-start.27 = (bf16[2,256,256]{2,1,0:T(8,128)(2,1)S(1)}, bf16[2,256,256]{2,1,0:T(8,128)(2,1)S(1)}, u32[]{:S(2)}, u32[]{:S(2)}) collective-permute-start(bf16[2,256,256]{2,1,0:T(8,128)(2,1)S(1)} %collective-permute-done.26.refs_3_), channel_id=1, source_target_pairs={{2,3},{6,7},{10,11},{14,15},{18,19},{22,23},{26,27},{30,31}} | collective-permute-start | bytes 786440 | tf_op jit(solution)/shard_map/ppermute | solution.py:445
  77.8 20.7 %collective-permute-start.29 = (bf16[2,256,256]{2,1,0:T(8,128)(2,1)S(1)}, bf16[2,256,256]{2,1,0:T(8,128)(2,1)S(1)}, u32[]{:S(2)}, u32[]{:S(2)}) collective-permute-start(bf16[2,256,256]{2,1,0:T(8,128)(2,1)S(1)} %collective-permute-done.28.refs_5_), channel_id=1, source_target_pairs={{2,3},{6,7},{10,11},{14,15},{18,19},{22,23},{26,27},{30,31}} | collective-permute-start | bytes 786440 | tf_op jit(solution)/shard_map/ppermute | solution.py:445
  86.5 15.3 %collective-permute-start.35 = (bf16[2,256,256]{2,1,0:T(8,128)(2,1)S(1)}, bf16[2,256,256]{2,1,0:T(8,128)(2,1)S(1)}, u32[]{:S(2)}, u32[]{:S(2)}) collective-permute-start(bf16[2,256,256]{2,1,0:T(8,128)(2,1)S(1)} %get-tuple-element.63.refs_11_), channel_id=1, source_target_pairs={{0,4},{4,0},{8,12},{12,8},{16,20},{20,16},{24,28},{28,24},{1,5},{5... | collective-permute-start | bytes 786440 | tf_op jit(solution)/shard_map/ppermute | solution.py:327
  89.7 12.7 %collective-permute-start.36 = (bf16[2,256,256]{2,1,0:T(8,128)(2,1)S(1)}, bf16[2,256,256]{2,1,0:T(8,128)(2,1)S(1)}, u32[]{:S(2)}, u32[]{:S(2)}) collective-permute-start(bf16[2,256,256]{2,1,0:T(8,128)(2,1)S(1)} %get-tuple-element.64.refs_12_), channel_id=1, source_target_pairs={{0,4},{4,0},{8,12},{12,8},{16,20},{20,16},{24,28},{28,24},{1,5},{5... | collective-permute-start | bytes 786440 | tf_op jit(solution)/shard_map/ppermute | solution.py:327
  90.9 11.5 %collective-permute-start.30 = (bf16[2,256,256]{2,1,0:T(8,128)(2,1)S(1)}, bf16[2,256,256]{2,1,0:T(8,128)(2,1)S(1)}, u32[]{:S(2)}, u32[]{:S(2)}) collective-permute-start(bf16[2,256,256]{2,1,0:T(8,128)(2,1)S(1)} %get-tuple-element.58.refs_2_), channel_id=1, source_target_pairs={{0,4},{4,0},{8,12},{12,8},{16,20},{20,16},{24,28},{28,24},{1,5},{5... | collective-permute-start | bytes 786440 | tf_op jit(solution)/shard_map/ppermute | solution.py:327
  98.6 3.8 %collective-permute-start.31 = (bf16[2,256,256]{2,1,0:T(8,128)(2,1)S(1)}, bf16[2,256,256]{2,1,0:T(8,128)(2,1)S(1)}, u32[]{:S(2)}, u32[]{:S(2)}) collective-permute-start(bf16[2,256,256]{2,1,0:T(8,128)(2,1)S(1)} %get-tuple-element.59.refs_3_), channel_id=1, source_target_pairs={{0,4},{4,0},{8,12},{12,8},{16,20},{20,16},{24,28},{28,24},{1,5},{5... | collective-permute-start | bytes 786440 | tf_op jit(solution)/shard_map/ppermute | solution.py:327
  101.9 1.9 %collective-permute-start.33 = (bf16[2,256,256]{2,1,0:T(8,128)(2,1)S(1)}, bf16[2,256,256]{2,1,0:T(8,128)(2,1)S(1)}, u32[]{:S(2)}, u32[]{:S(2)}) collective-permute-start(bf16[2,256,256]{2,1,0:T(8,128)(2,1)S(1)} %get-tuple-element.66.refs_5_), channel_id=1, source_target_pairs={{0,4},{4,0},{8,12},{12,8},{16,20},{20,16},{24,28},{28,24},{1,5},{5... | collective-permute-start | bytes 786440 | tf_op jit(solution)/shard_map/ppermute | solution.py:327
  (13 other events, 28.7 us)

commit v4 on v3

--- a/solution.py
+++ b/solution.py
@@ -469,11 +469,11 @@
     else:
         product = times(core_s, 0, lefts, [[found[0]]], None, maps[1:])
         late = [found[1]]
-    sums = [adjoint_half(core_s, 0, product, swap_all(product), lefts, (), 1, befores)]
+    sums = [adjoint_half(core_s, 0, product, swap_all(product), lefts)]
     groups = [arrivals(1, sums[0])]
     product = times(core_s, 1, lefts, [[part] for part in late], places, sums[0])
     source, source_sent = adjoint_half(
-        core_s, 1, product, swap_all(product), lefts, copies=2
+        core_s, 1, product, swap_all(product), lefts, after=befores, copies=2
     )
     sums.append(source)
     groups.append(arrivals(1, source_sent))
@@ -498,8 +498,10 @@
             befores = maps_before(span, own)
     if slabs > 1:
         others = [swap_all(value) for value in sums]
-        carried = [times(core_s, n, maps, groups[n]) for n in range(2)]
-        theirs = [swap_all(value) for value in carried]
+        carried = [times(core_s, 0, maps, groups[0])]
+        theirs = [swap_all(carried[0])]
+        carried.append(times(core_s, 1, maps, groups[1], None, theirs[0]))
+        theirs.append(swap_all(carried[1]))
         result = adjoint_own(core_s, carried, theirs, maps[0], sums, others)
         return result[:, None, None]
     sums = [value[0] for value in sums]

time: 106 us -> 102 us (0.962)
  waiting for transfers between devices: 42.8 us -> 40.8 us
  local copies, waits for them, and re-layouts: 3.9 us -> 2.21 us
  Pallas kernels: 17.3 us -> 15.7 us
    ppermute x9, waiting for transfers between devices: 20 us -> 16.8 us  [across(): return lax.ppermute(value, 'energy', moves)]
    unnamed x16 -> x22, local copies, waits for them, and re-layouts: 2.62 us -> 0.93 us
    pallas_call x15, Pallas kernels: 17.3 us -> 15.7 us  [call(): pl.pallas_call(body, out_shape=[*outs, *(jax.ShapeDtypeStruct(t.shape, t....]
    ppermute x8, waiting for transfers between devices: 17.6 us -> 18.8 us  [arrivals(): moving = lax.ppermute(moving, 'slab', moves)]
  transfers between devices with their start and end apart: 37 -> 37, of which waited for: 21 -> 23; matrix products, arithmetic and copies ran while one was open for 3% -> 3% of each run, Pallas kernels for 13% -> 13%
where the time goes in v4:
time: 102 us; the launch traced here: 101 us
  waiting for transfers between devices  40.8 us (40%)
  starting transfers between devices  39.9 us (39%)
  Pallas kernels  15.7 us (15%)
  local copies, waits for them, and re-layouts  2.21 us (2%)
  other arithmetic  2.2 us (2%)
    ppermute x19, starting transfers between devices, swap(): return lax.ppermute(value, 'energy', [(i, i ^ 1) for i in range(energies)])  21.9 us
    ppermute x8, waiting for transfers between devices, arrivals(): moving = lax.ppermute(moving, 'slab', moves)  18.8 us
    ppermute x9, waiting for transfers between devices, across(): return lax.ppermute(value, 'energy', moves)  16.8 us
    pallas_call x15, Pallas kernels, call(): pl.pallas_call(body, out_shape=[*outs, *(jax.ShapeDtypeStruct(t.shape, t....  15.7 us
    ppermute x8, starting transfers between devices, arrivals(): moving = lax.ppermute(moving, 'slab', moves)  8.62 us
    ppermute x9, starting transfers between devices, across(): return lax.ppermute(value, 'energy', moves)  8.14 us
    ppermute x19, waiting for transfers between devices, swap(): return lax.ppermute(value, 'energy', [(i, i ^ 1) for i in range(energies)])  5.2 us
  transfers between devices with their start and end apart: 37, of which 23 were waited for; matrix products, arithmetic and copies ran while one was open for 3% of the time, Pallas kernels for 13%

profile of v4, /device:TPU:25, one launch (start us, length us, event | category | flops | bytes accessed | tf_op | source)
XLA Modules:
  0.0 101.4 jit_solution(10742725700407526651)
XLA Ops:
  1.3 1.1 %constant_dynamic-slice_fusion.1 = (bf16[2,1,1,128,256]{4,3,2,1,0:T(8,128)(2,1)S(1)}, bf16[2,1,1,128,256]{4,3,2,1,0:T(8,128)(2,1)S(1)}, bf16[2,1,1,128,256]{4,3,...) fusion(bf16[2,1,1,512,512]{4,3,2,1,0:T(8,128)(2,1)} %param.8, s32[]{:T(128)S(6)} %select_n.46, s32[]{:T(128)S(6)} %select_n.43, ...), kind=kLoop, calls=%fused_computation.7 | loop fusion | bytes 1048596 | tf_op jit(solution)/shard_map/dynamic_slice | solution.py:356
  3.5 1.3 %collective-permute-start.4 = (bf16[528,256]{1,0:T(8,128)(2,1)S(1)}, bf16[528,256]{1,0:T(8,128)(2,1)S(1)}, u32[]{:S(2)}, u32[]{:S(2)}) collective-permute-start(bf16[528,256]{1,0:T(8,128)(2,1)S(1)} %get-tuple-element.78.refs_2_), channel_id=1, source_target_pairs={{0,8},{4,12},{8,0},{12,4},{16,24},{20,28},{24,16},{28,20},{1,9},{5... | collective-permute-start | bytes 811016 | tf_op jit(solution)/shard_map/ppermute | solution.py:352
  4.8 1.2 %collective-permute-start.5 = (bf16[528,256]{1,0:T(8,128)(2,1)S(1)}, bf16[528,256]{1,0:T(8,128)(2,1)S(1)}, u32[]{:S(2)}, u32[]{:S(2)}) collective-permute-start(bf16[528,256]{1,0:T(8,128)(2,1)S(1)} %get-tuple-element.76.refs_3_), channel_id=1, source_target_pairs={{0,16},{4,20},{8,24},{12,28},{16,0},{20,4},{24,8},{28,12},{1,17},{... | collective-permute-start | bytes 811016 | tf_op jit(solution)/shard_map/ppermute | solution.py:352
  8.4 1.3 %collective-permute-start.2 = (bf16[2,512,512]{2,1,0:T(8,128)(2,1)S(1)}, bf16[2,512,512]{2,1,0:T(8,128)(2,1)S(1)}, u32[]{:S(2)}, u32[]{:S(2)}) collective-permute-start(bf16[2,512,512]{2,1,0:T(8,128)(2,1)S(1)} %get-tuple-element.37), channel_id=1, source_target_pairs={{2,3},{6,7},{10,11},{14,15},{18,19},{22,23},{26,27},{30,31}} | collective-permute-start | bytes 3145736 | tf_op jit(solution)/shard_map/ppermute | solution.py:428
  12.1 5.9 %collective-permute-done.6.refs_6_ = bf16[528,256]{1,0:T(8,128)(2,1)S(1)} collective-permute-done((bf16[528,256]{1,0:T(8,128)(2,1)S(1)}, bf16[528,256]{1,0:T(8,128)(2,1)S(1)}, u32[]{:S(2)}, u32[]{:S(2)}) %collective-permute-start.6) | collective-permute-done | bytes 270368 | tf_op jit(solution)/shard_map/ppermute | solution.py:352
  18.0 1.2 %shard_map.65 = (bf16[2,128,256]{2,1,0:T(8,128)(2,1)S(1)}, bf16[2,128,256]{2,1,0:T(8,128)(2,1)S(1)}, bf16[2,128,256]{2,1,0:T(8,128)(2,1)S(1)}, bf16[2,128,256]{2...) custom-call(s32[1]{0:T(128)} %bitcast.12.refs_0_, ...), custom_call_target="tpu_custom_call" | custom-call | flops 6291456 | bytes 2654208 | tf_op jit(solution)/shard_map/pallas_call | solution.py:42
  19.3 1.2 %collective-permute-start.7 = (bf16[2,128,256]{2,1,0:T(8,128)(2,1)S(1)}, bf16[2,128,256]{2,1,0:T(8,128)(2,1)S(1)}, u32[]{:S(2)}, u32[]{:S(2)}) collective-permute-start(bf16[2,128,256]{2,1,0:T(8,128)(2,1)S(1)} %get-tuple-element.39), channel_id=1, source_target_pairs={{0,8},{4,12},{8,0},{12,4},{16,24},{20,28},{24,16},{28,20},{1,9},{5... | collective-permute-start | bytes 393224 | tf_op jit(solution)/shard_map/ppermute | solution.py:352
  20.8 1.2 %collective-permute-start.9 = (bf16[2,128,256]{2,1,0:T(8,128)(2,1)S(1)}, bf16[2,128,256]{2,1,0:T(8,128)(2,1)S(1)}, u32[]{:S(2)}, u32[]{:S(2)}) collective-permute-start(bf16[2,128,256]{2,1,0:T(8,128)(2,1)S(1)} %get-tuple-element.41), channel_id=1, source_target_pairs={{0,24},{4,28},{8,16},{12,20},{16,8},{20,12},{24,0},{28,4},{1,25},{... | collective-permute-start | bytes 393224 | tf_op jit(solution)/shard_map/ppermute | solution.py:352
  23.5 1.8 %collective-permute-done.8.refs_6_ = bf16[2,128,256]{2,1,0:T(8,128)(2,1)S(1)} collective-permute-done((bf16[2,128,256]{2,1,0:T(8,128)(2,1)S(1)}, bf16[2,128,256]{2,1,0:T(8,128)(2,1)S(1)}, u32[]{:S(2)}, u32[]{:S(2)}) %collective-permute-start.8) | collective-permute-done | bytes 131104 | tf_op jit(solution)/shard_map/ppermute | solution.py:352
  25.3 1.2 %collective-permute-done.9.refs_7_ = bf16[2,128,256]{2,1,0:T(8,128)(2,1)S(1)} collective-permute-done((bf16[2,128,256]{2,1,0:T(8,128)(2,1)S(1)}, bf16[2,128,256]{2,1,0:T(8,128)(2,1)S(1)}, u32[]{:S(2)}, u32[]{:S(2)}) %collective-permute-start.9) | collective-permute-done | bytes 131104 | tf_op jit(solution)/shard_map/ppermute | solution.py:352
  26.5 1.3 %shard_map.67 = (bf16[2,256,256]{2,1,0:T(8,128)(2,1)S(1)}, bf16[2,256,256]{2,1,0:T(8,128)(2,1)S(1)}, bf16[2,128,256]{2,1,0:T(8,128)(2,1)S(1)}, bf16[2,128,256]{2,1,0:T(8,128)(2,1)S(1)}, bf16[2,128,256]{2,1,0:T(8,128)(2,1)S(1)}) custom-call(s32[1]{0:T(128)} %bitcast.refs_0_, s32[4]{0:T(128)S(1)} %iota_xor_fusion.refs_1_, bf16[2,512,512]{2,1,0:T(8,128)(2,1)S(1)} %bitcast.27, ...), custom_call_target="tpu_custom_call" | custom-call | flops 536870912 | bytes 3145728 | tf_op jit(solution)/shard_map/pallas_call | solution.py:42
  27.8 2.8 %collective-permute-start.10 = (bf16[2,256,256]{2,1,0:T(8,128)(2,1)S(1)}, bf16[2,256,256]{2,1,0:T(8,128)(2,1)S(1)}, u32[]{:S(2)}, u32[]{:S(2)}) collective-permute-start(bf16[2,256,256]{2,1,0:T(8,128)(2,1)S(1)} %get-tuple-element.45.refs_1_), channel_id=1, source_target_pairs={{0,4},{4,0},{8,12},{12,8},{16,20},{20,16},{24,28},{28,24},{1,5},{5... | collective-permute-start | bytes 786440 | tf_op jit(solution)/shard_map/ppermute | solution.py:327
  32.9 1.3 %collective-permute-start.12 = (bf16[2,512,256]{2,1,0:T(8,128)(2,1)S(1)}, bf16[2,512,256]{2,1,0:T(8,128)(2,1)S(1)}, u32[]{:S(2)}, u32[]{:S(2)}) collective-permute-start(bf16[2,512,256]{2,1,0:T(8,128)(2,1)S(1)} %shard_map.68.refs_8_.refs_7_), channel_id=1, source_target_pairs={{0,1},{2,3},{4,5},{6,7},{8,9},{10,11},{12,13},{14,15},{16,17},{18,... | collective-permute-start | bytes 1572872 | tf_op jit(solution)/shard_map/ppermute | solution.py:445
  36.9 2.0 %collective-permute-done.13.refs_5_ = bf16[2,128,256]{2,1,0:T(8,128)(2,1)S(1)} collective-permute-done((bf16[2,128,256]{2,1,0:T(8,128)(2,1)S(1)}, bf16[2,128,256]{2,1,0:T(8,128)(2,1)S(1)}, u32[]{:S(2)}, u32[]{:S(2)}) %collective-permute-start.13) | collective-permute-done | bytes 131104 | tf_op jit(solution)/shard_map/ppermute | solution.py:352
  39.6 2.9 %collective-permute-done.15.refs_7_ = bf16[2,128,256]{2,1,0:T(8,128)(2,1)S(1)} collective-permute-done((bf16[2,128,256]{2,1,0:T(8,128)(2,1)S(1)}, bf16[2,128,256]{2,1,0:T(8,128)(2,1)S(1)}, u32[]{:S(2)}, u32[]{:S(2)}) %collective-permute-start.15) | collective-permute-done | bytes 131104 | tf_op jit(solution)/shard_map/ppermute | solution.py:352
  42.5 1.3 %shard_map.69 = (bf16[2,256,256]{2,1,0:T(8,128)(2,1)S(1)}, bf16[2,256,256]{2,1,0:T(8,128)(2,1)S(1)}) custom-call(s32[1]{0:T(128)} %bitcast.refs_0_, s32[4]{0:T(128)S(1)} %iota_xor_fusion.refs_1_, bf16[2,512,512]{2,1,0:T(8,128)(2,1)S(1)} %bitcast.29, bf16[2,512,512]{2,1,0:T(8,128)(2,1)S(1)} %collective-permute-done.3.refs_0_.refs_3_.refs_6_, ...), custom_call_target="tpu_custom_call" | custom-call | flops 536870912 | bytes 3145728 | tf_op jit(solution)/shard_map/pallas_call | solution.py:42
  43.8 1.5 %collective-permute-start.16 = (bf16[2,256,256]{2,1,0:T(8,128)(2,1)S(1)}, bf16[2,256,256]{2,1,0:T(8,128)(2,1)S(1)}, u32[]{:S(2)}, u32[]{:S(2)}) collective-permute-start(bf16[2,256,256]{2,1,0:T(8,128)(2,1)S(1)} %get-tuple-element.51.refs_1_), channel_id=1, source_target_pairs={{0,4},{4,0},{8,12},{12,8},{16,20},{20,16},{24,28},{28,24},{1,5},{5... | collective-permute-start | bytes 786440 | tf_op jit(solution)/shard_map/ppermute | solution.py:327
  48.9 1.1 %collective-permute-start.18 = (bf16[2,256,256]{2,1,0:T(8,128)(2,1)S(1)}, bf16[2,256,256]{2,1,0:T(8,128)(2,1)S(1)}, u32[]{:S(2)}, u32[]{:S(2)}) collective-permute-start(bf16[2,256,256]{2,1,0:T(8,128)(2,1)S(1)} %get-tuple-element.54.refs_1_), channel_id=1, source_target_pairs={{0,4},{4,0},{8,12},{12,8},{16,20},{20,16},{24,28},{28,24},{1,5},{5... | collective-permute-start | bytes 786440 | tf_op jit(solution)/shard_map/ppermute | solution.py:327
  50.0 1.4 %collective-permute-start.23 = (bf16[2,512,256]{2,1,0:T(8,128)(2,1)}, bf16[2,512,256]{2,1,0:T(8,128)(2,1)S(1)}, u32[]{:S(2)}, u32[]{:S(2)}) collective-permute-start(bf16[2,512,256]{2,1,0:T(8,128)(2,1)} %copy-done.8), channel_id=1, source_target_pairs={{0,1},{2,3},{4,5},{6,7},{8,9},{10,11},{12,13},{14,15},{16,17},{18,... | collective-permute-start | bytes 1572872 | tf_op jit(solution)/shard_map/ppermute | solution.py:445
  51.6 1.7 %shard_map.72 = (bf16[2,512,256]{2,1,0:T(8,128)(2,1)S(1)}, bf16[2,512,256]{2,1,0:T(8,128)(2,1)S(1)}) custom-call(s32[1]{0:T(128)} %bitcast.refs_0_, bf16[2,256,256]{2,1,0:T(8,128)(2,1)S(1)} %get-tuple-element.54.refs_1_, bf16[2,256,256]{2,1,0:T(8,128)(2,1)S(1)} %get-tuple-element.55.refs_2_, bf16[2,256,256]{2,1,0:T(8,128)(2,1)S(1)} %collective-permute-done.18.refs_3_, ...), custom_call_target="tpu_custom_call" | custom-call | flops 536870912 | bytes 4718592 | tf_op jit(solution)/shard_map/pallas_call | solution.py:42
  54.0 1.4 %shard_map.73.refs_1_.refs_4_ = bf16[2,512,512]{2,1,0:T(8,128)(2,1)S(1)} custom-call(s32[1]{0:T(128)} %bitcast.1.refs_0_, bf16[2,512,512]{2,1,0:T(8,128)(2,1)S(1)} %get-tuple-element.36.refs_1_.refs_5_, bf16[2,512,512]{2,1,0:T(8,128)(2,1)S(1)} %copy-done.7, bf16[2,512,256]{2,1,0:T(8,128)(2,1)S(1)} %get-tuple-element.56.refs_3_.refs_5_.refs_10_), custom_call_target="tpu_custom_call" | custom-call | flops 1073741824 | bytes 3145728 | tf_op jit(solution)/shard_map/pallas_call | solution.py:42
  56.0 9.4 %collective-permute-done.23.refs_3_ = bf16[2,512,256]{2,1,0:T(8,128)(2,1)S(1)} collective-permute-done((bf16[2,512,256]{2,1,0:T(8,128)(2,1)}, bf16[2,512,256]{2,1,0:T(8,128)(2,1)S(1)}, u32[]{:S(2)}, u32[]{:S(2)}) %collective-permute-start.23) | collective-permute-done | bytes 524320 | tf_op jit(solution)/shard_map/ppermute | solution.py:445
  66.1 1.3 %collective-permute-start.24 = (bf16[2,256,256]{2,1,0:T(8,128)(2,1)S(1)}, bf16[2,256,256]{2,1,0:T(8,128)(2,1)S(1)}, u32[]{:S(2)}, u32[]{:S(2)}) collective-permute-start(bf16[2,256,256]{2,1,0:T(8,128)(2,1)S(1)} %get-tuple-element.61.refs_1_), channel_id=1, source_target_pairs={{0,4},{4,0},{8,12},{12,8},{16,20},{20,16},{24,28},{28,24},{1,5},{5... | collective-permute-start | bytes 786440 | tf_op jit(solution)/shard_map/ppermute | solution.py:327
  67.5 1.3 %collective-permute-start.22 = (bf16[2,512,256]{2,1,0:T(8,128)(2,1)S(1)}, bf16[2,512,256]{2,1,0:T(8,128)(2,1)S(1)}, u32[]{:S(2)}, u32[]{:S(2)}) collective-permute-start(bf16[2,512,256]{2,1,0:T(8,128)(2,1)S(1)} %collective-permute-done.21.refs_3_.refs_8_), channel_id=1, source_target_pairs={{2,3},{6,7},{10,11},{14,15},{18,19},{22,23},{26,27},{30,31}} | collective-permute-start | bytes 1572872 | tf_op jit(solution)/shard_map/ppermute | solution.py:445
  71.1 1.3 %collective-permute-start.27 = (bf16[2,256,256]{2,1,0:T(8,128)(2,1)S(1)}, bf16[2,256,256]{2,1,0:T(8,128)(2,1)S(1)}, u32[]{:S(2)}, u32[]{:S(2)}) collective-permute-start(bf16[2,256,256]{2,1,0:T(8,128)(2,1)S(1)} %collective-permute-done.26.refs_3_), channel_id=1, source_target_pairs={{2,3},{6,7},{10,11},{14,15},{18,19},{22,23},{26,27},{30,31}} | collective-permute-start | bytes 786440 | tf_op jit(solution)/shard_map/ppermute | solution.py:445
  72.4 1.3 %collective-permute-start.29 = (bf16[2,256,256]{2,1,0:T(8,128)(2,1)S(1)}, bf16[2,256,256]{2,1,0:T(8,128)(2,1)S(1)}, u32[]{:S(2)}, u32[]{:S(2)}) collective-permute-start(bf16[2,256,256]{2,1,0:T(8,128)(2,1)S(1)} %collective-permute-done.28.refs_5_), channel_id=1, source_target_pairs={{2,3},{6,7},{10,11},{14,15},{18,19},{22,23},{26,27},{30,31}} | collective-permute-start | bytes 786440 | tf_op jit(solution)/shard_map/ppermute | solution.py:445
  73.7 8.2 %collective-permute-done.22.refs_4_ = bf16[2,512,256]{2,1,0:T(8,128)(2,1)S(1)} collective-permute-done((bf16[2,512,256]{2,1,0:T(8,128)(2,1)S(1)}, bf16[2,512,256]{2,1,0:T(8,128)(2,1)S(1)}, u32[]{:S(2)}, u32[]{:S(2)}) %collective-permute-start.22) | collective-permute-done | bytes 524320 | tf_op jit(solution)/shard_map/ppermute | solution.py:445
  82.6 3.2 %collective-permute-start.30 = (bf16[2,256,256]{2,1,0:T(8,128)(2,1)S(1)}, bf16[2,256,256]{2,1,0:T(8,128)(2,1)S(1)}, u32[]{:S(2)}, u32[]{:S(2)}) collective-permute-start(bf16[2,256,256]{2,1,0:T(8,128)(2,1)S(1)} %get-tuple-element.58.refs_2_), channel_id=1, source_target_pairs={{0,4},{4,0},{8,12},{12,8},{16,20},{20,16},{24,28},{28,24},{1,5},{5... | collective-permute-start | bytes 786440 | tf_op jit(solution)/shard_map/ppermute | solution.py:327
  86.4 6.3 %collective-permute-start.35 = (bf16[2,256,256]{2,1,0:T(8,128)(2,1)S(1)}, bf16[2,256,256]{2,1,0:T(8,128)(2,1)S(1)}, u32[]{:S(2)}, u32[]{:S(2)}) collective-permute-start(bf16[2,256,256]{2,1,0:T(8,128)(2,1)S(1)} %get-tuple-element.63.refs_11_), channel_id=1, source_target_pairs={{0,4},{4,0},{8,12},{12,8},{16,20},{20,16},{24,28},{28,24},{1,5},{5... | collective-permute-start | bytes 786440 | tf_op jit(solution)/shard_map/ppermute | solution.py:327
  92.7 1.2 %collective-permute-done.29.refs_6_ = bf16[2,256,256]{2,1,0:T(8,128)(2,1)S(1)} collective-permute-done((bf16[2,256,256]{2,1,0:T(8,128)(2,1)S(1)}, bf16[2,256,256]{2,1,0:T(8,128)(2,1)S(1)}, u32[]{:S(2)}, u32[]{:S(2)}) %collective-permute-start.29) | collective-permute-done | bytes 262176 | tf_op jit(solution)/shard_map/ppermute | solution.py:445
  93.9 2.4 %collective-permute-start.36 = (bf16[2,256,256]{2,1,0:T(8,128)(2,1)S(1)}, bf16[2,256,256]{2,1,0:T(8,128)(2,1)S(1)}, u32[]{:S(2)}, u32[]{:S(2)}) collective-permute-start(bf16[2,256,256]{2,1,0:T(8,128)(2,1)S(1)} %get-tuple-element.64.refs_12_), channel_id=1, source_target_pairs={{0,4},{4,0},{8,12},{12,8},{16,20},{20,16},{24,28},{28,24},{1,5},{5... | collective-permute-start | bytes 786440 | tf_op jit(solution)/shard_map/ppermute | solution.py:327
  99.1 2.1 %shard_map.78 = bf16[2,512,512]{2,1,0:T(8,128)(2,1)} custom-call(s32[1]{0:T(128)} %bitcast.refs_0_, bf16[2,512,512]{2,1,0:T(8,128)(2,1)S(1)} %shard_map.73.refs_1_.refs_4_, bf16[2,256,256]{2,1,0:T(8,128)(2,1)S(1)} %get-tuple-element.58.refs_2_, bf16[2,256,256]{2,1,0:T(8,128)(2,1)S(1)} %get-tuple-element.59.refs_3_, ...), custom_call_target="tpu_custom_call" | custom-call | flops 1073741824 | bytes 6291456 | tf_op jit(solution)/shard_map/pallas_call | solution.py:42
  (91 shorter events, 26.5 us)
Async XLA Ops:
  0.0 3.2 %collective-permute-start = (bf16[2,512,512]{2,1,0:T(8,128)(2,1)}, bf16[2,512,512]{2,1,0:T(8,128)(2,1)S(1)}, u32[]{:S(2)}, u32[]{:S(2)}) collective-permute-start(bf16[2,512,512]{2,1,0:T(8,128)(2,1)} %bitcast.41), channel_id=1, source_target_pairs={{0,4},{4,0},{8,12},{12,8},{16,20},{20,16},{24,28},{28,24},{1,5},{5... | collective-permute-start | bytes 3145736 | tf_op jit(solution)/shard_map/ppermute | solution.py:327
  0.7 2.3 %collective-permute-start.1 = (s32[1,2]{1,0:T(1,128)S(1)}, s32[1,2]{1,0:T(1,128)S(1)}, u32[]{:S(2)}, u32[]{:S(2)}) collective-permute-start(s32[1,2]{1,0:T(1,128)S(1)} %copy-done.10), channel_id=1, source_target_pairs={{0,4},{4,0},{8,12},{12,8},{16,20},{20,16},{24,28},{28,24},{1,5},{5... | collective-permute-start | bytes 32 | tf_op jit(solution)/shard_map/ppermute | solution.py:327
  1.3 20.7 %collective-permute-start.3 = (bf16[2,512,512]{2,1,0:T(8,128)(2,1)}, bf16[2,512,512]{2,1,0:T(8,128)(2,1)S(1)}, u32[]{:S(2)}, u32[]{:S(2)}) collective-permute-start(bf16[2,512,512]{2,1,0:T(8,128)(2,1)} %bitcast.25), channel_id=1, source_target_pairs={{0,4},{4,0},{8,12},{12,8},{16,20},{20,16},{24,28},{28,24},{1,5},{5... | collective-permute-start | bytes 3145736 | tf_op jit(solution)/shard_map/ppermute | solution.py:327
  3.5 7.8 %collective-permute-start.4 = (bf16[528,256]{1,0:T(8,128)(2,1)S(1)}, bf16[528,256]{1,0:T(8,128)(2,1)S(1)}, u32[]{:S(2)}, u32[]{:S(2)}) collective-permute-start(bf16[528,256]{1,0:T(8,128)(2,1)S(1)} %get-tuple-element.78.refs_2_), channel_id=1, source_target_pairs={{0,8},{4,12},{8,0},{12,4},{16,24},{20,28},{24,16},{28,20},{1,9},{5... | collective-permute-start | bytes 811016 | tf_op jit(solution)/shard_map/ppermute | solution.py:352
  4.8 7.4 %collective-permute-start.5 = (bf16[528,256]{1,0:T(8,128)(2,1)S(1)}, bf16[528,256]{1,0:T(8,128)(2,1)S(1)}, u32[]{:S(2)}, u32[]{:S(2)}) collective-permute-start(bf16[528,256]{1,0:T(8,128)(2,1)S(1)} %get-tuple-element.76.refs_3_), channel_id=1, source_target_pairs={{0,16},{4,20},{8,24},{12,28},{16,0},{20,4},{24,8},{28,12},{1,17},{... | collective-permute-start | bytes 811016 | tf_op jit(solution)/shard_map/ppermute | solution.py:352
  6.0 12.0 %collective-permute-start.6 = (bf16[528,256]{1,0:T(8,128)(2,1)S(1)}, bf16[528,256]{1,0:T(8,128)(2,1)S(1)}, u32[]{:S(2)}, u32[]{:S(2)}) collective-permute-start(bf16[528,256]{1,0:T(8,128)(2,1)S(1)} %get-tuple-element.77.refs_4_), channel_id=1, source_target_pairs={{0,24},{4,28},{8,16},{12,20},{16,8},{20,12},{24,0},{28,4},{1,25},{... | collective-permute-start | bytes 811016 | tf_op jit(solution)/shard_map/ppermute | solution.py:352
  8.4 38.5 %collective-permute-start.2 = (bf16[2,512,512]{2,1,0:T(8,128)(2,1)S(1)}, bf16[2,512,512]{2,1,0:T(8,128)(2,1)S(1)}, u32[]{:S(2)}, u32[]{:S(2)}) collective-permute-start(bf16[2,512,512]{2,1,0:T(8,128)(2,1)S(1)} %get-tuple-element.37), channel_id=1, source_target_pairs={{2,3},{6,7},{10,11},{14,15},{18,19},{22,23},{26,27},{30,31}} | collective-permute-start | bytes 3145736 | tf_op jit(solution)/shard_map/ppermute | solution.py:428
  19.3 4.2 %collective-permute-start.7 = (bf16[2,128,256]{2,1,0:T(8,128)(2,1)S(1)}, bf16[2,128,256]{2,1,0:T(8,128)(2,1)S(1)}, u32[]{:S(2)}, u32[]{:S(2)}) collective-permute-start(bf16[2,128,256]{2,1,0:T(8,128)(2,1)S(1)} %get-tuple-element.39), channel_id=1, source_target_pairs={{0,8},{4,12},{8,0},{12,4},{16,24},{20,28},{24,16},{28,20},{1,9},{5... | collective-permute-start | bytes 393224 | tf_op jit(solution)/shard_map/ppermute | solution.py:352
  20.5 4.8 %collective-permute-start.8 = (bf16[2,128,256]{2,1,0:T(8,128)(2,1)S(1)}, bf16[2,128,256]{2,1,0:T(8,128)(2,1)S(1)}, u32[]{:S(2)}, u32[]{:S(2)}) collective-permute-start(bf16[2,128,256]{2,1,0:T(8,128)(2,1)S(1)} %get-tuple-element.40), channel_id=1, source_target_pairs={{0,16},{4,20},{8,24},{12,28},{16,0},{20,4},{24,8},{28,12},{1,17},{... | collective-permute-start | bytes 393224 | tf_op jit(solution)/shard_map/ppermute | solution.py:352
  20.8 5.7 %collective-permute-start.9 = (bf16[2,128,256]{2,1,0:T(8,128)(2,1)S(1)}, bf16[2,128,256]{2,1,0:T(8,128)(2,1)S(1)}, u32[]{:S(2)}, u32[]{:S(2)}) collective-permute-start(bf16[2,128,256]{2,1,0:T(8,128)(2,1)S(1)} %get-tuple-element.41), channel_id=1, source_target_pairs={{0,24},{4,28},{8,16},{12,20},{16,8},{20,12},{24,0},{28,4},{1,25},{... | collective-permute-start | bytes 393224 | tf_op jit(solution)/shard_map/ppermute | solution.py:352
  27.8 4.0 %collective-permute-start.10 = (bf16[2,256,256]{2,1,0:T(8,128)(2,1)S(1)}, bf16[2,256,256]{2,1,0:T(8,128)(2,1)S(1)}, u32[]{:S(2)}, u32[]{:S(2)}) collective-permute-start(bf16[2,256,256]{2,1,0:T(8,128)(2,1)S(1)} %get-tuple-element.45.refs_1_), channel_id=1, source_target_pairs={{0,4},{4,0},{8,12},{12,8},{16,20},{20,16},{24,28},{28,24},{1,5},{5... | collective-permute-start | bytes 786440 | tf_op jit(solution)/shard_map/ppermute | solution.py:327
  32.9 15.0 %collective-permute-start.12 = (bf16[2,512,256]{2,1,0:T(8,128)(2,1)S(1)}, bf16[2,512,256]{2,1,0:T(8,128)(2,1)S(1)}, u32[]{:S(2)}, u32[]{:S(2)}) collective-permute-start(bf16[2,512,256]{2,1,0:T(8,128)(2,1)S(1)} %shard_map.68.refs_8_.refs_7_), channel_id=1, source_target_pairs={{0,1},{2,3},{4,5},{6,7},{8,9},{10,11},{12,13},{14,15},{16,17},{18,... | collective-permute-start | bytes 1572872 | tf_op jit(solution)/shard_map/ppermute | solution.py:445
  34.2 4.7 %collective-permute-start.13 = (bf16[2,128,256]{2,1,0:T(8,128)(2,1)S(1)}, bf16[2,128,256]{2,1,0:T(8,128)(2,1)S(1)}, u32[]{:S(2)}, u32[]{:S(2)}) collective-permute-start(bf16[2,128,256]{2,1,0:T(8,128)(2,1)S(1)} %get-tuple-element.48), channel_id=1, source_target_pairs={{0,8},{4,12},{8,0},{12,4},{16,24},{20,28},{24,16},{28,20},{1,9},{5... | collective-permute-start | bytes 393224 | tf_op jit(solution)/shard_map/ppermute | solution.py:352
  35.2 4.4 %collective-permute-start.14 = (bf16[2,128,256]{2,1,0:T(8,128)(2,1)S(1)}, bf16[2,128,256]{2,1,0:T(8,128)(2,1)S(1)}, u32[]{:S(2)}, u32[]{:S(2)}) collective-permute-start(bf16[2,128,256]{2,1,0:T(8,128)(2,1)S(1)} %get-tuple-element.49), channel_id=1, source_target_pairs={{0,16},{4,20},{8,24},{12,28},{16,0},{20,4},{24,8},{28,12},{1,17},{... | collective-permute-start | bytes 393224 | tf_op jit(solution)/shard_map/ppermute | solution.py:352
  36.0 6.6 %collective-permute-start.15 = (bf16[2,128,256]{2,1,0:T(8,128)(2,1)S(1)}, bf16[2,128,256]{2,1,0:T(8,128)(2,1)S(1)}, u32[]{:S(2)}, u32[]{:S(2)}) collective-permute-start(bf16[2,128,256]{2,1,0:T(8,128)(2,1)S(1)} %get-tuple-element.50), channel_id=1, source_target_pairs={{0,24},{4,28},{8,16},{12,20},{16,8},{20,12},{24,0},{28,4},{1,25},{... | collective-permute-start | bytes 393224 | tf_op jit(solution)/shard_map/ppermute | solution.py:352
  43.8 2.7 %collective-permute-start.16 = (bf16[2,256,256]{2,1,0:T(8,128)(2,1)S(1)}, bf16[2,256,256]{2,1,0:T(8,128)(2,1)S(1)}, u32[]{:S(2)}, u32[]{:S(2)}) collective-permute-start(bf16[2,256,256]{2,1,0:T(8,128)(2,1)S(1)} %get-tuple-element.51.refs_1_), channel_id=1, source_target_pairs={{0,4},{4,0},{8,12},{12,8},{16,20},{20,16},{24,28},{28,24},{1,5},{5... | collective-permute-start | bytes 786440 | tf_op jit(solution)/shard_map/ppermute | solution.py:327
  48.9 2.6 %collective-permute-start.18 = (bf16[2,256,256]{2,1,0:T(8,128)(2,1)S(1)}, bf16[2,256,256]{2,1,0:T(8,128)(2,1)S(1)}, u32[]{:S(2)}, u32[]{:S(2)}) collective-permute-start(bf16[2,256,256]{2,1,0:T(8,128)(2,1)S(1)} %get-tuple-element.54.refs_1_), channel_id=1, source_target_pairs={{0,4},{4,0},{8,12},{12,8},{16,20},{20,16},{24,28},{28,24},{1,5},{5... | collective-permute-start | bytes 786440 | tf_op jit(solution)/shard_map/ppermute | solution.py:327
  50.0 1.7 %collective-permute-start.19 = (bf16[2,256,256]{2,1,0:T(8,128)(2,1)S(1)}, bf16[2,256,256]{2,1,0:T(8,128)(2,1)}, u32[]{:S(2)}, u32[]{:S(2)}) collective-permute-start(bf16[2,256,256]{2,1,0:T(8,128)(2,1)S(1)} %get-tuple-element.55.refs_2_), channel_id=1, source_target_pairs={{0,4},{4,0},{8,12},{12,8},{16,20},{20,16},{24,28},{28,24},{1,5},{5... | collective-permute-start | bytes 786440 | tf_op jit(solution)/shard_map/ppermute | solution.py:327
  50.0 15.3 %collective-permute-start.23 = (bf16[2,512,256]{2,1,0:T(8,128)(2,1)}, bf16[2,512,256]{2,1,0:T(8,128)(2,1)S(1)}, u32[]{:S(2)}, u32[]{:S(2)}) collective-permute-start(bf16[2,512,256]{2,1,0:T(8,128)(2,1)} %copy-done.8), channel_id=1, source_target_pairs={{0,1},{2,3},{4,5},{6,7},{8,9},{10,11},{12,13},{14,15},{16,17},{18,... | collective-permute-start | bytes 1572872 | tf_op jit(solution)/shard_map/ppermute | solution.py:445
  53.3 14.1 %collective-permute-start.21 = (bf16[2,512,256]{2,1,0:T(8,128)(2,1)S(1)}, bf16[2,512,256]{2,1,0:T(8,128)(2,1)S(1)}, u32[]{:S(2)}, u32[]{:S(2)}) collective-permute-start(bf16[2,512,256]{2,1,0:T(8,128)(2,1)S(1)} %get-tuple-element.57), channel_id=1, source_target_pairs={{1,2},{5,6},{9,10},{13,14},{17,18},{21,22},{25,26},{29,30}} | collective-permute-start | bytes 1572872 | tf_op jit(solution)/shard_map/ppermute | solution.py:445
  55.5 18.2 %collective-permute-start.20 = (bf16[2,512,512]{2,1,0:T(8,128)(2,1)S(1)}, bf16[2,512,512]{2,1,0:T(8,128)(2,1)S(1)}, u32[]{:S(2)}, u32[]{:S(2)}) collective-permute-start(bf16[2,512,512]{2,1,0:T(8,128)(2,1)S(1)} %shard_map.73.refs_1_.refs_4_), channel_id=1, source_target_pairs={{0,4},{4,0},{8,12},{12,8},{16,20},{20,16},{24,28},{28,24},{1,5},{5... | collective-permute-start | bytes 3145736 | tf_op jit(solution)/shard_map/ppermute | solution.py:327
  66.1 2.7 %collective-permute-start.24 = (bf16[2,256,256]{2,1,0:T(8,128)(2,1)S(1)}, bf16[2,256,256]{2,1,0:T(8,128)(2,1)S(1)}, u32[]{:S(2)}, u32[]{:S(2)}) collective-permute-start(bf16[2,256,256]{2,1,0:T(8,128)(2,1)S(1)} %get-tuple-element.61.refs_1_), channel_id=1, source_target_pairs={{0,4},{4,0},{8,12},{12,8},{16,20},{20,16},{24,28},{28,24},{1,5},{5... | collective-permute-start | bytes 786440 | tf_op jit(solution)/shard_map/ppermute | solution.py:327
  67.5 14.4 %collective-permute-start.22 = (bf16[2,512,256]{2,1,0:T(8,128)(2,1)S(1)}, bf16[2,512,256]{2,1,0:T(8,128)(2,1)S(1)}, u32[]{:S(2)}, u32[]{:S(2)}) collective-permute-start(bf16[2,512,256]{2,1,0:T(8,128)(2,1)S(1)} %collective-permute-done.21.refs_3_.refs_8_), channel_id=1, source_target_pairs={{2,3},{6,7},{10,11},{14,15},{18,19},{22,23},{26,27},{30,31}} | collective-permute-start | bytes 1572872 | tf_op jit(solution)/shard_map/ppermute | solution.py:445
  70.4 2.0 %collective-permute-start.28 = (bf16[2,256,256]{2,1,0:T(8,128)(2,1)S(1)}, bf16[2,256,256]{2,1,0:T(8,128)(2,1)S(1)}, u32[]{:S(2)}, u32[]{:S(2)}) collective-permute-start(bf16[2,256,256]{2,1,0:T(8,128)(2,1)S(1)} %get-tuple-element.64.refs_12_), channel_id=1, source_target_pairs={{1,2},{5,6},{9,10},{13,14},{17,18},{21,22},{25,26},{29,30}} | collective-permute-start | bytes 786440 | tf_op jit(solution)/shard_map/ppermute | solution.py:445
  71.1 15.3 %collective-permute-start.27 = (bf16[2,256,256]{2,1,0:T(8,128)(2,1)S(1)}, bf16[2,256,256]{2,1,0:T(8,128)(2,1)S(1)}, u32[]{:S(2)}, u32[]{:S(2)}) collective-permute-start(bf16[2,256,256]{2,1,0:T(8,128)(2,1)S(1)} %collective-permute-done.26.refs_3_), channel_id=1, source_target_pairs={{2,3},{6,7},{10,11},{14,15},{18,19},{22,23},{26,27},{30,31}} | collective-permute-start | bytes 786440 | tf_op jit(solution)/shard_map/ppermute | solution.py:445
  72.4 21.5 %collective-permute-start.29 = (bf16[2,256,256]{2,1,0:T(8,128)(2,1)S(1)}, bf16[2,256,256]{2,1,0:T(8,128)(2,1)S(1)}, u32[]{:S(2)}, u32[]{:S(2)}) collective-permute-start(bf16[2,256,256]{2,1,0:T(8,128)(2,1)S(1)} %collective-permute-done.28.refs_5_), channel_id=1, source_target_pairs={{2,3},{6,7},{10,11},{14,15},{18,19},{22,23},{26,27},{30,31}} | collective-permute-start | bytes 786440 | tf_op jit(solution)/shard_map/ppermute | solution.py:445
  82.6 13.7 %collective-permute-start.30 = (bf16[2,256,256]{2,1,0:T(8,128)(2,1)S(1)}, bf16[2,256,256]{2,1,0:T(8,128)(2,1)S(1)}, u32[]{:S(2)}, u32[]{:S(2)}) collective-permute-start(bf16[2,256,256]{2,1,0:T(8,128)(2,1)S(1)} %get-tuple-element.58.refs_2_), channel_id=1, source_target_pairs={{0,4},{4,0},{8,12},{12,8},{16,20},{20,16},{24,28},{28,24},{1,5},{5... | collective-permute-start | bytes 786440 | tf_op jit(solution)/shard_map/ppermute | solution.py:327
  85.9 10.4 %collective-permute-start.31 = (bf16[2,256,256]{2,1,0:T(8,128)(2,1)S(1)}, bf16[2,256,256]{2,1,0:T(8,128)(2,1)S(1)}, u32[]{:S(2)}, u32[]{:S(2)}) collective-permute-start(bf16[2,256,256]{2,1,0:T(8,128)(2,1)S(1)} %get-tuple-element.59.refs_3_), channel_id=1, source_target_pairs={{0,4},{4,0},{8,12},{12,8},{16,20},{20,16},{24,28},{28,24},{1,5},{5... | collective-permute-start | bytes 786440 | tf_op jit(solution)/shard_map/ppermute | solution.py:327
  85.9 11.7 %collective-permute-start.34 = (bf16[2,512,256]{2,1,0:T(8,128)(2,1)S(1)}, bf16[2,512,256]{2,1,0:T(8,128)(2,1)S(1)}, u32[]{:S(2)}, u32[]{:S(2)}) collective-permute-start(bf16[2,512,256]{2,1,0:T(8,128)(2,1)S(1)} %get-tuple-element.56.refs_3_.refs_5_.refs_10_), channel_id=1, source_target_pairs={{0,4},{4,0},{8,12},{12,8},{16,20},{20,16},{24,28},{28,24},{1,5},{5... | collective-permute-start | bytes 1572872 | tf_op jit(solution)/shard_map/ppermute | solution.py:327
  86.4 11.3 %collective-permute-start.35 = (bf16[2,256,256]{2,1,0:T(8,128)(2,1)S(1)}, bf16[2,256,256]{2,1,0:T(8,128)(2,1)S(1)}, u32[]{:S(2)}, u32[]{:S(2)}) collective-permute-start(bf16[2,256,256]{2,1,0:T(8,128)(2,1)S(1)} %get-tuple-element.63.refs_11_), channel_id=1, source_target_pairs={{0,4},{4,0},{8,12},{12,8},{16,20},{20,16},{24,28},{28,24},{1,5},{5... | collective-permute-start | bytes 786440 | tf_op jit(solution)/shard_map/ppermute | solution.py:327
  93.9 3.8 %collective-permute-start.36 = (bf16[2,256,256]{2,1,0:T(8,128)(2,1)S(1)}, bf16[2,256,256]{2,1,0:T(8,128)(2,1)S(1)}, u32[]{:S(2)}, u32[]{:S(2)}) collective-permute-start(bf16[2,256,256]{2,1,0:T(8,128)(2,1)S(1)} %get-tuple-element.64.refs_12_), channel_id=1, source_target_pairs={{0,4},{4,0},{8,12},{12,8},{16,20},{20,16},{24,28},{28,24},{1,5},{5... | collective-permute-start | bytes 786440 | tf_op jit(solution)/shard_map/ppermute | solution.py:327
  97.2 1.9 %collective-permute-start.33 = (bf16[2,256,256]{2,1,0:T(8,128)(2,1)S(1)}, bf16[2,256,256]{2,1,0:T(8,128)(2,1)S(1)}, u32[]{:S(2)}, u32[]{:S(2)}) collective-permute-start(bf16[2,256,256]{2,1,0:T(8,128)(2,1)S(1)} %get-tuple-element.66.refs_5_), channel_id=1, source_target_pairs={{0,4},{4,0},{8,12},{12,8},{16,20},{20,16},{24,28},{28,24},{1,5},{5... | collective-permute-start | bytes 786440 | tf_op jit(solution)/shard_map/ppermute | solution.py:327
  (16 other events, 52.7 us)

commit v5 on v4

--- a/solution.py
+++ b/solution.py
@@ -55,6 +55,15 @@
 
 def block(*shape):
     return jax.ShapeDtypeStruct(shape, BF)
+
+
+def where_active(active_ref, work, otherwise=None):
+    if active_ref is None:
+        work()
+        return
+    pl.when(active_ref[0] == 1)(work)
+    if otherwise is not None:
+        pl.when(active_ref[0] != 1)(otherwise)
 
 
 def either(core_ref, number, work):
@@ -132,17 +141,19 @@
         put_rows(outs, 1, i, tile, dot(lr, imag) + dot(li, real))
 
 
-def times(core, number, lefts, groups, places=None, after=(), tied=()):
+def times(core, number, lefts, groups, places=None, after=(), tied=(), active=None):
     size = lefts[0].shape[1]
     rows, width = groups[0][0].shape[1:]
     full = (2, rows * len(groups), width)
     counts = [len(group) for group in groups]
     scalars = [core] if places is None else [core, places]
+    scalars += [] if active is None else [active]
     whole = counts == [1]
 
     def kernel(core_ref, *refs):
         refs = list(refs)
         places_ref = refs.pop(0) if places is not None else None
+        active_ref = refs.pop(0) if active is not None else None
         left_refs = [refs.pop(0) for _ in range(2)]
         if whole:
             right, *out_refs = refs
@@ -158,7 +169,11 @@
                 for _ in range(count - 1):
                     value = value + refs.pop(0)[...]
                 right[:, at, :] = value
-        either(core_ref, number, lambda n: times_into(left_refs[n], right, out_refs))
+
+        def work():
+            either(core_ref, number, lambda n: times_into(left_refs[n], right, out_refs))
+
+        where_active(active_ref, work)
 
     return call(
         kernel,
@@ -235,12 +250,14 @@
     return *found, refs
 
 
-def adjoint_half(core, number, mine, theirs, rights, summand=(), cuts=1, after=(), copies=1):
+def adjoint_half(core, number, mine, theirs, rights, summand=(), cuts=1, after=(), copies=1, active=None):
     half, size = mine[0].shape[2], rights[0].shape[1]
 
+    scalars = [core] if active is None else [core, active]
+
     def kernel(core_ref, *refs):
-        mine_refs, theirs_refs, right_refs, sum_refs, out_refs = split(
-            refs, len(mine), len(theirs), 2, len(summand)
+        active_refs, mine_refs, theirs_refs, right_refs, sum_refs, out_refs = split(
+            refs, len(scalars) - 1, len(mine), len(theirs), 2, len(summand)
         )
 
         def store(i, tile, *values):
@@ -256,13 +273,25 @@
             other = slice((1 - held) * half, (2 - held) * half)
             adjoint_into(mine_refs, theirs_refs, right_refs[n], own, other, own, store)
 
-        either(core_ref, number, work)
+        def keep():
+            tile = min(mine[0].shape[1], size // cuts)
+            for i in range(0, size, tile):
+                for part in range(2):
+                    for n in range(copies):
+                        value = rows_in(sum_refs, part, i, tile)
+                        put_rows(out_refs[n * cuts : (n + 1) * cuts], part, i, tile, value)
+
+        where_active(
+            active_refs[0] if active_refs else None,
+            lambda: either(core_ref, number, work),
+            keep,
+        )
 
     arrays = [*mine, *theirs, *rights, *summand]
     found = call(
         kernel,
         [block(2, size // cuts, half)] * (cuts * copies),
-        [core],
+        scalars,
         arrays,
         16 * size * half * half,
         (),
@@ -480,17 +509,17 @@
 
     span = 1
     while 2 * span < slabs:
+        active = lax.rem(slab // span, 2)[None]
         carried = times(core_s, 0, maps, groups[0], None, sums[1])
         early, early_sent = adjoint_half(
             core_s, 0, carried, swap_all(carried), maps, sums[0], PARTS, copies=2
         )
         early_groups = arrivals(2 * span, early_sent)
-        wanted = lax.rem(slab // span, 2)[None]
-        own = composed(wanted, own, befores, after=early)
+        own = composed(active, own, befores, after=early)
         ahead = [group[0] for group in early_groups]
-        carried = times(core_s, 1, maps, groups[1], None, [own, *early, *ahead[:AHEAD]])
+        carried = times(core_s, 1, maps, groups[1], None, [own, *early, *ahead[:AHEAD]], active=active)
         behind = ahead[AHEAD:]
-        late = adjoint_half(core_s, 1, carried, swap_all(carried), maps, sums[1], 2, behind)
+        late = adjoint_half(core_s, 1, carried, swap_all(carried), maps, sums[1], 2, behind, active=active)
         sums, groups = [early, late], [early_groups, arrivals(2 * span, late)]
         maps = (own, swap(own))
         span *= 2

time: 102 us -> 101 us (level)
  no operation moved by 1% of the time
where the time goes in v5:
time: 101 us
  waiting for transfers between devices  40.7 us (40%)
  starting transfers between devices  39.3 us (39%)
  Pallas kernels  15.8 us (16%)
  other arithmetic  2.2 us (2%)
  local copies, waits for them, and re-layouts  2.17 us (2%)
    ppermute x19, starting transfers between devices, swap(): return lax.ppermute(value, 'energy', [(i, i ^ 1) for i in range(energies)])  21.2 us
    ppermute x8, waiting for transfers between devices, arrivals(): moving = lax.ppermute(moving, 'slab', moves)  18.8 us
    ppermute x9, waiting for transfers between devices, across(): return lax.ppermute(value, 'energy', moves)  16.8 us
    pallas_call x15, Pallas kernels, call(): pl.pallas_call(body, out_shape=[*outs, *(jax.ShapeDtypeStruct(t.shape, t....  15.8 us
    ppermute x8, starting transfers between devices, arrivals(): moving = lax.ppermute(moving, 'slab', moves)  8.62 us
    ppermute x9, starting transfers between devices, across(): return lax.ppermute(value, 'energy', moves)  8.14 us
    ppermute x19, waiting for transfers between devices, swap(): return lax.ppermute(value, 'energy', [(i, i ^ 1) for i in range(energies)])  5.2 us
  transfers between devices with their start and end apart: 37, of which 23 were waited for; matrix products, arithmetic and copies ran while one was open for 3% of the time, Pallas kernels for 13%

profile of v5, /device:TPU:25, one launch (start us, length us, event | category | flops | bytes accessed | tf_op | source)
XLA Modules:
  0.0 100.6 jit_solution(12719273549325634890)
XLA Ops:
  1.3 1.1 %constant_dynamic-slice_fusion.1 = (bf16[2,1,1,128,256]{4,3,2,1,0:T(8,128)(2,1)S(1)}, bf16[2,1,1,128,256]{4,3,2,1,0:T(8,128)(2,1)S(1)}, bf16[2,1,1,128,256]{4,3,...) fusion(bf16[2,1,1,512,512]{4,3,2,1,0:T(8,128)(2,1)} %param.8, s32[]{:T(128)S(6)} %select_n.46, s32[]{:T(128)S(6)} %select_n.43, ...), kind=kLoop, calls=%fused_computation.7 | loop fusion | bytes 1048596 | tf_op jit(solution)/shard_map/dynamic_slice | solution.py:385
  3.5 1.3 %collective-permute-start.4 = (bf16[528,256]{1,0:T(8,128)(2,1)S(1)}, bf16[528,256]{1,0:T(8,128)(2,1)S(1)}, u32[]{:S(2)}, u32[]{:S(2)}) collective-permute-start(bf16[528,256]{1,0:T(8,128)(2,1)S(1)} %get-tuple-element.78.refs_2_), channel_id=1, source_target_pairs={{0,8},{4,12},{8,0},{12,4},{16,24},{20,28},{24,16},{28,20},{1,9},{5... | collective-permute-start | bytes 811016 | tf_op jit(solution)/shard_map/ppermute | solution.py:381
  4.8 1.2 %collective-permute-start.5 = (bf16[528,256]{1,0:T(8,128)(2,1)S(1)}, bf16[528,256]{1,0:T(8,128)(2,1)S(1)}, u32[]{:S(2)}, u32[]{:S(2)}) collective-permute-start(bf16[528,256]{1,0:T(8,128)(2,1)S(1)} %get-tuple-element.76.refs_3_), channel_id=1, source_target_pairs={{0,16},{4,20},{8,24},{12,28},{16,0},{20,4},{24,8},{28,12},{1,17},{... | collective-permute-start | bytes 811016 | tf_op jit(solution)/shard_map/ppermute | solution.py:381
  8.4 1.3 %collective-permute-start.2 = (bf16[2,512,512]{2,1,0:T(8,128)(2,1)S(1)}, bf16[2,512,512]{2,1,0:T(8,128)(2,1)S(1)}, u32[]{:S(2)}, u32[]{:S(2)}) collective-permute-start(bf16[2,512,512]{2,1,0:T(8,128)(2,1)S(1)} %get-tuple-element.37), channel_id=1, source_target_pairs={{2,3},{6,7},{10,11},{14,15},{18,19},{22,23},{26,27},{30,31}} | collective-permute-start | bytes 3145736 | tf_op jit(solution)/shard_map/ppermute | solution.py:457
  12.1 5.9 %collective-permute-done.6.refs_6_ = bf16[528,256]{1,0:T(8,128)(2,1)S(1)} collective-permute-done((bf16[528,256]{1,0:T(8,128)(2,1)S(1)}, bf16[528,256]{1,0:T(8,128)(2,1)S(1)}, u32[]{:S(2)}, u32[]{:S(2)}) %collective-permute-start.6) | collective-permute-done | bytes 270368 | tf_op jit(solution)/shard_map/ppermute | solution.py:381
  18.0 1.2 %shard_map.65 = (bf16[2,128,256]{2,1,0:T(8,128)(2,1)S(1)}, bf16[2,128,256]{2,1,0:T(8,128)(2,1)S(1)}, bf16[2,128,256]{2,1,0:T(8,128)(2,1)S(1)}, bf16[2,128,256]{2...) custom-call(s32[1]{0:T(128)} %bitcast.12.refs_0_, ...), custom_call_target="tpu_custom_call" | custom-call | flops 6291456 | bytes 2654208 | tf_op jit(solution)/shard_map/pallas_call | solution.py:42
  19.3 1.2 %collective-permute-start.7 = (bf16[2,128,256]{2,1,0:T(8,128)(2,1)S(1)}, bf16[2,128,256]{2,1,0:T(8,128)(2,1)S(1)}, u32[]{:S(2)}, u32[]{:S(2)}) collective-permute-start(bf16[2,128,256]{2,1,0:T(8,128)(2,1)S(1)} %get-tuple-element.39), channel_id=1, source_target_pairs={{0,8},{4,12},{8,0},{12,4},{16,24},{20,28},{24,16},{28,20},{1,9},{5... | collective-permute-start | bytes 393224 | tf_op jit(solution)/shard_map/ppermute | solution.py:381
  20.8 1.2 %collective-permute-start.9 = (bf16[2,128,256]{2,1,0:T(8,128)(2,1)S(1)}, bf16[2,128,256]{2,1,0:T(8,128)(2,1)S(1)}, u32[]{:S(2)}, u32[]{:S(2)}) collective-permute-start(bf16[2,128,256]{2,1,0:T(8,128)(2,1)S(1)} %get-tuple-element.41), channel_id=1, source_target_pairs={{0,24},{4,28},{8,16},{12,20},{16,8},{20,12},{24,0},{28,4},{1,25},{... | collective-permute-start | bytes 393224 | tf_op jit(solution)/shard_map/ppermute | solution.py:381
  23.5 1.8 %collective-permute-done.8.refs_6_ = bf16[2,128,256]{2,1,0:T(8,128)(2,1)S(1)} collective-permute-done((bf16[2,128,256]{2,1,0:T(8,128)(2,1)S(1)}, bf16[2,128,256]{2,1,0:T(8,128)(2,1)S(1)}, u32[]{:S(2)}, u32[]{:S(2)}) %collective-permute-start.8) | collective-permute-done | bytes 131104 | tf_op jit(solution)/shard_map/ppermute | solution.py:381
  25.3 1.2 %collective-permute-done.9.refs_7_ = bf16[2,128,256]{2,1,0:T(8,128)(2,1)S(1)} collective-permute-done((bf16[2,128,256]{2,1,0:T(8,128)(2,1)S(1)}, bf16[2,128,256]{2,1,0:T(8,128)(2,1)S(1)}, u32[]{:S(2)}, u32[]{:S(2)}) %collective-permute-start.9) | collective-permute-done | bytes 131104 | tf_op jit(solution)/shard_map/ppermute | solution.py:381
  26.5 1.3 %shard_map.67 = (bf16[2,256,256]{2,1,0:T(8,128)(2,1)S(1)}, bf16[2,256,256]{2,1,0:T(8,128)(2,1)S(1)}, bf16[2,128,256]{2,1,0:T(8,128)(2,1)S(1)}, bf16[2,128,256]{2,1,0:T(8,128)(2,1)S(1)}, bf16[2,128,256]{2,1,0:T(8,128)(2,1)S(1)}) custom-call(s32[1]{0:T(128)} %bitcast.refs_0_, s32[4]{0:T(128)S(1)} %iota_xor_fusion.refs_1_, bf16[2,512,512]{2,1,0:T(8,128)(2,1)S(1)} %bitcast.27, ...), custom_call_target="tpu_custom_call" | custom-call | flops 536870912 | bytes 3145728 | tf_op jit(solution)/shard_map/pallas_call | solution.py:42
  27.8 2.8 %collective-permute-start.10 = (bf16[2,256,256]{2,1,0:T(8,128)(2,1)S(1)}, bf16[2,256,256]{2,1,0:T(8,128)(2,1)S(1)}, u32[]{:S(2)}, u32[]{:S(2)}) collective-permute-start(bf16[2,256,256]{2,1,0:T(8,128)(2,1)S(1)} %get-tuple-element.45.refs_1_), channel_id=1, source_target_pairs={{0,4},{4,0},{8,12},{12,8},{16,20},{20,16},{24,28},{28,24},{1,5},{5... | collective-permute-start | bytes 786440 | tf_op jit(solution)/shard_map/ppermute | solution.py:356
  32.9 1.3 %collective-permute-start.12 = (bf16[2,512,256]{2,1,0:T(8,128)(2,1)S(1)}, bf16[2,512,256]{2,1,0:T(8,128)(2,1)S(1)}, u32[]{:S(2)}, u32[]{:S(2)}) collective-permute-start(bf16[2,512,256]{2,1,0:T(8,128)(2,1)S(1)} %shard_map.68.refs_8_.refs_7_), channel_id=1, source_target_pairs={{0,1},{2,3},{4,5},{6,7},{8,9},{10,11},{12,13},{14,15},{16,17},{18,... | collective-permute-start | bytes 1572872 | tf_op jit(solution)/shard_map/ppermute | solution.py:474
  36.9 2.0 %collective-permute-done.13.refs_5_ = bf16[2,128,256]{2,1,0:T(8,128)(2,1)S(1)} collective-permute-done((bf16[2,128,256]{2,1,0:T(8,128)(2,1)S(1)}, bf16[2,128,256]{2,1,0:T(8,128)(2,1)S(1)}, u32[]{:S(2)}, u32[]{:S(2)}) %collective-permute-start.13) | collective-permute-done | bytes 131104 | tf_op jit(solution)/shard_map/ppermute | solution.py:381
  39.6 2.9 %collective-permute-done.15.refs_7_ = bf16[2,128,256]{2,1,0:T(8,128)(2,1)S(1)} collective-permute-done((bf16[2,128,256]{2,1,0:T(8,128)(2,1)S(1)}, bf16[2,128,256]{2,1,0:T(8,128)(2,1)S(1)}, u32[]{:S(2)}, u32[]{:S(2)}) %collective-permute-start.15) | collective-permute-done | bytes 131104 | tf_op jit(solution)/shard_map/ppermute | solution.py:381
  42.5 1.3 %shard_map.69 = (bf16[2,256,256]{2,1,0:T(8,128)(2,1)S(1)}, bf16[2,256,256]{2,1,0:T(8,128)(2,1)S(1)}) custom-call(s32[1]{0:T(128)} %bitcast.refs_0_, s32[4]{0:T(128)S(1)} %iota_xor_fusion.refs_1_, bf16[2,512,512]{2,1,0:T(8,128)(2,1)S(1)} %bitcast.29, bf16[2,512,512]{2,1,0:T(8,128)(2,1)S(1)} %collective-permute-done.3.refs_0_.refs_3_.refs_6_, ...), custom_call_target="tpu_custom_call" | custom-call | flops 536870912 | bytes 3145728 | tf_op jit(solution)/shard_map/pallas_call | solution.py:42
  43.8 1.5 %collective-permute-start.16 = (bf16[2,256,256]{2,1,0:T(8,128)(2,1)S(1)}, bf16[2,256,256]{2,1,0:T(8,128)(2,1)S(1)}, u32[]{:S(2)}, u32[]{:S(2)}) collective-permute-start(bf16[2,256,256]{2,1,0:T(8,128)(2,1)S(1)} %get-tuple-element.51.refs_1_), channel_id=1, source_target_pairs={{0,4},{4,0},{8,12},{12,8},{16,20},{20,16},{24,28},{28,24},{1,5},{5... | collective-permute-start | bytes 786440 | tf_op jit(solution)/shard_map/ppermute | solution.py:356
  48.8 1.1 %collective-permute-start.18 = (bf16[2,256,256]{2,1,0:T(8,128)(2,1)S(1)}, bf16[2,256,256]{2,1,0:T(8,128)(2,1)S(1)}, u32[]{:S(2)}, u32[]{:S(2)}) collective-permute-start(bf16[2,256,256]{2,1,0:T(8,128)(2,1)S(1)} %get-tuple-element.54.refs_1_), channel_id=1, source_target_pairs={{0,4},{4,0},{8,12},{12,8},{16,20},{20,16},{24,28},{28,24},{1,5},{5... | collective-permute-start | bytes 786440 | tf_op jit(solution)/shard_map/ppermute | solution.py:356
  50.0 1.4 %collective-permute-start.23 = (bf16[2,512,256]{2,1,0:T(8,128)(2,1)}, bf16[2,512,256]{2,1,0:T(8,128)(2,1)S(1)}, u32[]{:S(2)}, u32[]{:S(2)}) collective-permute-start(bf16[2,512,256]{2,1,0:T(8,128)(2,1)} %copy-done.8), channel_id=1, source_target_pairs={{0,1},{2,3},{4,5},{6,7},{8,9},{10,11},{12,13},{14,15},{16,17},{18,... | collective-permute-start | bytes 1572872 | tf_op jit(solution)/shard_map/ppermute | solution.py:474
  51.6 1.7 %shard_map.72 = (bf16[2,512,256]{2,1,0:T(8,128)(2,1)S(1)}, bf16[2,512,256]{2,1,0:T(8,128)(2,1)S(1)}) custom-call(s32[1]{0:T(128)} %bitcast.refs_0_, bf16[2,256,256]{2,1,0:T(8,128)(2,1)S(1)} %get-tuple-element.54.refs_1_, bf16[2,256,256]{2,1,0:T(8,128)(2,1)S(1)} %get-tuple-element.55.refs_2_, bf16[2,256,256]{2,1,0:T(8,128)(2,1)S(1)} %collective-permute-done.18.refs_3_, ...), custom_call_target="tpu_custom_call" | custom-call | flops 536870912 | bytes 4718592 | tf_op jit(solution)/shard_map/pallas_call | solution.py:42
  54.0 1.4 %shard_map.73.refs_1_.refs_5_ = bf16[2,512,512]{2,1,0:T(8,128)(2,1)S(1)} custom-call(s32[1]{0:T(128)} %bitcast.1.refs_0_.refs_1_, bf16[2,512,512]{2,1,0:T(8,128)(2,1)S(1)} %get-tuple-element.36.refs_1_.refs_5_.refs_2_.refs_6_, bf16[2,512,512]{2,1,0:T(8,128)(2,1)S(1)} %copy-done.7, bf16[2,512,256]{2,1,0:T(8,128)(2,1)S(1)} %get-tuple-element.56.refs_3_.refs_6_.refs_10_), custom_call_target="tpu_custom_call" | custom-call | flops 1073741824 | bytes 3145728 | tf_op jit(solution)/shard_map/pallas_call | solution.py:42
  56.0 9.4 %collective-permute-done.23.refs_4_ = bf16[2,512,256]{2,1,0:T(8,128)(2,1)S(1)} collective-permute-done((bf16[2,512,256]{2,1,0:T(8,128)(2,1)}, bf16[2,512,256]{2,1,0:T(8,128)(2,1)S(1)}, u32[]{:S(2)}, u32[]{:S(2)}) %collective-permute-start.23) | collective-permute-done | bytes 524320 | tf_op jit(solution)/shard_map/ppermute | solution.py:474
  66.1 1.3 %collective-permute-start.24 = (bf16[2,256,256]{2,1,0:T(8,128)(2,1)S(1)}, bf16[2,256,256]{2,1,0:T(8,128)(2,1)S(1)}, u32[]{:S(2)}, u32[]{:S(2)}) collective-permute-start(bf16[2,256,256]{2,1,0:T(8,128)(2,1)S(1)} %get-tuple-element.61.refs_2_), channel_id=1, source_target_pairs={{0,4},{4,0},{8,12},{12,8},{16,20},{20,16},{24,28},{28,24},{1,5},{5... | collective-permute-start | bytes 786440 | tf_op jit(solution)/shard_map/ppermute | solution.py:356
  67.5 1.3 %collective-permute-start.22 = (bf16[2,512,256]{2,1,0:T(8,128)(2,1)S(1)}, bf16[2,512,256]{2,1,0:T(8,128)(2,1)S(1)}, u32[]{:S(2)}, u32[]{:S(2)}) collective-permute-start(bf16[2,512,256]{2,1,0:T(8,128)(2,1)S(1)} %collective-permute-done.21.refs_3_.refs_9_), channel_id=1, source_target_pairs={{2,3},{6,7},{10,11},{14,15},{18,19},{22,23},{26,27},{30,31}} | collective-permute-start | bytes 1572872 | tf_op jit(solution)/shard_map/ppermute | solution.py:474
  71.1 1.3 %collective-permute-start.27 = (bf16[2,256,256]{2,1,0:T(8,128)(2,1)S(1)}, bf16[2,256,256]{2,1,0:T(8,128)(2,1)S(1)}, u32[]{:S(2)}, u32[]{:S(2)}) collective-permute-start(bf16[2,256,256]{2,1,0:T(8,128)(2,1)S(1)} %collective-permute-done.26.refs_3_), channel_id=1, source_target_pairs={{2,3},{6,7},{10,11},{14,15},{18,19},{22,23},{26,27},{30,31}} | collective-permute-start | bytes 786440 | tf_op jit(solution)/shard_map/ppermute | solution.py:474
  72.4 1.3 %collective-permute-start.29 = (bf16[2,256,256]{2,1,0:T(8,128)(2,1)S(1)}, bf16[2,256,256]{2,1,0:T(8,128)(2,1)S(1)}, u32[]{:S(2)}, u32[]{:S(2)}) collective-permute-start(bf16[2,256,256]{2,1,0:T(8,128)(2,1)S(1)} %collective-permute-done.28.refs_5_), channel_id=1, source_target_pairs={{2,3},{6,7},{10,11},{14,15},{18,19},{22,23},{26,27},{30,31}} | collective-permute-start | bytes 786440 | tf_op jit(solution)/shard_map/ppermute | solution.py:474
  73.7 8.1 %collective-permute-done.22.refs_4_ = bf16[2,512,256]{2,1,0:T(8,128)(2,1)S(1)} collective-permute-done((bf16[2,512,256]{2,1,0:T(8,128)(2,1)S(1)}, bf16[2,512,256]{2,1,0:T(8,128)(2,1)S(1)}, u32[]{:S(2)}, u32[]{:S(2)}) %collective-permute-start.22) | collective-permute-done | bytes 524320 | tf_op jit(solution)/shard_map/ppermute | solution.py:474
  82.6 4.0 %collective-permute-start.30 = (bf16[2,256,256]{2,1,0:T(8,128)(2,1)S(1)}, bf16[2,256,256]{2,1,0:T(8,128)(2,1)S(1)}, u32[]{:S(2)}, u32[]{:S(2)}) collective-permute-start(bf16[2,256,256]{2,1,0:T(8,128)(2,1)S(1)} %get-tuple-element.58.refs_2_), channel_id=1, source_target_pairs={{0,4},{4,0},{8,12},{12,8},{16,20},{20,16},{24,28},{28,24},{1,5},{5... | collective-permute-start | bytes 786440 | tf_op jit(solution)/shard_map/ppermute | solution.py:356
  87.1 4.9 %collective-permute-start.35 = (bf16[2,256,256]{2,1,0:T(8,128)(2,1)S(1)}, bf16[2,256,256]{2,1,0:T(8,128)(2,1)S(1)}, u32[]{:S(2)}, u32[]{:S(2)}) collective-permute-start(bf16[2,256,256]{2,1,0:T(8,128)(2,1)S(1)} %get-tuple-element.63.refs_11_), channel_id=1, source_target_pairs={{0,4},{4,0},{8,12},{12,8},{16,20},{20,16},{24,28},{28,24},{1,5},{5... | collective-permute-start | bytes 786440 | tf_op jit(solution)/shard_map/ppermute | solution.py:356
  92.0 1.2 %collective-permute-done.29.refs_6_ = bf16[2,256,256]{2,1,0:T(8,128)(2,1)S(1)} collective-permute-done((bf16[2,256,256]{2,1,0:T(8,128)(2,1)S(1)}, bf16[2,256,256]{2,1,0:T(8,128)(2,1)S(1)}, u32[]{:S(2)}, u32[]{:S(2)}) %collective-permute-start.29) | collective-permute-done | bytes 262176 | tf_op jit(solution)/shard_map/ppermute | solution.py:474
  93.2 2.4 %collective-permute-start.36 = (bf16[2,256,256]{2,1,0:T(8,128)(2,1)S(1)}, bf16[2,256,256]{2,1,0:T(8,128)(2,1)S(1)}, u32[]{:S(2)}, u32[]{:S(2)}) collective-permute-start(bf16[2,256,256]{2,1,0:T(8,128)(2,1)S(1)} %get-tuple-element.64.refs_12_), channel_id=1, source_target_pairs={{0,4},{4,0},{8,12},{12,8},{16,20},{20,16},{24,28},{28,24},{1,5},{5... | collective-permute-start | bytes 786440 | tf_op jit(solution)/shard_map/ppermute | solution.py:356
  98.4 2.1 %shard_map.78 = bf16[2,512,512]{2,1,0:T(8,128)(2,1)} custom-call(s32[1]{0:T(128)} %bitcast.refs_0_, bf16[2,512,512]{2,1,0:T(8,128)(2,1)S(1)} %shard_map.73.refs_1_.refs_5_, bf16[2,256,256]{2,1,0:T(8,128)(2,1)S(1)} %get-tuple-element.58.refs_2_, bf16[2,256,256]{2,1,0:T(8,128)(2,1)S(1)} %get-tuple-element.59.refs_3_, ...), custom_call_target="tpu_custom_call" | custom-call | flops 1073741824 | bytes 6291456 | tf_op jit(solution)/shard_map/pallas_call | solution.py:42
  (91 shorter events, 26.4 us)
Async XLA Ops:
  0.0 3.2 %collective-permute-start = (bf16[2,512,512]{2,1,0:T(8,128)(2,1)}, bf16[2,512,512]{2,1,0:T(8,128)(2,1)S(1)}, u32[]{:S(2)}, u32[]{:S(2)}) collective-permute-start(bf16[2,512,512]{2,1,0:T(8,128)(2,1)} %bitcast.41), channel_id=1, source_target_pairs={{0,4},{4,0},{8,12},{12,8},{16,20},{20,16},{24,28},{28,24},{1,5},{5... | collective-permute-start | bytes 3145736 | tf_op jit(solution)/shard_map/ppermute | solution.py:356
  0.7 2.3 %collective-permute-start.1 = (s32[1,2]{1,0:T(1,128)S(1)}, s32[1,2]{1,0:T(1,128)S(1)}, u32[]{:S(2)}, u32[]{:S(2)}) collective-permute-start(s32[1,2]{1,0:T(1,128)S(1)} %copy-done.10), channel_id=1, source_target_pairs={{0,4},{4,0},{8,12},{12,8},{16,20},{20,16},{24,28},{28,24},{1,5},{5... | collective-permute-start | bytes 32 | tf_op jit(solution)/shard_map/ppermute | solution.py:356
  1.3 20.7 %collective-permute-start.3 = (bf16[2,512,512]{2,1,0:T(8,128)(2,1)}, bf16[2,512,512]{2,1,0:T(8,128)(2,1)S(1)}, u32[]{:S(2)}, u32[]{:S(2)}) collective-permute-start(bf16[2,512,512]{2,1,0:T(8,128)(2,1)} %bitcast.25), channel_id=1, source_target_pairs={{0,4},{4,0},{8,12},{12,8},{16,20},{20,16},{24,28},{28,24},{1,5},{5... | collective-permute-start | bytes 3145736 | tf_op jit(solution)/shard_map/ppermute | solution.py:356
  3.5 7.8 %collective-permute-start.4 = (bf16[528,256]{1,0:T(8,128)(2,1)S(1)}, bf16[528,256]{1,0:T(8,128)(2,1)S(1)}, u32[]{:S(2)}, u32[]{:S(2)}) collective-permute-start(bf16[528,256]{1,0:T(8,128)(2,1)S(1)} %get-tuple-element.78.refs_2_), channel_id=1, source_target_pairs={{0,8},{4,12},{8,0},{12,4},{16,24},{20,28},{24,16},{28,20},{1,9},{5... | collective-permute-start | bytes 811016 | tf_op jit(solution)/shard_map/ppermute | solution.py:381
  4.8 7.4 %collective-permute-start.5 = (bf16[528,256]{1,0:T(8,128)(2,1)S(1)}, bf16[528,256]{1,0:T(8,128)(2,1)S(1)}, u32[]{:S(2)}, u32[]{:S(2)}) collective-permute-start(bf16[528,256]{1,0:T(8,128)(2,1)S(1)} %get-tuple-element.76.refs_3_), channel_id=1, source_target_pairs={{0,16},{4,20},{8,24},{12,28},{16,0},{20,4},{24,8},{28,12},{1,17},{... | collective-permute-start | bytes 811016 | tf_op jit(solution)/shard_map/ppermute | solution.py:381
  6.0 12.0 %collective-permute-start.6 = (bf16[528,256]{1,0:T(8,128)(2,1)S(1)}, bf16[528,256]{1,0:T(8,128)(2,1)S(1)}, u32[]{:S(2)}, u32[]{:S(2)}) collective-permute-start(bf16[528,256]{1,0:T(8,128)(2,1)S(1)} %get-tuple-element.77.refs_4_), channel_id=1, source_target_pairs={{0,24},{4,28},{8,16},{12,20},{16,8},{20,12},{24,0},{28,4},{1,25},{... | collective-permute-start | bytes 811016 | tf_op jit(solution)/shard_map/ppermute | solution.py:381
  8.4 38.5 %collective-permute-start.2 = (bf16[2,512,512]{2,1,0:T(8,128)(2,1)S(1)}, bf16[2,512,512]{2,1,0:T(8,128)(2,1)S(1)}, u32[]{:S(2)}, u32[]{:S(2)}) collective-permute-start(bf16[2,512,512]{2,1,0:T(8,128)(2,1)S(1)} %get-tuple-element.37), channel_id=1, source_target_pairs={{2,3},{6,7},{10,11},{14,15},{18,19},{22,23},{26,27},{30,31}} | collective-permute-start | bytes 3145736 | tf_op jit(solution)/shard_map/ppermute | solution.py:457
  19.3 4.2 %collective-permute-start.7 = (bf16[2,128,256]{2,1,0:T(8,128)(2,1)S(1)}, bf16[2,128,256]{2,1,0:T(8,128)(2,1)S(1)}, u32[]{:S(2)}, u32[]{:S(2)}) collective-permute-start(bf16[2,128,256]{2,1,0:T(8,128)(2,1)S(1)} %get-tuple-element.39), channel_id=1, source_target_pairs={{0,8},{4,12},{8,0},{12,4},{16,24},{20,28},{24,16},{28,20},{1,9},{5... | collective-permute-start | bytes 393224 | tf_op jit(solution)/shard_map/ppermute | solution.py:381
  20.5 4.8 %collective-permute-start.8 = (bf16[2,128,256]{2,1,0:T(8,128)(2,1)S(1)}, bf16[2,128,256]{2,1,0:T(8,128)(2,1)S(1)}, u32[]{:S(2)}, u32[]{:S(2)}) collective-permute-start(bf16[2,128,256]{2,1,0:T(8,128)(2,1)S(1)} %get-tuple-element.40), channel_id=1, source_target_pairs={{0,16},{4,20},{8,24},{12,28},{16,0},{20,4},{24,8},{28,12},{1,17},{... | collective-permute-start | bytes 393224 | tf_op jit(solution)/shard_map/ppermute | solution.py:381
  20.8 5.7 %collective-permute-start.9 = (bf16[2,128,256]{2,1,0:T(8,128)(2,1)S(1)}, bf16[2,128,256]{2,1,0:T(8,128)(2,1)S(1)}, u32[]{:S(2)}, u32[]{:S(2)}) collective-permute-start(bf16[2,128,256]{2,1,0:T(8,128)(2,1)S(1)} %get-tuple-element.41), channel_id=1, source_target_pairs={{0,24},{4,28},{8,16},{12,20},{16,8},{20,12},{24,0},{28,4},{1,25},{... | collective-permute-start | bytes 393224 | tf_op jit(solution)/shard_map/ppermute | solution.py:381
  27.8 4.0 %collective-permute-start.10 = (bf16[2,256,256]{2,1,0:T(8,128)(2,1)S(1)}, bf16[2,256,256]{2,1,0:T(8,128)(2,1)S(1)}, u32[]{:S(2)}, u32[]{:S(2)}) collective-permute-start(bf16[2,256,256]{2,1,0:T(8,128)(2,1)S(1)} %get-tuple-element.45.refs_1_), channel_id=1, source_target_pairs={{0,4},{4,0},{8,12},{12,8},{16,20},{20,16},{24,28},{28,24},{1,5},{5... | collective-permute-start | bytes 786440 | tf_op jit(solution)/shard_map/ppermute | solution.py:356
  32.9 15.0 %collective-permute-start.12 = (bf16[2,512,256]{2,1,0:T(8,128)(2,1)S(1)}, bf16[2,512,256]{2,1,0:T(8,128)(2,1)S(1)}, u32[]{:S(2)}, u32[]{:S(2)}) collective-permute-start(bf16[2,512,256]{2,1,0:T(8,128)(2,1)S(1)} %shard_map.68.refs_8_.refs_7_), channel_id=1, source_target_pairs={{0,1},{2,3},{4,5},{6,7},{8,9},{10,11},{12,13},{14,15},{16,17},{18,... | collective-permute-start | bytes 1572872 | tf_op jit(solution)/shard_map/ppermute | solution.py:474
  34.2 4.7 %collective-permute-start.13 = (bf16[2,128,256]{2,1,0:T(8,128)(2,1)S(1)}, bf16[2,128,256]{2,1,0:T(8,128)(2,1)S(1)}, u32[]{:S(2)}, u32[]{:S(2)}) collective-permute-start(bf16[2,128,256]{2,1,0:T(8,128)(2,1)S(1)} %get-tuple-element.48), channel_id=1, source_target_pairs={{0,8},{4,12},{8,0},{12,4},{16,24},{20,28},{24,16},{28,20},{1,9},{5... | collective-permute-start | bytes 393224 | tf_op jit(solution)/shard_map/ppermute | solution.py:381
  35.2 4.4 %collective-permute-start.14 = (bf16[2,128,256]{2,1,0:T(8,128)(2,1)S(1)}, bf16[2,128,256]{2,1,0:T(8,128)(2,1)S(1)}, u32[]{:S(2)}, u32[]{:S(2)}) collective-permute-start(bf16[2,128,256]{2,1,0:T(8,128)(2,1)S(1)} %get-tuple-element.49), channel_id=1, source_target_pairs={{0,16},{4,20},{8,24},{12,28},{16,0},{20,4},{24,8},{28,12},{1,17},{... | collective-permute-start | bytes 393224 | tf_op jit(solution)/shard_map/ppermute | solution.py:381
  36.0 6.6 %collective-permute-start.15 = (bf16[2,128,256]{2,1,0:T(8,128)(2,1)S(1)}, bf16[2,128,256]{2,1,0:T(8,128)(2,1)S(1)}, u32[]{:S(2)}, u32[]{:S(2)}) collective-permute-start(bf16[2,128,256]{2,1,0:T(8,128)(2,1)S(1)} %get-tuple-element.50), channel_id=1, source_target_pairs={{0,24},{4,28},{8,16},{12,20},{16,8},{20,12},{24,0},{28,4},{1,25},{... | collective-permute-start | bytes 393224 | tf_op jit(solution)/shard_map/ppermute | solution.py:381
  43.8 2.7 %collective-permute-start.16 = (bf16[2,256,256]{2,1,0:T(8,128)(2,1)S(1)}, bf16[2,256,256]{2,1,0:T(8,128)(2,1)S(1)}, u32[]{:S(2)}, u32[]{:S(2)}) collective-permute-start(bf16[2,256,256]{2,1,0:T(8,128)(2,1)S(1)} %get-tuple-element.51.refs_1_), channel_id=1, source_target_pairs={{0,4},{4,0},{8,12},{12,8},{16,20},{20,16},{24,28},{28,24},{1,5},{5... | collective-permute-start | bytes 786440 | tf_op jit(solution)/shard_map/ppermute | solution.py:356
  48.8 2.6 %collective-permute-start.18 = (bf16[2,256,256]{2,1,0:T(8,128)(2,1)S(1)}, bf16[2,256,256]{2,1,0:T(8,128)(2,1)S(1)}, u32[]{:S(2)}, u32[]{:S(2)}) collective-permute-start(bf16[2,256,256]{2,1,0:T(8,128)(2,1)S(1)} %get-tuple-element.54.refs_1_), channel_id=1, source_target_pairs={{0,4},{4,0},{8,12},{12,8},{16,20},{20,16},{24,28},{28,24},{1,5},{5... | collective-permute-start | bytes 786440 | tf_op jit(solution)/shard_map/ppermute | solution.py:356
  50.0 1.7 %collective-permute-start.19 = (bf16[2,256,256]{2,1,0:T(8,128)(2,1)S(1)}, bf16[2,256,256]{2,1,0:T(8,128)(2,1)}, u32[]{:S(2)}, u32[]{:S(2)}) collective-permute-start(bf16[2,256,256]{2,1,0:T(8,128)(2,1)S(1)} %get-tuple-element.55.refs_2_), channel_id=1, source_target_pairs={{0,4},{4,0},{8,12},{12,8},{16,20},{20,16},{24,28},{28,24},{1,5},{5... | collective-permute-start | bytes 786440 | tf_op jit(solution)/shard_map/ppermute | solution.py:356
  50.0 15.3 %collective-permute-start.23 = (bf16[2,512,256]{2,1,0:T(8,128)(2,1)}, bf16[2,512,256]{2,1,0:T(8,128)(2,1)S(1)}, u32[]{:S(2)}, u32[]{:S(2)}) collective-permute-start(bf16[2,512,256]{2,1,0:T(8,128)(2,1)} %copy-done.8), channel_id=1, source_target_pairs={{0,1},{2,3},{4,5},{6,7},{8,9},{10,11},{12,13},{14,15},{16,17},{18,... | collective-permute-start | bytes 1572872 | tf_op jit(solution)/shard_map/ppermute | solution.py:474
  53.3 14.1 %collective-permute-start.21 = (bf16[2,512,256]{2,1,0:T(8,128)(2,1)S(1)}, bf16[2,512,256]{2,1,0:T(8,128)(2,1)S(1)}, u32[]{:S(2)}, u32[]{:S(2)}) collective-permute-start(bf16[2,512,256]{2,1,0:T(8,128)(2,1)S(1)} %get-tuple-element.57), channel_id=1, source_target_pairs={{1,2},{5,6},{9,10},{13,14},{17,18},{21,22},{25,26},{29,30}} | collective-permute-start | bytes 1572872 | tf_op jit(solution)/shard_map/ppermute | solution.py:474
  55.5 18.2 %collective-permute-start.20 = (bf16[2,512,512]{2,1,0:T(8,128)(2,1)S(1)}, bf16[2,512,512]{2,1,0:T(8,128)(2,1)S(1)}, u32[]{:S(2)}, u32[]{:S(2)}) collective-permute-start(bf16[2,512,512]{2,1,0:T(8,128)(2,1)S(1)} %shard_map.73.refs_1_.refs_5_), channel_id=1, source_target_pairs={{0,4},{4,0},{8,12},{12,8},{16,20},{20,16},{24,28},{28,24},{1,5},{5... | collective-permute-start | bytes 3145736 | tf_op jit(solution)/shard_map/ppermute | solution.py:356
  66.1 2.7 %collective-permute-start.24 = (bf16[2,256,256]{2,1,0:T(8,128)(2,1)S(1)}, bf16[2,256,256]{2,1,0:T(8,128)(2,1)S(1)}, u32[]{:S(2)}, u32[]{:S(2)}) collective-permute-start(bf16[2,256,256]{2,1,0:T(8,128)(2,1)S(1)} %get-tuple-element.61.refs_2_), channel_id=1, source_target_pairs={{0,4},{4,0},{8,12},{12,8},{16,20},{20,16},{24,28},{28,24},{1,5},{5... | collective-permute-start | bytes 786440 | tf_op jit(solution)/shard_map/ppermute | solution.py:356
  67.5 14.4 %collective-permute-start.22 = (bf16[2,512,256]{2,1,0:T(8,128)(2,1)S(1)}, bf16[2,512,256]{2,1,0:T(8,128)(2,1)S(1)}, u32[]{:S(2)}, u32[]{:S(2)}) collective-permute-start(bf16[2,512,256]{2,1,0:T(8,128)(2,1)S(1)} %collective-permute-done.21.refs_3_.refs_9_), channel_id=1, source_target_pairs={{2,3},{6,7},{10,11},{14,15},{18,19},{22,23},{26,27},{30,31}} | collective-permute-start | bytes 1572872 | tf_op jit(solution)/shard_map/ppermute | solution.py:474
  70.4 2.0 %collective-permute-start.28 = (bf16[2,256,256]{2,1,0:T(8,128)(2,1)S(1)}, bf16[2,256,256]{2,1,0:T(8,128)(2,1)S(1)}, u32[]{:S(2)}, u32[]{:S(2)}) collective-permute-start(bf16[2,256,256]{2,1,0:T(8,128)(2,1)S(1)} %get-tuple-element.64.refs_12_), channel_id=1, source_target_pairs={{1,2},{5,6},{9,10},{13,14},{17,18},{21,22},{25,26},{29,30}} | collective-permute-start | bytes 786440 | tf_op jit(solution)/shard_map/ppermute | solution.py:474
  71.1 16.0 %collective-permute-start.27 = (bf16[2,256,256]{2,1,0:T(8,128)(2,1)S(1)}, bf16[2,256,256]{2,1,0:T(8,128)(2,1)S(1)}, u32[]{:S(2)}, u32[]{:S(2)}) collective-permute-start(bf16[2,256,256]{2,1,0:T(8,128)(2,1)S(1)} %collective-permute-done.26.refs_3_), channel_id=1, source_target_pairs={{2,3},{6,7},{10,11},{14,15},{18,19},{22,23},{26,27},{30,31}} | collective-permute-start | bytes 786440 | tf_op jit(solution)/shard_map/ppermute | solution.py:474
  72.4 20.8 %collective-permute-start.29 = (bf16[2,256,256]{2,1,0:T(8,128)(2,1)S(1)}, bf16[2,256,256]{2,1,0:T(8,128)(2,1)S(1)}, u32[]{:S(2)}, u32[]{:S(2)}) collective-permute-start(bf16[2,256,256]{2,1,0:T(8,128)(2,1)S(1)} %collective-permute-done.28.refs_5_), channel_id=1, source_target_pairs={{2,3},{6,7},{10,11},{14,15},{18,19},{22,23},{26,27},{30,31}} | collective-permute-start | bytes 786440 | tf_op jit(solution)/shard_map/ppermute | solution.py:474
  82.6 13.0 %collective-permute-start.30 = (bf16[2,256,256]{2,1,0:T(8,128)(2,1)S(1)}, bf16[2,256,256]{2,1,0:T(8,128)(2,1)S(1)}, u32[]{:S(2)}, u32[]{:S(2)}) collective-permute-start(bf16[2,256,256]{2,1,0:T(8,128)(2,1)S(1)} %get-tuple-element.58.refs_2_), channel_id=1, source_target_pairs={{0,4},{4,0},{8,12},{12,8},{16,20},{20,16},{24,28},{28,24},{1,5},{5... | collective-permute-start | bytes 786440 | tf_op jit(solution)/shard_map/ppermute | solution.py:356
  86.6 9.0 %collective-permute-start.31 = (bf16[2,256,256]{2,1,0:T(8,128)(2,1)S(1)}, bf16[2,256,256]{2,1,0:T(8,128)(2,1)S(1)}, u32[]{:S(2)}, u32[]{:S(2)}) collective-permute-start(bf16[2,256,256]{2,1,0:T(8,128)(2,1)S(1)} %get-tuple-element.59.refs_3_), channel_id=1, source_target_pairs={{0,4},{4,0},{8,12},{12,8},{16,20},{20,16},{24,28},{28,24},{1,5},{5... | collective-permute-start | bytes 786440 | tf_op jit(solution)/shard_map/ppermute | solution.py:356
  86.7 10.3 %collective-permute-start.34 = (bf16[2,512,256]{2,1,0:T(8,128)(2,1)S(1)}, bf16[2,512,256]{2,1,0:T(8,128)(2,1)S(1)}, u32[]{:S(2)}, u32[]{:S(2)}) collective-permute-start(bf16[2,512,256]{2,1,0:T(8,128)(2,1)S(1)} %get-tuple-element.56.refs_3_.refs_6_.refs_10_), channel_id=1, source_target_pairs={{0,4},{4,0},{8,12},{12,8},{16,20},{20,16},{24,28},{28,24},{1,5},{5... | collective-permute-start | bytes 1572872 | tf_op jit(solution)/shard_map/ppermute | solution.py:356
  87.1 9.9 %collective-permute-start.35 = (bf16[2,256,256]{2,1,0:T(8,128)(2,1)S(1)}, bf16[2,256,256]{2,1,0:T(8,128)(2,1)S(1)}, u32[]{:S(2)}, u32[]{:S(2)}) collective-permute-start(bf16[2,256,256]{2,1,0:T(8,128)(2,1)S(1)} %get-tuple-element.63.refs_11_), channel_id=1, source_target_pairs={{0,4},{4,0},{8,12},{12,8},{16,20},{20,16},{24,28},{28,24},{1,5},{5... | collective-permute-start | bytes 786440 | tf_op jit(solution)/shard_map/ppermute | solution.py:356
  93.2 3.8 %collective-permute-start.36 = (bf16[2,256,256]{2,1,0:T(8,128)(2,1)S(1)}, bf16[2,256,256]{2,1,0:T(8,128)(2,1)S(1)}, u32[]{:S(2)}, u32[]{:S(2)}) collective-permute-start(bf16[2,256,256]{2,1,0:T(8,128)(2,1)S(1)} %get-tuple-element.64.refs_12_), channel_id=1, source_target_pairs={{0,4},{4,0},{8,12},{12,8},{16,20},{20,16},{24,28},{28,24},{1,5},{5... | collective-permute-start | bytes 786440 | tf_op jit(solution)/shard_map/ppermute | solution.py:356
  96.5 1.9 %collective-permute-start.33 = (bf16[2,256,256]{2,1,0:T(8,128)(2,1)S(1)}, bf16[2,256,256]{2,1,0:T(8,128)(2,1)S(1)}, u32[]{:S(2)}, u32[]{:S(2)}) collective-permute-start(bf16[2,256,256]{2,1,0:T(8,128)(2,1)S(1)} %get-tuple-element.66.refs_5_), channel_id=1, source_target_pairs={{0,4},{4,0},{8,12},{12,8},{16,20},{20,16},{24,28},{28,24},{1,5},{5... | collective-permute-start | bytes 786440 | tf_op jit(solution)/shard_map/ppermute | solution.py:356
  (16 other events, 52.6 us)
